TPU v7x, 32 devices: a whole 2x2x4 slice. The times are simulated.
32 devices in a mesh: dp: 4 (over z), seq: 8 (over y, x, core).
Axes of the slice: x: 2, y: 2, z: 4, core: 2. Of those that a mesh axis runs over, the one named last changes fastest.
Arguments:
- tokens: bfloat16 [8, 1024, 1600], P('dp', 'seq'), may hold values from -6 to 6
- lengths: int32 [8], P('dp'), may hold values from 256 to 1024, as said below
- cotangent: bfloat16 [8, 1024, 1600], P('dp', 'seq'), may hold values from -6 to 6
- w_qkv: bfloat16 [1600, 2240], P('seq'), may hold values from -0.15625 to 0.15625
- w_ao: bfloat16 [1600, 1600], P('seq'), may hold values from -0.15625 to 0.15625
- w_in: bfloat16 [1600, 6400], P('seq'), may hold values from -0.15625 to 0.15625
- w_xp: bfloat16 [3200, 132], P('seq'), may hold values from -0.21875 to 0.21875
- w_dt: bfloat16 [100, 3200], replicated, may hold values from -0.625 to 0.625
- w_so: bfloat16 [3200, 1600], P('seq'), may hold values from -0.109375 to 0.109375
- w_gu: bfloat16 [1600, 2, 5504], P(None, None, 'seq'), may hold values from -0.15625 to 0.15625
- w_down: bfloat16 [5504, 1600], P('seq'), may hold values from -0.15625 to 0.15625
- norm_in: float32 [1600], replicated, may hold values from 0.5 to 1.5
- norm_attn: float32 [1600], replicated, may hold values from 0.5 to 1.5
- norm_ssm: float32 [3200], replicated, may hold values from 0.5 to 1.5
- norm_ffn: float32 [1600], replicated, may hold values from 0.5 to 1.5
- conv_w: float32 [4, 3200], replicated, may hold values from -3 to 3
- conv_b: float32 [3200], replicated, may hold values from -0.5 to 0.5
- dt_bias: float32 [3200], replicated, may hold values from -6 to -2
- a_log: float32 [16, 3200], replicated, may hold values from -3 to 2.5
- d_skip: float32 [3200], replicated, may hold values from 0.5 to 1.5
Outputs:
- block_out: bfloat16 [8, 1024, 1600], P('dp', 'seq')
- grad_tokens: float32 [8, 1024, 1600], P('dp', 'seq')
- grad_w_qkv: float32 [1600, 2240], P('seq')
- grad_w_ao: float32 [1600, 1600], P('seq')
- grad_w_in: float32 [1600, 6400], P('seq')
- grad_w_xp: float32 [3200, 132], P('seq')
- grad_w_dt: float32 [100, 3200], P(None, 'seq')
- grad_w_so: float32 [3200, 1600], P('seq')
- grad_w_gu: float32 [1600, 2, 5504], P(None, None, 'seq')
- grad_w_down: float32 [5504, 1600], P('seq')
- grad_norm_in: float32 [1600], P('seq')
- grad_norm_attn: float32 [1600], P('seq')
- grad_norm_ssm: float32 [3200], P('seq')
- grad_norm_ffn: float32 [1600], P('seq')
- grad_conv_w: float32 [4, 3200], P(None, 'seq')
- grad_conv_b: float32 [3200], P('seq')
- grad_dt_bias: float32 [3200], P('seq')
- grad_a_log: float32 [16, 3200], P(None, 'seq')
- grad_d_skip: float32 [3200], P('seq')
Inputs may be any that keep to these rules, and one draw needn't show every extreme that they name: `lengths`: in each aligned group of 2 sequences (one dp index) one sequence, which one drawn from the seed, has length 1024; one other sequence of some group has length 256.
All inputs are finite; a program needn't handle non-finite values.
Results may differ from a plain program's by a relative error of at most 0.025.
Values may be sent and summed in bfloat16 or wider, within the bound.
A program may use at most 512 MiB of HBM per device.

v0:
```python
import math

import jax
import jax.numpy as jnp
from jax import lax
from jax.sharding import PartitionSpec as P

HEADS = 25
HEAD = 64
KVH = 5
INNER = 3200
NST = 16
KCONV = 4
DTR = 100


EPSILON = 1e-05
NEGATIVE = -1e30


def shifted(value, axis, steps):
    count = lax.axis_size(axis)
    leading, last = (max(0, -steps), min(count, count - steps))
    return lax.ppermute(value, axis, [(source, source + steps) for source in range(leading, last)])


def carried_in_2(array, axis, join, neutral):
    place = lax.axis_index(axis)
    gathered = jax.tree.map(
        lambda a, kind: lax.all_gather(a.astype(kind), axis), array, (jnp.bfloat16, jnp.bfloat16)
    )
    state = jax.tree.map(lambda a, e: jnp.zeros_like(a) + jnp.asarray(e, a.dtype), array, neutral)

    def one(step, state):
        return join(
            state,
            jax.tree.map(
                lambda a, own: lax.dynamic_index_in_dim(a, step, 0, False).astype(own.dtype),
                gathered,
                array,
            ),
        )

    return lax.fori_loop(0, place, one, state)


def prefix(array, axis, combine, identity):
    length, here = (lax.axis_size(axis), lax.axis_index(axis))
    everything = jax.tree.map(
        lambda part, kind: lax.all_gather(part.astype(kind), axis),
        array,
        jax.tree.map(lambda a: jnp.bfloat16 if a.dtype == jnp.float32 else a.dtype, array),
    )
    start = jax.tree.map(
        lambda part, zero: jnp.broadcast_to(jnp.asarray(zero, part.dtype), part.shape),
        array,
        identity,
    )

    def step(k, before):
        at = length - 1 - k
        reached = at > here
        new = combine(
            before, jax.tree.map(lambda part, own: part[at].astype(own.dtype), everything, array)
        )
        return jax.tree.map(lambda a, b: jnp.where(reached, a, b), new, before)

    return lax.fori_loop(0, length, step, start)


def for_sending(array):
    return jax.tree.map(lambda a: a.astype(jnp.bfloat16) if a.dtype == jnp.float32 else a, array)


def scaled_norm(values, gain):
    return values * lax.rsqrt(jnp.mean(values * values, axis=-1, keepdims=True) + EPSILON) * gain


def silu_grad(values):
    logistic = jax.nn.sigmoid(values)
    return logistic * (1.0 + values * (1.0 - logistic))


def chain_states(earlier, later):
    return (earlier[0] * later[0], later[0] * earlier[1] + later[1])


def gather_weights(w_qkv, w_ao, w_in, w_xp, w_so):
    return (
        lax.all_gather(w_qkv, "seq", axis=0, tiled=True),
        lax.all_gather(w_ao, "seq", axis=0, tiled=True),
        lax.all_gather(w_in, "seq", axis=0, tiled=True),
        lax.all_gather(w_xp, "seq", axis=0, tiled=True),
        lax.all_gather(w_so, "seq", axis=0, tiled=True),
    )


def local_scan(step_size, b_input, c_output, inputs, decay_rate, initial):

    def advance(carried, current):
        step_now, b_now, c_now, input_now = current
        carried = (
            jnp.exp(step_now[:, None, :] * decay_rate[None]) * carried
            + b_now[:, :, None] * (step_now * input_now)[:, None, :]
        )
        return (carried, jnp.sum(c_now[:, :, None] * carried, axis=1))

    @jax.checkpoint
    def run_block(carried, block_series):
        return lax.scan(advance, carried, block_series, unroll=4)

    length = step_size.shape[1]
    block = math.gcd(length, 16)
    series = tuple(
        (
            jnp.swapaxes(v, 0, 1).reshape((length // block, block, v.shape[0], v.shape[2]))
            for v in (step_size, b_input, c_output, inputs)
        )
    )
    final_state, results = lax.scan(run_block, initial, series)
    results = results.reshape((length,) + results.shape[2:])
    return (jnp.swapaxes(results, 0, 1), final_state)


def per_device(
    tokens,
    lengths,
    cotangent,
    w_qkv,
    w_ao,
    w_in,
    w_xp,
    w_dt,
    w_so,
    w_gu,
    w_down,
    norm_in,
    norm_attn,
    norm_ssm,
    norm_ffn,
    conv_w,
    conv_b,
    dt_bias,
    a_log,
    d_skip,
):
    seq_count, slot_len, model_width = tokens.shape
    group_size = lax.axis_size("seq")
    shard_index = lax.axis_index("seq")
    row_count = seq_count * slot_len
    capacity = slot_len * group_size
    query_dim = HEADS * HEAD
    kv_dim = KVH * HEAD
    group_heads = HEADS // KVH
    score_scale = HEAD ** (-0.5)
    key_block = math.gcd(capacity, 512)
    block_count = capacity // key_block
    rim_rows = KCONV - 1
    hidden_part = w_down.shape[0]
    gate_up_cols = w_gu.reshape(model_width, 2 * hidden_part)
    full_qkv, full_ao, full_in, full_xp, full_so = gather_weights(w_qkv, w_ao, w_in, w_xp, w_so)
    query_pos = shard_index * slot_len + jnp.arange(slot_len, dtype=jnp.int32)
    is_valid = query_pos[None, :] < lengths[:, None]
    x_float = tokens.astype(jnp.float32).reshape(row_count, model_width)
    normed = scaled_norm(x_float, norm_in).astype(jnp.bfloat16)
    qkv_out = jnp.dot(normed, full_qkv, preferred_element_type=jnp.float32)
    queries = (
        qkv_out[:, :query_dim]
        .astype(jnp.bfloat16)
        .reshape(seq_count, slot_len, KVH, group_heads, HEAD)
    )
    kv_local = qkv_out[:, query_dim:].astype(jnp.bfloat16).reshape(seq_count, slot_len, 2 * kv_dim)
    kv_whole = lax.all_gather(kv_local, "seq", axis=1, tiled=True)

    def block_scores(block_index):
        kv_piece = lax.dynamic_slice_in_dim(kv_whole, block_index * key_block, key_block, 1)
        key_part = kv_piece[:, :, :kv_dim].reshape(seq_count, key_block, KVH, HEAD)
        value_part = kv_piece[:, :, kv_dim:].reshape(seq_count, key_block, KVH, HEAD)
        key_pos = block_index * key_block + jnp.arange(key_block, dtype=jnp.int32)
        allowed = (key_pos[None, None, :] <= query_pos[None, :, None]) & (
            key_pos[None, None, :] < lengths[:, None, None]
        )
        allowed = allowed[:, None, None]
        scores = (
            jnp.einsum("stgrd,sjgd->sgrtj", queries, key_part, preferred_element_type=jnp.float32)
            * score_scale
        )
        return (jnp.where(allowed, scores, NEGATIVE), allowed, key_part, value_part)

    def max_pass(block_index, carried):
        highest, denominator = carried
        scores, allowed, key_part, value_part = block_scores(block_index)
        updated = jnp.maximum(highest, jnp.max(scores, axis=-1))
        exponent = jnp.where(allowed, jnp.exp(scores - updated[..., None]), 0.0)
        denominator = denominator * jnp.exp(highest - updated) + jnp.sum(exponent, axis=-1)
        return (updated, denominator)

    stat_shape = (seq_count, KVH, group_heads, slot_len)
    highest, denominator = lax.fori_loop(
        0,
        block_count,
        max_pass,
        (jnp.full(stat_shape, NEGATIVE, jnp.float32), jnp.zeros(stat_shape, jnp.float32)),
    )
    log_total = highest + jnp.log(denominator)

    def value_pass(block_index, accum):
        scores, allowed, key_part, value_part = block_scores(block_index)
        weights = jnp.where(allowed, jnp.exp(scores - log_total[..., None]), 0.0).astype(
            jnp.bfloat16
        )
        return accum + jnp.einsum(
            "sgrtj,sjgd->sgrtd", weights, value_part, preferred_element_type=jnp.float32
        )

    accum = lax.fori_loop(0, block_count, value_pass, jnp.zeros(stat_shape + (HEAD,), jnp.float32))
    attended = jnp.transpose(accum, (0, 3, 1, 2, 4)).reshape(row_count, query_dim)
    attn_low = scaled_norm(attended, norm_attn).astype(jnp.bfloat16)
    x_and_z = jnp.dot(normed, full_in, preferred_element_type=jnp.float32)
    x_conv = x_and_z[:, :INNER].astype(jnp.bfloat16).reshape(seq_count, slot_len, INNER)
    z_gate = x_and_z[:, INNER:].reshape(seq_count, slot_len, INNER)
    left_rows = shifted(x_conv[:, slot_len - rim_rows :, :], "seq", 1)
    padded = jnp.concatenate([left_rows, x_conv], axis=1).astype(jnp.float32)
    conv_pre = conv_b + sum(
        (conv_w[offset] * padded[:, offset : offset + slot_len] for offset in range(KCONV))
    )
    mixer_in = jax.nn.silu(conv_pre)
    mixer_low = mixer_in.astype(jnp.bfloat16).reshape(row_count, INNER)
    projected = jnp.dot(mixer_low, full_xp, preferred_element_type=jnp.float32)
    step_low = projected[:, :DTR].astype(jnp.bfloat16)
    step_pre = jnp.dot(step_low, w_dt, preferred_element_type=jnp.float32) + dt_bias
    step_size = jax.nn.softplus(step_pre).reshape(seq_count, slot_len, INNER)
    b_input = projected[:, DTR : DTR + NST].reshape(seq_count, slot_len, NST)
    c_output = projected[:, DTR + NST :].reshape(seq_count, slot_len, NST)
    decay_rate = -jnp.exp(a_log)
    zero_state = jnp.zeros((seq_count, NST, INNER), jnp.float32)
    scanned, end_state = local_scan(step_size, b_input, c_output, mixer_in, decay_rate, zero_state)
    elapsed = jnp.cumsum(step_size, axis=1)
    through = jnp.exp(decay_rate[None] * elapsed[:, -1][:, None, :])
    carried_in = carried_in_2(
        (through, end_state),
        "seq",
        chain_states,
        (jnp.ones_like(through), jnp.zeros_like(end_state)),
    )
    incoming = carried_in[1]
    correction = jnp.zeros_like(scanned)
    for state_index in range(NST):
        correction = (
            correction
            + c_output[:, :, state_index : state_index + 1]
            * jnp.exp(decay_rate[state_index] * elapsed)
            * incoming[:, None, state_index, :]
        )
    mamba_core = scanned + correction + d_skip * mixer_in
    gated_out = (mamba_core * jax.nn.silu(z_gate)).reshape(row_count, INNER)
    ssm_low = scaled_norm(gated_out, norm_ssm).astype(jnp.bfloat16)
    mixed_out = 0.5 * (
        jnp.dot(attn_low, full_ao, preferred_element_type=jnp.float32)
        + jnp.dot(ssm_low, full_so, preferred_element_type=jnp.float32)
    )
    residual = x_float + mixed_out
    normed_two = scaled_norm(residual, norm_ffn).astype(jnp.bfloat16)
    normed_all = lax.all_gather(normed_two, "seq", axis=0, tiled=True)
    gate_up = jnp.dot(normed_all, gate_up_cols, preferred_element_type=jnp.float32)
    gate_part = gate_up[:, :hidden_part]
    up_part = gate_up[:, hidden_part:]
    activated = (jax.nn.silu(gate_part) * up_part).astype(jnp.bfloat16)
    ffn_sum = lax.psum_scatter(
        jnp.dot(activated, w_down, preferred_element_type=jnp.float32).astype(jnp.bfloat16),
        "seq",
        scatter_dimension=0,
        tiled=True,
    ).astype(jnp.float32)
    block_out = residual + ffn_sum
    result_tokens = block_out.astype(jnp.bfloat16).reshape(seq_count, slot_len, model_width)
    full_qkv, full_ao, full_in, full_xp, full_so = gather_weights(w_qkv, w_ao, w_in, w_xp, w_so)
    upstream = (cotangent.astype(jnp.float32) * is_valid[..., None]).reshape(row_count, model_width)
    upstream_low = upstream.astype(jnp.bfloat16)
    upstream_all = lax.all_gather(upstream_low, "seq", axis=0, tiled=True)
    grad_down = jnp.einsum("tf,td->fd", activated, upstream_all, preferred_element_type=jnp.float32)
    grad_act = jnp.einsum("td,fd->tf", upstream_all, w_down, preferred_element_type=jnp.float32)
    grad_gate_up = jnp.concatenate(
        [grad_act * up_part * silu_grad(gate_part), grad_act * jax.nn.silu(gate_part)], axis=1
    ).astype(jnp.bfloat16)
    grad_gu = jnp.einsum(
        "td,tf->df", normed_all, grad_gate_up, preferred_element_type=jnp.float32
    ).reshape(model_width, 2, hidden_part)
    grad_normed_two = lax.psum_scatter(
        jnp.einsum(
            "tf,df->td", grad_gate_up, gate_up_cols, preferred_element_type=jnp.float32
        ).astype(jnp.bfloat16),
        "seq",
        scatter_dimension=0,
        tiled=True,
    ).astype(jnp.float32)
    _, ffn_pull = jax.vjp(scaled_norm, residual, norm_ffn)
    grad_res_add, grad_norm_ffn = ffn_pull(grad_normed_two)
    grad_residual = upstream + grad_res_add
    mix_low = grad_residual.astype(jnp.bfloat16)
    grad_ao = 0.5 * jnp.einsum("tq,td->qd", attn_low, mix_low, preferred_element_type=jnp.float32)
    grad_so = 0.5 * jnp.einsum("tc,td->cd", ssm_low, mix_low, preferred_element_type=jnp.float32)
    grad_attn_low = 0.5 * jnp.einsum(
        "td,qd->tq", mix_low, full_ao, preferred_element_type=jnp.float32
    )
    grad_ssm_low = 0.5 * jnp.einsum(
        "td,cd->tc", mix_low, full_so, preferred_element_type=jnp.float32
    )
    _, attn_pull = jax.vjp(scaled_norm, attended, norm_attn)
    grad_attended, grad_norm_attn = attn_pull(grad_attn_low)
    _, ssm_pull = jax.vjp(scaled_norm, gated_out, norm_ssm)
    grad_gated, grad_norm_ssm = ssm_pull(grad_ssm_low)
    grad_heads = jnp.transpose(
        grad_attended.reshape(seq_count, slot_len, KVH, group_heads, HEAD), (0, 2, 3, 1, 4)
    ).astype(jnp.bfloat16)
    row_delta = jnp.sum(grad_heads.astype(jnp.float32) * accum, axis=-1)

    def grad_pass(block_index, carried):
        grad_query, key_value_grads = carried
        scores, allowed, key_part, value_part = block_scores(block_index)
        probs = jnp.where(allowed, jnp.exp(scores - log_total[..., None]), 0.0)
        probs_low = probs.astype(jnp.bfloat16)
        grad_probs = jnp.einsum(
            "sgrtd,sjgd->sgrtj", grad_heads, value_part, preferred_element_type=jnp.float32
        )
        grad_scores = (probs * (grad_probs - row_delta[..., None])).astype(jnp.bfloat16)
        grad_query = (
            grad_query
            + jnp.einsum(
                "sgrtj,sjgd->sgrtd", grad_scores, key_part, preferred_element_type=jnp.float32
            )
            * score_scale
        )
        grad_keys = (
            jnp.einsum(
                "sgrtj,stgrd->sjgd", grad_scores, queries, preferred_element_type=jnp.float32
            )
            * score_scale
        )
        grad_values = jnp.einsum(
            "sgrtj,sgrtd->sjgd", probs_low, grad_heads, preferred_element_type=jnp.float32
        )
        update = jnp.concatenate(
            [
                grad_keys.reshape(seq_count, key_block, kv_dim),
                grad_values.reshape(seq_count, key_block, kv_dim),
            ],
            axis=2,
        )
        key_value_grads = lax.dynamic_update_slice_in_dim(
            key_value_grads, update, block_index * key_block, 1
        )
        return (grad_query, key_value_grads)

    grad_query, key_value_grads = lax.fori_loop(
        0,
        block_count,
        grad_pass,
        (
            jnp.zeros(stat_shape + (HEAD,), jnp.float32),
            jnp.zeros((seq_count, capacity, 2 * kv_dim), jnp.float32),
        ),
    )
    kv_home = lax.psum_scatter(
        key_value_grads.astype(jnp.bfloat16), "seq", scatter_dimension=1, tiled=True
    ).astype(jnp.float32)
    grad_q_rows = jnp.transpose(grad_query, (0, 3, 1, 2, 4)).reshape(row_count, query_dim)
    grad_qkv_low = jnp.concatenate(
        [grad_q_rows, kv_home.reshape(row_count, 2 * kv_dim)], axis=1
    ).astype(jnp.bfloat16)
    grad_qkv = jnp.einsum("tm,tq->mq", normed, grad_qkv_low, preferred_element_type=jnp.float32)
    grad_normed = jnp.einsum(
        "tq,mq->tm", grad_qkv_low, full_qkv, preferred_element_type=jnp.float32
    )
    grad_gated = grad_gated.reshape(seq_count, slot_len, INNER)
    grad_core = grad_gated * jax.nn.silu(z_gate)
    grad_z = grad_gated * mamba_core * silu_grad(z_gate)
    state_terms = jnp.stack(
        [
            jnp.sum(
                c_output[:, :, state_index : state_index + 1]
                * grad_core
                * jnp.exp(decay_rate[state_index] * elapsed),
                axis=1,
            )
            for state_index in range(NST)
        ],
        axis=1,
    )
    later_in = prefix(
        (through, state_terms),
        "seq",
        chain_states,
        (jnp.ones_like(through), jnp.zeros_like(state_terms)),
    )
    later = later_in[1]
    _, scan_pull = jax.vjp(local_scan, step_size, b_input, c_output, mixer_in, decay_rate, incoming)
    grad_step, grad_b, grad_c, grad_mixer, grad_rate, _ = scan_pull((grad_core, later))
    grad_skip = jnp.sum(grad_core * mixer_in, axis=(0, 1))
    grad_mixer = grad_mixer + d_skip * grad_core
    grad_a_log = grad_rate * decay_rate
    grad_step_pre = grad_step.reshape(row_count, INNER) * jax.nn.sigmoid(step_pre)
    grad_dt_bias = jnp.sum(grad_step_pre, axis=0)
    grad_step_low = grad_step_pre.astype(jnp.bfloat16)
    grad_wdt = jnp.einsum("tr,tc->rc", step_low, grad_step_low, preferred_element_type=jnp.float32)
    grad_step_in = jnp.einsum("tc,rc->tr", grad_step_low, w_dt, preferred_element_type=jnp.float32)
    grad_projected = jnp.concatenate(
        [grad_step_in, grad_b.reshape(row_count, NST), grad_c.reshape(row_count, NST)], axis=1
    ).astype(jnp.bfloat16)
    grad_xp = jnp.einsum("tc,tp->cp", mixer_low, grad_projected, preferred_element_type=jnp.float32)
    grad_mixer = grad_mixer + jnp.einsum(
        "tp,cp->tc", grad_projected, full_xp, preferred_element_type=jnp.float32
    ).reshape(seq_count, slot_len, INNER)
    grad_conv_pre = grad_mixer * silu_grad(conv_pre)
    grad_conv_b = jnp.sum(grad_conv_pre, axis=(0, 1))
    grad_conv_w = jnp.stack(
        [
            jnp.sum(grad_conv_pre * padded[:, offset : offset + slot_len], axis=(0, 1))
            for offset in range(KCONV)
        ],
        axis=0,
    )
    grad_padded = sum(
        (
            jnp.pad(conv_w[offset] * grad_conv_pre, ((0, 0), (offset, rim_rows - offset), (0, 0)))
            for offset in range(KCONV)
        )
    )
    returned = shifted(for_sending(grad_padded[:, :rim_rows]), "seq", -1)
    grad_x_conv = grad_padded[:, rim_rows:] + jnp.pad(
        returned, ((0, 0), (slot_len - rim_rows, 0), (0, 0))
    )
    grad_xz = (
        jnp.concatenate([grad_x_conv, grad_z], axis=2)
        .reshape(row_count, 2 * INNER)
        .astype(jnp.bfloat16)
    )
    grad_in = jnp.einsum("tm,tc->mc", normed, grad_xz, preferred_element_type=jnp.float32)
    grad_normed = grad_normed + jnp.einsum(
        "tc,mc->tm", grad_xz, full_in, preferred_element_type=jnp.float32
    )
    _, input_pull = jax.vjp(scaled_norm, x_float, norm_in)
    grad_x_add, grad_norm_in = input_pull(grad_normed)
    grad_tokens = (grad_residual + grad_x_add).reshape(seq_count, slot_len, model_width)
    mix_shards = (
        lax.psum_scatter(
            grad_qkv.astype(jnp.bfloat16), "seq", scatter_dimension=0, tiled=True
        ).astype(jnp.float32),
        lax.psum_scatter(
            grad_ao.astype(jnp.bfloat16), "seq", scatter_dimension=0, tiled=True
        ).astype(jnp.float32),
        lax.psum_scatter(
            grad_in.astype(jnp.bfloat16), "seq", scatter_dimension=0, tiled=True
        ).astype(jnp.float32),
        lax.psum_scatter(
            grad_xp.astype(jnp.bfloat16), "seq", scatter_dimension=0, tiled=True
        ).astype(jnp.float32),
        lax.psum_scatter(
            grad_so.astype(jnp.bfloat16), "seq", scatter_dimension=0, tiled=True
        ).astype(jnp.float32),
        lax.psum_scatter(
            grad_wdt.astype(jnp.bfloat16), "seq", scatter_dimension=1, tiled=True
        ).astype(jnp.float32),
        lax.psum_scatter(
            grad_norm_in.astype(jnp.bfloat16), "seq", scatter_dimension=0, tiled=True
        ).astype(jnp.float32),
        lax.psum_scatter(
            grad_norm_attn.astype(jnp.bfloat16), "seq", scatter_dimension=0, tiled=True
        ).astype(jnp.float32),
        lax.psum_scatter(
            grad_norm_ssm.astype(jnp.bfloat16), "seq", scatter_dimension=0, tiled=True
        ).astype(jnp.float32),
        lax.psum_scatter(
            grad_norm_ffn.astype(jnp.bfloat16), "seq", scatter_dimension=0, tiled=True
        ).astype(jnp.float32),
        lax.psum_scatter(
            grad_conv_w.astype(jnp.bfloat16), "seq", scatter_dimension=1, tiled=True
        ).astype(jnp.float32),
        lax.psum_scatter(
            grad_conv_b.astype(jnp.bfloat16), "seq", scatter_dimension=0, tiled=True
        ).astype(jnp.float32),
        lax.psum_scatter(
            grad_dt_bias.astype(jnp.bfloat16), "seq", scatter_dimension=0, tiled=True
        ).astype(jnp.float32),
        lax.psum_scatter(
            grad_a_log.astype(jnp.bfloat16), "seq", scatter_dimension=1, tiled=True
        ).astype(jnp.float32),
        lax.psum_scatter(
            grad_skip.astype(jnp.bfloat16), "seq", scatter_dimension=0, tiled=True
        ).astype(jnp.float32),
    )
    quarters = (
        lax.psum_scatter(
            mix_shards[0].astype(jnp.bfloat16), "dp", scatter_dimension=1, tiled=True
        ).astype(jnp.float32),
        lax.psum_scatter(
            mix_shards[1].astype(jnp.bfloat16), "dp", scatter_dimension=1, tiled=True
        ).astype(jnp.float32),
        lax.psum_scatter(
            mix_shards[2].astype(jnp.bfloat16), "dp", scatter_dimension=1, tiled=True
        ).astype(jnp.float32),
        lax.psum_scatter(
            mix_shards[3].astype(jnp.bfloat16), "dp", scatter_dimension=1, tiled=True
        ).astype(jnp.float32),
        lax.psum_scatter(
            mix_shards[4].astype(jnp.bfloat16), "dp", scatter_dimension=1, tiled=True
        ).astype(jnp.float32),
        lax.psum_scatter(
            grad_gu.astype(jnp.bfloat16), "dp", scatter_dimension=0, tiled=True
        ).astype(jnp.float32),
        lax.psum_scatter(
            grad_down.astype(jnp.bfloat16), "dp", scatter_dimension=1, tiled=True
        ).astype(jnp.float32),
    )
    large = (
        lax.all_gather(quarters[0].astype(jnp.bfloat16), "dp", axis=1, tiled=True).astype(
            jnp.float32
        ),
        lax.all_gather(quarters[1].astype(jnp.bfloat16), "dp", axis=1, tiled=True).astype(
            jnp.float32
        ),
        lax.all_gather(quarters[2].astype(jnp.bfloat16), "dp", axis=1, tiled=True).astype(
            jnp.float32
        ),
        lax.all_gather(quarters[3].astype(jnp.bfloat16), "dp", axis=1, tiled=True).astype(
            jnp.float32
        ),
        lax.all_gather(quarters[4].astype(jnp.bfloat16), "dp", axis=1, tiled=True).astype(
            jnp.float32
        ),
        lax.all_gather(quarters[5].astype(jnp.bfloat16), "dp", axis=0, tiled=True).astype(
            jnp.float32
        ),
        lax.all_gather(quarters[6].astype(jnp.bfloat16), "dp", axis=1, tiled=True).astype(
            jnp.float32
        ),
    )
    small = (
        lax.psum(mix_shards[5].astype(jnp.bfloat16), "dp").astype(jnp.float32),
        lax.psum(mix_shards[6].astype(jnp.bfloat16), "dp").astype(jnp.float32),
        lax.psum(mix_shards[7].astype(jnp.bfloat16), "dp").astype(jnp.float32),
        lax.psum(mix_shards[8].astype(jnp.bfloat16), "dp").astype(jnp.float32),
        lax.psum(mix_shards[9].astype(jnp.bfloat16), "dp").astype(jnp.float32),
        lax.psum(mix_shards[10].astype(jnp.bfloat16), "dp").astype(jnp.float32),
        lax.psum(mix_shards[11].astype(jnp.bfloat16), "dp").astype(jnp.float32),
        lax.psum(mix_shards[12].astype(jnp.bfloat16), "dp").astype(jnp.float32),
        lax.psum(mix_shards[13].astype(jnp.bfloat16), "dp").astype(jnp.float32),
        lax.psum(mix_shards[14].astype(jnp.bfloat16), "dp").astype(jnp.float32),
    )
    return (
        result_tokens,
        grad_tokens,
        large[0],
        large[1],
        large[2],
        large[3],
        small[0],
        large[4],
        large[5],
        large[6],
        small[1],
        small[2],
        small[3],
        small[4],
        small[5],
        small[6],
        small[7],
        small[8],
        small[9],
    )


def solution(mesh):
    in_specs = (
        P("dp", "seq", None),
        P("dp"),
        P("dp", "seq", None),
        P("seq", None),
        P("seq", None),
        P("seq", None),
        P("seq", None),
        P(),
        P("seq", None),
        P(None, None, "seq"),
        P("seq", None),
        P(),
        P(),
        P(),
        P(),
        P(),
        P(),
        P(),
        P(),
        P(),
    )
    out_specs = (
        P("dp", "seq", None),
        P("dp", "seq", None),
        P("seq", None),
        P("seq", None),
        P("seq", None),
        P("seq", None),
        P(None, "seq"),
        P("seq", None),
        P(None, None, "seq"),
        P("seq", None),
        P("seq"),
        P("seq"),
        P("seq"),
        P("seq"),
        P(None, "seq"),
        P("seq"),
        P("seq"),
        P(None, "seq"),
        P("seq"),
    )
    return jax.shard_map(
        per_device, mesh=mesh, in_specs=in_specs, out_specs=out_specs, check_vma=False
    )
```

profile of v0, /device:TPU:0, one launch (start us, length us, event | category | flops | bytes accessed | tf_op | source)
XLA Modules:
  0.0 3113.2 jit_solution(4889915486508824891)
XLA Ops:
  9.5 53.2 %all-gather.20.cloned.1.call-done = bf16[1600,2240]{1,0:T(8,128)(2,1)} async-done(((bf16[200,2240]{1,0:T(8,128)(2,1)}), bf16[1600,2240]{1,0:T(8,128)(2,1)}) %all-gather.20.cloned.1.call-update) | async-done | bytes 7168016 | tf_op jit(solution)/shard_map/all_gather | solution.py:90
  71.7 17.7 all-gather.1
  90.2 83.5 %all-gather.26.cloned.1.call-done = bf16[1600,6400]{1,0:T(8,128)(2,1)} async-done(((bf16[200,6400]{1,0:T(8,128)(2,1)}), bf16[1600,6400]{1,0:T(8,128)(2,1)}) %all-gather.26.cloned.1.call-update) | async-done | bytes 20480016 | tf_op jit(solution)/shard_map/all_gather | solution.py:92
  173.7 10.8 fusion.176
  229.2 110.3 %while.261 = (s32[]{:T(128)}, f32[2,16,3200]{2,1,0:T(8,128)S(1)}, f32[8,16,2,3200]{3,1,0,2:T(8,128)}, f32[8,16,2,3200]{3,2,1,0:T(2,128)}, f32[8,16,2,16]{3,2,1,0...) while((s32[]{:T(128)}, f32[2,16,3200]{2,1,0:T(8,128)S(1)}, ...), condition=%wide.region_15.16_spmd, body=%wide.region_8.15_spmd.sunk | while | flops 2534407 | bytes 4517358 | solution.py:120
  344.8 33.4 %while.265 = (s32[]{:T(128)}, f32[2,5,5,128]{3,2,1,0:T(8,128)S(1)}, f32[2,5,5,128]{3,2,1,0:T(8,128)S(1)}, s32[2]{0:T(128)S(1)}, bf16[2,1024,640]{1,2,0:T(8,128)(...) while((s32[]{:T(128)}, f32[2,5,5,128]{3,2,1,0:T(8,128)S(1)}, ...), condition=%wide.region_4.5_spmd.clone, body=%wide.region_1.4_spmd.clone.sunk | while | flops 445875072 | bytes 29866176 | solution.py:199
  378.3 19.7 while.266
  415.5 19.9 multiply_reduce_fusion.42
  453.2 53.3 %all-gather.32.cloned.1.call-done = bf16[2048,1600]{0,1:T(8,128)(2,1)} async-done(((bf16[256,1600]{0,1:T(8,128)(2,1)}), bf16[2048,1600]{0,1:T(8,128)(2,1)}) %all-gather.32.cloned.1.call-update) | async-done | bytes 6553616 | tf_op jit(solution)/shard_map/all_gather | solution.py:264
  506.5 16.4 fusion.178
  522.9 33.9 %all-gather.34.cloned.1.call-done = bf16[2048,1600]{0,1:T(8,128)(2,1)} async-done(((bf16[256,1600]{0,1:T(8,128)(2,1)}), bf16[2048,1600]{0,1:T(8,128)(2,1)}) %all-gather.34.cloned.1.call-update) | async-done | bytes 6553616 | tf_op jit(solution)/shard_map/all_gather | solution.py:280
  556.8 12.7 multiply_convert_fusion.3
  572.0 14.6 convolution_convert_fusion.3
  587.3 62.5 %reduce-scatter.39.cloned.1.call-done = bf16[256,1600]{0,1:T(8,128)(2,1)} async-done(((bf16[2048,1600]{0,1:T(8,128)(2,1)}), bf16[256,1600]{0,1:T(8,128)(2,1)}) %reduce-scatter.39.cloned.1.call-update) | async-done | bytes 819216 | tf_op jit(solution)/shard_map/reduce_scatter | solution.py:289
  655.6 13.4 multiply_reduce_fusion.25
  669.5 11.0 multiply_reduce_fusion.26
  688.3 99.3 %while.264 = (s32[]{:T(128)}, f32[2,16,3200]{2,1,0:T(8,128)S(1)}, f32[8,2,16,3200]{3,2,1,0:T(8,128)}, f32[8,16,2,3200]{3,2,1,0:T(2,128)}, f32[8,16,2,16]{3,2,1,0...) while((s32[]{:T(128)}, f32[2,16,3200]{2,1,0:T(8,128)S(1)}, ...), condition=%wide.region_51.52_spmd, body=%wide.region_48.51_spmd.sunk | while | flops 1664007 | bytes 4204490 | solution.py:120
  800.3 11.2 while.268
  817.5 895.6 %while.271 = (s32[]{:T(128)}, f32[16,3200]{1,0:T(8,128)}, f32[2,16,3200]{2,1,0:T(8,128)S(1)}, f32[8,16,2,3200]{3,2,1,0:T(2,128)}, bf16[8,16,2,16]{3,2,1,0:T(2,12...) while((s32[]{:T(128)}, f32[16,3200]{1,0:T(8,128)}, ...), condition=%wide.region_77.78_spmd.clone, body=%wide.region_52.77_spmd.clone.sunk | while | flops 12623376 | bytes 39926928 | solution.py:120
  823.4 31.5 %while.274 = (s32[]{:T(128)}, f32[2,16,3200]{2,1,0:T(8,128)S(1)}, f32[4,4,2,16,3200]{4,3,2,1,0:T(8,128)}, f32[4,4,2,16,1]{3,2,1,4,0:T(2,128)}, f32[4,4,2,1,3200]...) while((s32[]{:T(128)}, f32[2,16,3200]{2,1,0:T(8,128)S(1)}, ...), condition=%wide.region_54.54_spmd, body=%wide.region_53.53_spmd.sunk | while | flops 5939973 | bytes 15167801 | solution.py:110
  857.8 63.7 %while.275 = (s32[]{:T(128)}, f32[16,3200]{1,0:T(8,128)}, f32[2,16,3200]{2,1,0:T(8,128)S(1)}, f32[4,4,2,3200]{3,2,1,0:T(2,128)}, bf16[4,4,2,16]{3,2,1,0:T(2,128)...) while((s32[]{:T(128)}, f32[16,3200]{1,0:T(8,128)}, ...), condition=%wide.region_76.76_spmd.clone, body=%wide.region_55.75_spmd.clone.sunk | while | flops 6580999 | bytes 17547424 | solution.py:110
  935.3 31.5 %while.274 = (s32[]{:T(128)}, f32[2,16,3200]{2,1,0:T(8,128)S(1)}, f32[4,4,2,16,3200]{4,3,2,1,0:T(8,128)}, f32[4,4,2,16,1]{3,2,1,4,0:T(2,128)}, f32[4,4,2,1,3200]...) while((s32[]{:T(128)}, f32[2,16,3200]{2,1,0:T(8,128)S(1)}, ...), condition=%wide.region_54.54_spmd, body=%wide.region_53.53_spmd.sunk | while | flops 5939973 | bytes 15167801 | solution.py:110
  969.7 63.7 %while.275 = (s32[]{:T(128)}, f32[16,3200]{1,0:T(8,128)}, f32[2,16,3200]{2,1,0:T(8,128)S(1)}, f32[4,4,2,3200]{3,2,1,0:T(2,128)}, bf16[4,4,2,16]{3,2,1,0:T(2,128)...) while((s32[]{:T(128)}, f32[16,3200]{1,0:T(8,128)}, ...), condition=%wide.region_76.76_spmd.clone, body=%wide.region_55.75_spmd.clone.sunk | while | flops 6580999 | bytes 17547424 | solution.py:110
  1047.2 31.5 %while.274 = (s32[]{:T(128)}, f32[2,16,3200]{2,1,0:T(8,128)S(1)}, f32[4,4,2,16,3200]{4,3,2,1,0:T(8,128)}, f32[4,4,2,16,1]{3,2,1,4,0:T(2,128)}, f32[4,4,2,1,3200]...) while((s32[]{:T(128)}, f32[2,16,3200]{2,1,0:T(8,128)S(1)}, ...), condition=%wide.region_54.54_spmd, body=%wide.region_53.53_spmd.sunk | while | flops 5939973 | bytes 15167801 | solution.py:110
  1081.6 63.7 %while.275 = (s32[]{:T(128)}, f32[16,3200]{1,0:T(8,128)}, f32[2,16,3200]{2,1,0:T(8,128)S(1)}, f32[4,4,2,3200]{3,2,1,0:T(2,128)}, bf16[4,4,2,16]{3,2,1,0:T(2,128)...) while((s32[]{:T(128)}, f32[16,3200]{1,0:T(8,128)}, ...), condition=%wide.region_76.76_spmd.clone, body=%wide.region_55.75_spmd.clone.sunk | while | flops 6580999 | bytes 17547424 | solution.py:110
  1159.1 31.5 %while.274 = (s32[]{:T(128)}, f32[2,16,3200]{2,1,0:T(8,128)S(1)}, f32[4,4,2,16,3200]{4,3,2,1,0:T(8,128)}, f32[4,4,2,16,1]{3,2,1,4,0:T(2,128)}, f32[4,4,2,1,3200]...) while((s32[]{:T(128)}, f32[2,16,3200]{2,1,0:T(8,128)S(1)}, ...), condition=%wide.region_54.54_spmd, body=%wide.region_53.53_spmd.sunk | while | flops 5939973 | bytes 15167801 | solution.py:110
  1193.5 63.7 %while.275 = (s32[]{:T(128)}, f32[16,3200]{1,0:T(8,128)}, f32[2,16,3200]{2,1,0:T(8,128)S(1)}, f32[4,4,2,3200]{3,2,1,0:T(2,128)}, bf16[4,4,2,16]{3,2,1,0:T(2,128)...) while((s32[]{:T(128)}, f32[16,3200]{1,0:T(8,128)}, ...), condition=%wide.region_76.76_spmd.clone, body=%wide.region_55.75_spmd.clone.sunk | while | flops 6580999 | bytes 17547424 | solution.py:110
  1271.1 31.5 %while.274 = (s32[]{:T(128)}, f32[2,16,3200]{2,1,0:T(8,128)S(1)}, f32[4,4,2,16,3200]{4,3,2,1,0:T(8,128)}, f32[4,4,2,16,1]{3,2,1,4,0:T(2,128)}, f32[4,4,2,1,3200]...) while((s32[]{:T(128)}, f32[2,16,3200]{2,1,0:T(8,128)S(1)}, ...), condition=%wide.region_54.54_spmd, body=%wide.region_53.53_spmd.sunk | while | flops 5939973 | bytes 15167801 | solution.py:110
  1305.5 63.7 %while.275 = (s32[]{:T(128)}, f32[16,3200]{1,0:T(8,128)}, f32[2,16,3200]{2,1,0:T(8,128)S(1)}, f32[4,4,2,3200]{3,2,1,0:T(2,128)}, bf16[4,4,2,16]{3,2,1,0:T(2,128)...) while((s32[]{:T(128)}, f32[16,3200]{1,0:T(8,128)}, ...), condition=%wide.region_76.76_spmd.clone, body=%wide.region_55.75_spmd.clone.sunk | while | flops 6580999 | bytes 17547424 | solution.py:110
  1383.0 31.5 %while.274 = (s32[]{:T(128)}, f32[2,16,3200]{2,1,0:T(8,128)S(1)}, f32[4,4,2,16,3200]{4,3,2,1,0:T(8,128)}, f32[4,4,2,16,1]{3,2,1,4,0:T(2,128)}, f32[4,4,2,1,3200]...) while((s32[]{:T(128)}, f32[2,16,3200]{2,1,0:T(8,128)S(1)}, ...), condition=%wide.region_54.54_spmd, body=%wide.region_53.53_spmd.sunk | while | flops 5939973 | bytes 15167801 | solution.py:110
  1417.4 63.7 %while.275 = (s32[]{:T(128)}, f32[16,3200]{1,0:T(8,128)}, f32[2,16,3200]{2,1,0:T(8,128)S(1)}, f32[4,4,2,3200]{3,2,1,0:T(2,128)}, bf16[4,4,2,16]{3,2,1,0:T(2,128)...) while((s32[]{:T(128)}, f32[16,3200]{1,0:T(8,128)}, ...), condition=%wide.region_76.76_spmd.clone, body=%wide.region_55.75_spmd.clone.sunk | while | flops 6580999 | bytes 17547424 | solution.py:110
  1494.9 31.5 %while.274 = (s32[]{:T(128)}, f32[2,16,3200]{2,1,0:T(8,128)S(1)}, f32[4,4,2,16,3200]{4,3,2,1,0:T(8,128)}, f32[4,4,2,16,1]{3,2,1,4,0:T(2,128)}, f32[4,4,2,1,3200]...) while((s32[]{:T(128)}, f32[2,16,3200]{2,1,0:T(8,128)S(1)}, ...), condition=%wide.region_54.54_spmd, body=%wide.region_53.53_spmd.sunk | while | flops 5939973 | bytes 15167801 | solution.py:110
  1529.3 63.7 %while.275 = (s32[]{:T(128)}, f32[16,3200]{1,0:T(8,128)}, f32[2,16,3200]{2,1,0:T(8,128)S(1)}, f32[4,4,2,3200]{3,2,1,0:T(2,128)}, bf16[4,4,2,16]{3,2,1,0:T(2,128)...) while((s32[]{:T(128)}, f32[16,3200]{1,0:T(8,128)}, ...), condition=%wide.region_76.76_spmd.clone, body=%wide.region_55.75_spmd.clone.sunk | while | flops 6580999 | bytes 17547424 | solution.py:110
  1606.9 31.5 %while.274 = (s32[]{:T(128)}, f32[2,16,3200]{2,1,0:T(8,128)S(1)}, f32[4,4,2,16,3200]{4,3,2,1,0:T(8,128)}, f32[4,4,2,16,1]{3,2,1,4,0:T(2,128)}, f32[4,4,2,1,3200]...) while((s32[]{:T(128)}, f32[2,16,3200]{2,1,0:T(8,128)S(1)}, ...), condition=%wide.region_54.54_spmd, body=%wide.region_53.53_spmd.sunk | while | flops 5939973 | bytes 15167801 | solution.py:110
  1641.3 63.7 %while.275 = (s32[]{:T(128)}, f32[16,3200]{1,0:T(8,128)}, f32[2,16,3200]{2,1,0:T(8,128)S(1)}, f32[4,4,2,3200]{3,2,1,0:T(2,128)}, bf16[4,4,2,16]{3,2,1,0:T(2,128)...) while((s32[]{:T(128)}, f32[16,3200]{1,0:T(8,128)}, ...), condition=%wide.region_76.76_spmd.clone, body=%wide.region_55.75_spmd.clone.sunk | while | flops 6580999 | bytes 17547424 | solution.py:110
  1722.1 75.4 %while.267 = (s32[]{:T(128)}, f32[2,5,5,128,64]{3,4,2,1,0:T(8,128)}, bf16[2,1024,640]{2,1,0:T(8,128)(2,1)}, s32[2]{0:T(128)S(1)}, bf16[2,1024,640]{1,2,0:T(8,128...) while((s32[]{:T(128)}, f32[2,5,5,128,64]{3,4,2,1,0:T(8,128)}, ...), condition=%wide.region_27.28_spmd.clone, body=%wide.region_26.27_spmd.clone.sunk | while | flops 2141177472 | bytes 161829296 | solution.py:355
  1843.3 12.9 bitcast_convert_fusion
  1863.9 16.0 convolution_convert_fusion.1
  1887.1 14.2 copy.158
  1912.8 18.9 reduce-scatter.47.cloned.1.call-done
  1935.3 48.2 %reduce-scatter.49.cloned.1.call-done = bf16[688,400]{0,1:T(8,128)(2,1)} async-done(((bf16[688,1600]{0,1:T(8,128)(2,1)}), bf16[688,400]{0,1:T(8,128)(2,1)}) %reduce-scatter.49.cloned.1.call-update) | async-done | bytes 550416 | tf_op jit(solution)/shard_map/reduce_scatter | solution.py:511
  1987.4 171.0 %reduce-scatter.67.cloned.1.call-done = bf16[200,6400]{1,0:T(8,128)(2,1)} async-done(((bf16[1600,6400]{1,0:T(8,128)(2,1)}), bf16[200,6400]{1,0:T(8,128)(2,1)}) %reduce-scatter.67.cloned.1.call-update) | async-done | bytes 2560016
  2178.1 48.7 %reduce-scatter.65.cloned.1.call-done = bf16[200,1600]{1,0:T(8,128)(2,1)} async-done(((bf16[1600,1600]{1,0:T(8,128)(2,1)}), bf16[200,1600]{1,0:T(8,128)(2,1)}) %reduce-scatter.65.cloned.1.call-update) | async-done | bytes 640016
  2230.5 181.6 %all-reduce.22.cloned.1.call-done = (bf16[1600,2,688]{2,1,0:T(2,128)(2,1)}, bf16[100,400]{0,1:T(8,128)(2,1)}) async-done(((bf16[1600,2,688]{2,1,0:T(2,128)(2,1)}, bf16[100,400]{0,1:T(8,128)(2,1)}), (bf16[1600,2,688]{2,1,0:T(2,128)(2,1)}, bf16[100,400]{0,1:T(8,128)(2,1)})) %all-reduce.22.cloned.1.call-update) | async-done | bytes 4483216
  2415.3 68.0 %reduce-scatter.43.cloned.1.call-done = bf16[200,2240]{1,0:T(8,128)(2,1)} async-done(((bf16[1600,2240]{1,0:T(8,128)(2,1)}), bf16[200,2240]{1,0:T(8,128)(2,1)}) %reduce-scatter.43.cloned.1.call-update) | async-done | bytes 896016 | tf_op jit(solution)/shard_map/reduce_scatter | solution.py:446
  2485.7 36.7 %reduce-scatter.59.cloned.1.call-done = bf16[400,400]{1,0:T(8,128)(2,1)} async-done(((bf16[1600,400]{1,0:T(8,128)(2,1)}), bf16[400,400]{1,0:T(8,128)(2,1)}) %reduce-scatter.59.cloned.1.call-update) | async-done | bytes 320016
  2525.4 49.8 %all-gather.42.cloned.1.call-done = bf16[688,1600]{0,1:T(8,128)(2,1)} async-done(((bf16[688,400]{0,1:T(8,128)(2,1)}), bf16[688,1600]{0,1:T(8,128)(2,1)}) %all-gather.42.cloned.1.call-update) | async-done | bytes 2201616 | tf_op jit(solution)/shard_map/all_gather | solution.py:534
  2580.0 32.2 %reduce-scatter.61.cloned.1.call-done = bf16[400,4]{1,0:T(8,128)(2,1)} async-done(((bf16[3200,4]{1,0:T(8,128)(2,1)}), bf16[400,4]{1,0:T(8,128)(2,1)}) %reduce-scatter.61.cloned.1.call-update) | async-done | bytes 3216
  2617.1 33.0 %reduce-scatter.63.cloned.1.call-done = bf16[400,16]{1,0:T(8,128)(2,1)} async-done(((bf16[3200,16]{1,0:T(8,128)(2,1)}), bf16[400,16]{1,0:T(8,128)(2,1)}) %reduce-scatter.63.cloned.1.call-update) | async-done | bytes 12816
  2657.6 57.1 %reduce-scatter.55.cloned.1.call-done = bf16[1600,200]{1,0:T(8,128)(2,1)} async-done(((bf16[6400,200]{1,0:T(8,128)(2,1)}), bf16[1600,200]{1,0:T(8,128)(2,1)}) %reduce-scatter.55.cloned.1.call-update) | async-done | bytes 640016
  2717.0 15.5 multiply_reduce_fusion.44
  2732.5 25.3 reduce-scatter.57.cloned.1.call-done
  2758.9 13.8 fusion.6
  2775.2 49.4 %reduce-scatter.37.cloned.1.call-done = bf16[256,1600]{0,1:T(8,128)(2,1)} async-done(((bf16[2048,1600]{0,1:T(8,128)(2,1)}), bf16[256,1600]{0,1:T(8,128)(2,1)}) %reduce-scatter.37.cloned.1.call-update) | async-done | bytes 819216 | tf_op jit(solution)/shard_map/reduce_scatter | solution.py:269
  2830.2 24.2 all-reduce.17
  2855.0 19.5 all-reduce.18
  2879.9 15.0 all-gather.4
  2896.3 29.7 all_gather.79
  2927.4 33.1 %all-gather.40.cloned.1.call-done = bf16[1600,2,688]{2,1,0:T(2,128)(2,1)} async-done(((bf16[400,2,688]{2,1,0:T(2,128)(2,1)}), bf16[1600,2,688]{2,1,0:T(2,128)(2,1)}) %all-gather.40.cloned.1.call-update) | async-done | bytes 4403216 | tf_op jit(solution)/shard_map/all_gather | solution.py:531
  2960.5 15.2 copy.163
  2975.8 14.2 reduce-scatter.51.cloned.1.call-done
  2991.1 31.4 %all-gather.2 = bf16[4,560,200]{1,2,0:T(8,128)(2,1)S(1)} all-gather(bf16[1,560,200]{1,2,0:T(8,128)(2,1)S(1)} %bitcast.1256), channel_id=1, replica_groups=mesh['dp'=4,'seq'=8] {'dp'}, dimensions={0}, use_global_device_ids=true | all-gather | bytes 1120000 | tf_op jit(solution)/shard_map/all_gather | solution.py:516
  3027.4 9.8 all-gather.38.cloned.1.call-done
  3040.8 53.7 %all-gather.46.cloned.1.call-done = bf16[4,1600,200]{1,2,0:T(8,128)(2,1)} async-done(((bf16[1,1600,200]{1,2,0:T(8,128)(2,1)}), bf16[4,1600,200]{1,2,0:T(8,128)(2,1)}) %all-gather.46.cloned.1.call-update) | async-done | bytes 2560016 | tf_op jit(solution)/shard_map/all_gather | solution.py:522
  (1968 shorter events, 1692.9 us)
Async XLA Ops:
  7.2 549.6 %copy-start = (bf16[688,1600]{1,0:T(8,128)(2,1)S(1)}, bf16[688,1600]{1,0:T(8,128)(2,1)}, u32[]{:S(2)}) copy-start(bf16[688,1600]{1,0:T(8,128)(2,1)} %param.54) | copy-start | bytes 6604804
  7.2 55.6 %copy-start.31 = (f32[1600]{0:T(1024)S(1)}, f32[1600]{0:T(1024)}, u32[]{:S(2)}) copy-start(f32[1600]{0:T(1024)} %param.55) | copy-start | bytes 19204
  7.2 55.6 %all-gather.20.cloned.1.call-start = ((), (), s32[]{:S(2)}) async-start(), calls=%async_computation.16 | async-start | bytes 8294400 | tf_op jit(solution)/shard_map/all_gather | solution.py:90
  8.0 165.7 %all-gather.26.cloned.1.call-start = ((), (), s32[]{:S(2)}) async-start(), calls=%async_computation.19 | async-start | bytes 23040000 | tf_op jit(solution)/shard_map/all_gather | solution.py:92
  8.7 336.1 %all-gather.22.cloned.1.call-start = ((), (), s32[]{:S(2)}) async-start(), calls=%async_computation.17 | async-start | bytes 2949120 | tf_op jit(solution)/shard_map/all_gather | solution.py:173
  9.5 164.2 %copy-start.65 = (f32[256]{0:T(256)}, f32[256]{0:T(256)S(1)}, u32[]{:S(2)}) copy-start(f32[256]{0:T(256)S(1)} %bitcast_rsqrt_fusion.2) | copy-start | bytes 3076
  9.5 62.2 %copy-start.52 = (bf16[400,132]{0,1:T(8,128)(2,1)S(1)}, bf16[400,132]{0,1:T(8,128)(2,1)}, u32[]{:S(2)}) copy-start(bf16[400,132]{0,1:T(8,128)(2,1)} %param.50) | copy-start | bytes 316804
  9.5 79.9 %copy-start.35 = (f32[16,3200]{1,0:T(8,128)S(1)}, f32[16,3200]{1,0:T(8,128)}, u32[]{:S(2)}) copy-start(f32[16,3200]{1,0:T(8,128)} %param.62) | copy-start | bytes 614404
  71.1 331.5 %all-gather.24.cloned.1.call-start = ((), (), s32[]{:S(2)}) async-start(), calls=%async_computation.18 | async-start | bytes 5990400 | tf_op jit(solution)/shard_map/all_gather | solution.py:91
  71.7 342.4 %all-gather.28.cloned.1.call-start = ((), (), s32[]{:S(2)}) async-start(), calls=%async_computation.20 | async-start | bytes 1843200 | tf_op jit(solution)/shard_map/all_gather | solution.py:30
  187.5 6.8 collective-permute-start
  201.3 17.4 copy-start.38
  227.2 186.8 %all-gather.44.cloned.1.call-start = ((), (), s32[]{:S(2)}) async-start(), calls=%async_computation.35 | async-start | bytes 1843200 | tf_op jit(solution)/shard_map/all_gather | solution.py:30
  340.4 98.4 %all-gather.30.cloned.1.call-start = ((), (), s32[]{:S(2)}) async-start(), calls=%async_computation.21 | async-start | bytes 11980800 | tf_op jit(solution)/shard_map/all_gather | solution.py:94
  341.1 165.4 %all-gather.32.cloned.1.call-start = ((), (), s32[]{:S(2)}) async-start(), calls=%async_computation.22 | async-start | bytes 7372800 | tf_op jit(solution)/shard_map/all_gather | solution.py:264
  398.0 52.6 %copy-start.54 = (s32[2]{0:T(128)}, s32[2]{0:T(128)S(1)}, u32[]{:S(2)}) copy-start(s32[2]{0:T(128)S(1)} %get-tuple-element.4497) | copy-start | bytes 28
  415.5 21.6 copy-start.59
  435.4 233.7 %copy-start.97 = (f32[256]{0:T(256)}, f32[256]{0:T(256)S(1)}, u32[]{:S(2)}) copy-start(f32[256]{0:T(256)S(1)} %bitcast_rsqrt_fusion) | copy-start | bytes 3076
  448.2 204.8 %copy-start.73 = (f32[256]{0:T(256)}, f32[256]{0:T(256)S(1)}, u32[]{:S(2)}) copy-start(f32[256]{0:T(256)S(1)} %fusion.154) | copy-start | bytes 3076
  450.5 106.2 %all-gather.34.cloned.1.call-start = ((), (), s32[]{:S(2)}) async-start(), calls=%async_computation.24 | async-start | bytes 7372800 | tf_op jit(solution)/shard_map/all_gather | solution.py:280
  450.7 202.4 %copy-start.99 = (f32[2,128]{1,0:T(2,128)}, f32[2,128]{1,0:T(2,128)S(1)}, u32[]{:S(2)}) copy-start(f32[2,128]{1,0:T(2,128)S(1)} %compare_convert_fusion) | copy-start | bytes 3076
  452.9 196.9 %reduce-scatter.39.cloned.1.call-start = ((), (), s32[]{:S(2)}) async-start(), calls=%async_computation.25 | async-start | bytes 7372800 | tf_op jit(solution)/shard_map/reduce_scatter | solution.py:289
  586.6 213.7 %all-gather.36.cloned.1.call-start = ((), (), s32[]{:S(2)}) async-start(), calls=%async_computation.27 | async-start | bytes 1843200 | tf_op jit(solution)/shard_map/all_gather | solution.py:50
  587.3 81.8 %copy-start.50 = (f32[3200]{0:T(1024)}, f32[3200]{0:T(1024)S(1)}, u32[]{:S(2)}) copy-start(f32[3200]{0:T(1024)S(1)} %broadcast_multiply_fusion.4) | copy-start | bytes 38404
  649.8 19.4 slice-start.2
  653.1 16.0 copy-start.105
  655.5 13.6 slice-start.3
  655.5 13.6 copy-start.13
  655.5 13.6 copy-start.61
  688.1 1213.2 %reduce-scatter.45.cloned.1.call-start = ((), (), s32[]{:S(2)}) async-start(), calls=%async_computation.29 | async-start | bytes 921600 | tf_op jit(solution)/shard_map/reduce_scatter | solution.py:461
  688.3 99.3 %copy-start.128 = (f32[256]{0:T(256)S(1)}, f32[256]{0:T(256)}, u32[]{:S(2)}) copy-start(f32[256]{0:T(256)} %copy-done.127) | copy-start | bytes 3076
  1720.4 184.7 %reduce-scatter.41.cloned.1.call-start = ((), (), s32[]{:S(2)}) async-start(), calls=%async_computation.26 | async-start | bytes 2949120 | tf_op jit(solution)/shard_map/reduce_scatter | solution.py:364
  1737.8 13.8 slice-start
  1775.3 14.0 slice-start
  1797.6 134.2 %reduce-scatter.47.cloned.1.call-start = ((), (), s32[]{:S(2)}) async-start(), calls=%async_computation.30 | async-start | bytes 11980800 | tf_op jit(solution)/shard_map/reduce_scatter | solution.py:458
  1807.0 176.5 %reduce-scatter.49.cloned.1.call-start = ((), (), s32[]{:S(2)}) async-start(), calls=%async_computation.33 | async-start | bytes 3072000 | tf_op jit(solution)/shard_map/reduce_scatter | solution.py:511
  1816.8 341.6 %reduce-scatter.67.cloned.1.call-start = ((), (), s32[]{:S(2)}) async-start(), calls=%async_computation.45 | async-start | bytes 23040000
  1835.5 6.4 collective-permute-start.1
  1856.2 370.6 %reduce-scatter.65.cloned.1.call-start = ((), (), s32[]{:S(2)}) async-start(), calls=%async_computation.44 | async-start | bytes 5990400
  1863.8 548.2 %all-reduce.22.cloned.1.call-start = ((), (), s32[]{:S(2)}) async-start(), calls=%async_computation.46 | async-start | bytes 10035200
  1901.4 582.0 %reduce-scatter.43.cloned.1.call-start = ((), (), s32[]{:S(2)}) async-start(), calls=%async_computation.28 | async-start | bytes 8294400 | tf_op jit(solution)/shard_map/reduce_scatter | solution.py:446
  1912.8 70.8 %copy-start.72 = (bf16[3200]{0:T(1024)(128)(2,1)S(1)}, bf16[3200]{0:T(1024)(128)(2,1)}, u32[]{:S(2)}) copy-start(bf16[3200]{0:T(1024)(128)(2,1)} %get-tuple-element.2151) | copy-start | bytes 19204
  1912.8 72.3 %copy-start.23 = (f32[16,3200]{1,0:T(8,128)S(1)}, f32[16,3200]{1,0:T(8,128)}, u32[]{:S(2)}) copy-start(f32[16,3200]{1,0:T(8,128)} %get-tuple-element.4354) | copy-start | bytes 614404
  1912.8 609.6 %reduce-scatter.59.cloned.1.call-start = ((), (), s32[]{:S(2)}) async-start(), calls=%async_computation.41 | async-start | bytes 2048000
  1935.2 640.0 %all-gather.42.cloned.1.call-start = ((), (), s32[]{:S(2)}) async-start(), calls=%async_computation.34 | async-start | bytes 3072000 | tf_op jit(solution)/shard_map/all_gather | solution.py:534
  1983.5 628.7 %reduce-scatter.61.cloned.1.call-start = ((), (), s32[]{:S(2)}) async-start(), calls=%async_computation.42 | async-start | bytes 921600
  1985.0 665.0 %reduce-scatter.63.cloned.1.call-start = ((), (), s32[]{:S(2)}) async-start(), calls=%async_computation.43 | async-start | bytes 921600
  1987.3 727.3 %reduce-scatter.55.cloned.1.call-start = ((), (), s32[]{:S(2)}) async-start(), calls=%async_computation.39 | async-start | bytes 4096000
  2163.0 594.8 %reduce-scatter.57.cloned.1.call-start = ((), (), s32[]{:S(2)}) async-start(), calls=%async_computation.40 | async-start | bytes 1843200
  2168.4 656.2 %reduce-scatter.37.cloned.1.call-start = ((), (), s32[]{:S(2)}) async-start(), calls=%async_computation.23 | async-start | bytes 7372800 | tf_op jit(solution)/shard_map/reduce_scatter | solution.py:269
  2178.1 51.1 %copy-start.133 = (u32[32]{0:T(128)S(1)}, u32[32]{0:T(128)}, u32[]{:S(2)}) copy-start(u32[32]{0:T(128)} %constant.472) | copy-start | bytes 388
  2178.1 718.3 %reduce-scatter.53.cloned.1.call-start = ((), (), s32[]{:S(2)}) async-start(), calls=%async_computation.38 | async-start | bytes 1024000
  2229.1 731.4 %all-gather.40.cloned.1.call-start = ((), (), s32[]{:S(2)}) async-start(), calls=%async_computation.32 | async-start | bytes 6144000 | tf_op jit(solution)/shard_map/all_gather | solution.py:531
  2412.0 110.8 %copy-start.149 = (u32[32]{0:T(128)S(1)}, u32[32]{0:T(128)}, u32[]{:S(2)}) copy-start(u32[32]{0:T(128)} %constant.464) | copy-start | bytes 388
  2415.3 574.7 %reduce-scatter.51.cloned.1.call-start = ((), (), s32[]{:S(2)}) async-start(), calls=%async_computation.37 | async-start | bytes 1433600
  2485.7 551.5 %all-gather.38.cloned.1.call-start = ((), (), s32[]{:S(2)}) async-start(), calls=%async_computation.31 | async-start | bytes 2048000 | tf_op jit(solution)/shard_map/all_gather | solution.py:528
  2522.4 572.0 %all-gather.46.cloned.1.call-start = ((), (), s32[]{:S(2)}) async-start(), calls=%async_computation.36 | async-start | bytes 3328000 | tf_op jit(solution)/shard_map/all_gather | solution.py:522
  2613.2 37.8 %copy-start.30 = (bf16[256,640]{0,1:T(8,128)(2,1)S(1)}, bf16[256,640]{0,1:T(8,128)(2,1)}, u32[]{:S(2)}) copy-start(bf16[256,640]{0,1:T(8,128)(2,1)} %copy-done.29) | copy-start | bytes 983044
  2717.0 107.6 %copy-start.57 = (f32[1600]{0:T(1024)S(1)}, f32[1600]{0:T(1024)}, u32[]{:S(2)}) copy-start(f32[1600]{0:T(1024)} %param.58) | copy-start | bytes 19204
  2717.0 107.6 %copy-start.74 = (f32[256]{0:T(256)S(1)}, f32[256]{0:T(256)}, u32[]{:S(2)}) copy-start(f32[256]{0:T(256)} %copy-done.73) | copy-start | bytes 3076
  2717.0 107.6 %copy-start.100 = (f32[2,128]{1,0:T(2,128)S(1)}, f32[2,128]{1,0:T(2,128)}, u32[]{:S(2)}) copy-start(f32[2,128]{1,0:T(2,128)} %copy-done.99) | copy-start | bytes 3076
  2717.0 107.6 %copy-start.106 = (f32[256]{0:T(256)S(1)}, f32[256]{0:T(256)}, u32[]{:S(2)}) copy-start(f32[256]{0:T(256)} %copy-done.105) | copy-start | bytes 3076
  2772.7 107.0 %collective-permute-start.2 = (bf16[400,21]{0,1:T(8,128)(2,1)S(1)}, bf16[400,21]{0,1:T(8,128)(2,1)S(1)}, u32[]{:S(2)}, u32[]{:S(2)}) collective-permute-start(bf16[400,21]{0,1:T(8,128)(2,1)S(1)} %slice.946), channel_id=1, source_target_pairs={{0,8},{8,16},{16,24},{1,9},{9,17},{17,25},{2,10},{10,18},{18,26},{... | collective-permute-start | bytes 50408
  2828.0 67.7 %copy-start.58 = (bf16[100,400]{0,1:T(8,128)(2,1)S(1)}, bf16[100,400]{0,1:T(8,128)(2,1)}, u32[]{:S(2)}) copy-start(bf16[100,400]{0,1:T(8,128)(2,1)} %get-tuple-element.2435) | copy-start | bytes 240004
  (135 other events, 770.7 us)
Sparse Core Ops, SparseCore 0:
  10.0 52.7 all-gather.19
  64.7 108.9 all-gather.25
  176.1 30.5 all-gather.21
  208.4 41.4 all-gather.23
  252.2 25.9 all-gather.27
  340.5 26.1 all-gather.43
  368.5 63.9 all-gather.29
  450.7 55.7 all-gather.31
  508.9 47.8 all-gather.33
  586.7 63.0 reduce-scatter.38
  688.2 25.9 all-gather.35
  1720.5 34.4 reduce-scatter.44
  1797.7 43.5 reduce-scatter.40
  1844.7 87.0 reduce-scatter.46
  1933.9 49.5 reduce-scatter.48
  1986.9 171.4 reduce-scatter.66
  2162.0 64.7 reduce-scatter.64
  2229.7 182.2 all-reduce.21
  2416.5 66.7 reduce-scatter.42
  2486.1 36.2 reduce-scatter.58
  2524.0 51.1 all-gather.41
  2578.9 33.2 reduce-scatter.60
  2615.6 34.4 reduce-scatter.62
  2652.3 62.2 reduce-scatter.54
  2718.9 38.8 reduce-scatter.56
  2761.5 62.9 reduce-scatter.36
  2827.3 23.6 reduce-scatter.52
  2852.5 107.9 all-gather.39
  2962.8 27.0 reduce-scatter.50
  2991.3 45.7 all-gather.37
  3038.7 55.6 all-gather.45
where the time goes:
time: 3150 us; the launch traced here: 3110 us
  waiting for transfers between devices  1220 us (39%)
  other arithmetic  876 us (28%)
  local copies, waits for them, and re-layouts  551 us (17%)
  matrix products  280 us (9%)
  blocking collectives  151 us (5%)
    unnamed x42, waiting for transfers between devices  603 us
    dynamic_update_slice x192, other arithmetic, run_block(): return lax.scan(advance, carried, block_series, unroll=4)  207 us
    mul x160, other arithmetic, advance(): step_now * input_now  138 us
    reduce_sum x64, other arithmetic, advance(): return (carried, jnp.sum(c_now[:, :, None] * carried, axis=1))  121 us
    mul x32, other arithmetic, advance(): jnp.exp(step_now[:, None, :] * decay_rate[None]) * carried  99.4 us
    all_gather x1, waiting for transfers between devices, gather_weights(): lax.all_gather(w_in, 'seq', axis=0, tiled=True)  83.5 us
    unnamed x362, local copies, waits for them, and re-layouts  73.4 us
    dynamic_update_slice x48, local copies, waits for them, and re-layouts, local_scan(): final_state, results = lax.scan(run_block, initial, series)  70.1 us
  transfers between devices with their start and end apart: 34, of which 22 were waited for; matrix products, arithmetic and copies ran while one was open for 22% of the time, Pallas kernels for 0%

commit v1 on v0

v1 whole, which is shorter than its diff:
```python
import functools
import math

import jax
import jax.numpy as jnp
from jax import lax
from jax.experimental import pallas as pl
from jax.experimental.pallas import tpu as pltpu
from jax.sharding import PartitionSpec as P

HEADS = 25
HEAD = 64
KVH = 5
INNER = 3200
NST = 16
KCONV = 4
DTR = 100
EPSILON = 1e-05
NEGATIVE = -1e30
CHUNK = 16
LOG2E = math.log2(math.e)
LN2 = math.log(2.0)

BF = jnp.bfloat16
F32 = jnp.float32
NT = (((1,), (1,)), ((), ()))
TN = (((0,), (0,)), ((), ()))
GIANT = 60 * 1024 * 1024
MESH = pl.DeviceIdType.MESH


def ntdot(a, b):
    return lax.dot_general(a, b, NT, preferred_element_type=F32)


def tndot(a, b):
    return lax.dot_general(a, b, TN, preferred_element_type=F32)


def dot(a, b):
    return jnp.dot(a, b, preferred_element_type=F32)


def silu_grad(values):
    logistic = jax.nn.sigmoid(values)
    return logistic * (1.0 + values * (1.0 - logistic))


def chunk_masks():
    spread = NST * CHUNK
    row = lax.broadcasted_iota(jnp.int32, (CHUNK, spread), 0)
    col = lax.broadcasted_iota(jnp.int32, (CHUNK, spread), 1)
    own = (col // NST == row).astype(F32)
    tile = (col % NST == row).astype(BF)
    return own, tile


def scan_fwd_kernel(pre_ref, mix_ref, bt_ref, c_ref, rate_ref, skip_ref, core_ref, start_ref,
                    h_ref, dt_ref, u_ref, wide_ref, hs_ref):
    length, cols = pre_ref.shape[2:]
    own, tile = chunk_masks()

    @pl.when(pl.program_id(1) == 0)
    def _():
        for ref in (h_ref, dt_ref, u_ref, wide_ref):
            ref[...] = jnp.zeros_like(ref)
        wide_ref[:, :cols] = rate_ref[...] * LOG2E

    start_ref[0, 0] = h_ref[:, :cols]
    dt = jax.nn.softplus(pre_ref[0, 0])
    dt_ref[:, :cols] = dt
    u_ref[:, :cols] = dt * mix_ref[0, 0]
    rate = wide_ref[...]
    spread = NST * CHUNK

    def chunk(k, h):
        base = pl.multiple_of(k * CHUNK, CHUNK)
        bt = bt_ref[0, 0, k]
        for t in range(CHUNK):
            a = jnp.exp2(dt_ref[pl.ds(base + t, 1), :] * rate)
            h = a * h + bt[:, t : t + 1] * u_ref[pl.ds(base + t, 1), :]
            hs_ref[pl.ds(pl.multiple_of((base + t) * NST, NST), NST), :] = h.astype(BF)
        return h

    h_ref[...] = lax.fori_loop(0, length // CHUNK, chunk, h_ref[...])
    crep = dot(c_ref[0, 0].astype(BF), tile)
    for k in range(length // CHUNK):
        at = slice(k * CHUNK, (k + 1) * CHUNK)
        cb = (crep[at] * own).astype(BF)
        core_ref[0, 0, at, :] = dot(cb, hs_ref[k * spread : (k + 1) * spread])[:, :cols] + skip_ref[...] * mix_ref[0, 0, at, :]

def scan_forward(pre, mix, bt, c, rate, skip):
    n, seqs, length, cols = pre.shape
    wide = -(-cols // 128) * 128
    big = lambda w: pl.BlockSpec((1, 1, length, w), lambda s, i: (i, s, 0, 0))
    whole = lambda r: pl.BlockSpec((r, cols), lambda s, i: (0, 0))
    return pl.pallas_call(
        scan_fwd_kernel,
        grid=(seqs, n),
        in_specs=[
            big(cols), big(cols),
            pl.BlockSpec((1, 1) + bt.shape[2:], lambda s, i: (i, s, 0, 0, 0)),
            big(NST), whole(NST), whole(1),
        ],
        out_specs=[big(cols), pl.BlockSpec((1, 1, NST, cols), lambda s, i: (i, s, 0, 0))],
        out_shape=[
            jax.ShapeDtypeStruct(pre.shape, F32),
            jax.ShapeDtypeStruct((n, seqs, NST, cols), F32),
        ],
        scratch_shapes=[
            pltpu.VMEM((NST, wide), F32),
            pltpu.VMEM((length, wide), F32),
            pltpu.VMEM((length, wide), F32),
            pltpu.VMEM((NST, wide), F32),
            pltpu.VMEM((NST * length, wide), BF),
        ],
        compiler_params=pltpu.CompilerParams(vmem_limit_bytes=GIANT),
    )(pre, mix, bt, c, rate, skip)

def scan_bwd_kernel(pre_ref, mix_ref, gin_ref, start_ref, bt_ref, ct_ref, b_ref, rate_ref, skip_ref,
                    gpre_ref, gmix_ref, gb_ref, gc_ref, grate_ref, gskip_ref,
                    carry_ref, dt_ref, u_ref, gy_ref, wide_ref, hs_ref, gs_ref, q_ref):
    length, cols = pre_ref.shape[2:]
    own, tile = chunk_masks()
    spread = NST * CHUNK
    half = NST // 2
    folded = (lax.broadcasted_iota(jnp.int32, (2 * CHUNK, spread), 1) // half
              == lax.broadcasted_iota(jnp.int32, (2 * CHUNK, spread), 0)).astype(BF)

    @pl.when(pl.program_id(1) == 0)
    def _():
        carry_ref[...] = jnp.zeros_like(carry_ref)

    @pl.when((pl.program_id(1) == 0) & (pl.program_id(0) == 0))
    def _():
        grate_ref[...] = jnp.zeros_like(grate_ref)
        gskip_ref[...] = jnp.zeros_like(gskip_ref)
        for ref in (dt_ref, u_ref, gy_ref, wide_ref):
            ref[...] = jnp.zeros_like(ref)
        wide_ref[0:NST, :cols] = rate_ref[...] * LOG2E

    dt = jax.nn.softplus(pre_ref[0, 0])
    dt_ref[:, :cols] = dt
    u_ref[:, :cols] = dt * mix_ref[0, 0]
    gy_ref[:, :cols] = gin_ref[0, 0]
    wide_ref[NST:, :cols] = start_ref[0, 0]
    gskip_ref[...] += jnp.sum(gin_ref[0, 0] * mix_ref[0, 0], axis=0, keepdims=True)
    rate = wide_ref[0:NST]
    hs_ref[0:NST] = wide_ref[NST:].astype(BF)

    def ahead(k, h):
        base = pl.multiple_of(k * CHUNK, CHUNK)
        bt = bt_ref[0, 0, k]
        for t in range(CHUNK):
            a = jnp.exp2(dt_ref[pl.ds(base + t, 1), :] * rate)
            h = a * h + bt[:, t : t + 1] * u_ref[pl.ds(base + t, 1), :]
            hs_ref[pl.ds(pl.multiple_of((base + t + 1) * NST, NST), NST), :] = h.astype(BF)
        return h

    lax.fori_loop(0, length // CHUNK, ahead, wide_ref[NST:])

    def back(r, state):
        carry, grate = state
        k = length // CHUNK - 1 - r
        base = pl.multiple_of(k * CHUNK, CHUNK)
        ct = ct_ref[0, 0, k]
        qr_late = None
        for t in reversed(range(CHUNK)):
            at = pl.ds(pl.multiple_of((base + t) * NST, NST), NST)
            dt_row = dt_ref[pl.ds(base + t, 1), :]
            a = jnp.exp2(dt_row * rate)
            g = ct[:, t : t + 1] * gy_ref[pl.ds(base + t, 1), :] + carry
            carry = a * g
            q = carry * hs_ref[at, :].astype(F32)
            grate = grate + q * dt_row
            gs_ref[at, :] = g.astype(BF)
            qr = q * rate
            qr = qr[:half] + qr[half:]
            if t % 2:
                qr_late = qr
            else:
                both = jnp.concatenate([qr, qr_late], axis=0).astype(BF)
                q_ref[pl.ds(pl.multiple_of((base + t) * half, NST), NST), :] = both
        return carry, grate

    carry, grate = lax.fori_loop(
        0, length // CHUNK, back, (carry_ref[...], jnp.zeros(carry_ref.shape, F32))
    )
    carry_ref[...] = carry
    grate_ref[...] += grate[:, :cols]
    brep = dot(b_ref[0, 0].astype(BF), tile)
    gy_low = gy_ref[...].astype(BF)
    u_low = u_ref[...].astype(BF)
    gcs, gbs = [], []
    for pair in range(length // CHUNK // 2):
        gdts = dot(folded, q_ref[pair * spread : (pair + 1) * spread]) * LN2
        for k in (2 * pair, 2 * pair + 1):
            rows = slice(k * CHUNK, (k + 1) * CHUNK)
            deep = slice(k * spread, (k + 1) * spread)
            mix, dt_now, gy = mix_ref[0, 0, rows, :], dt_ref[rows, :cols], gin_ref[0, 0, rows, :]
            gs = gs_ref[deep]
            gu = dot((brep[rows] * own).astype(BF), gs)[:, :cols]
            gdt = gdts[(k % 2) * CHUNK : (k % 2 + 1) * CHUNK, :cols] + gu * mix
            gpre_ref[0, 0, rows, :] = gdt * jax.nn.sigmoid(pre_ref[0, 0, rows, :])
            gmix_ref[0, 0, rows, :] = gu * dt_now + skip_ref[...] * gy
            hs = hs_ref[k * spread + NST : (k + 1) * spread + NST]
            gcs.append((ntdot(gy_low[rows], hs) * own).astype(BF))
            gbs.append((ntdot(u_low[rows], gs) * own).astype(BF))
    gc_ref[0, 0] = ntdot(jnp.concatenate(gcs, axis=0), tile)
    gb_ref[0, 0] = ntdot(jnp.concatenate(gbs, axis=0), tile)

def scan_backward(pre, mix, gy, start, bt, ct, b, rate, skip):
    n, seqs, length, cols = pre.shape
    wide = -(-cols // 128) * 128
    at = lambda s, i: (n - 1 - i, s, 0, 0)
    big = lambda w: pl.BlockSpec((1, 1, length, w), at)
    whole = lambda r: pl.BlockSpec((r, cols), lambda s, i: (0, 0))
    turned = pl.BlockSpec((1, 1) + bt.shape[2:], lambda s, i: (n - 1 - i, s, 0, 0, 0))
    shape = lambda w: jax.ShapeDtypeStruct((n, seqs, length, w), F32)
    return pl.pallas_call(
        scan_bwd_kernel,
        grid=(seqs, n),
        in_specs=[
            big(cols), big(cols), big(cols), pl.BlockSpec((1, 1, NST, cols), at),
            turned, turned, big(NST), whole(NST), whole(1),
        ],
        out_specs=[big(cols), big(cols), big(NST), big(NST), whole(NST), whole(1)],
        out_shape=[
            shape(cols), shape(cols), shape(NST), shape(NST),
            jax.ShapeDtypeStruct((NST, cols), F32),
            jax.ShapeDtypeStruct((1, cols), F32),
        ],
        scratch_shapes=[
            pltpu.VMEM((NST, wide), F32),
            pltpu.VMEM((length, wide), F32),
            pltpu.VMEM((length, wide), F32),
            pltpu.VMEM((length, wide), F32),
            pltpu.VMEM((2 * NST, wide), F32),
            pltpu.VMEM((length * NST + NST, wide), BF),
            pltpu.VMEM((length * NST, wide), BF),
            pltpu.VMEM((length * NST // 2, wide), BF),
        ],
        compiler_params=pltpu.CompilerParams(vmem_limit_bytes=GIANT),
    )(pre, mix, gy, start, bt, ct, b, rate, skip)


def pick(ref, blocks, slots, slot):
    value = ref[0:blocks, 0, :, 0:HEAD].reshape(-1, HEAD)
    for other in range(1, slots):
        here = ref[0:blocks, 0, :, other * HEAD : (other + 1) * HEAD].reshape(-1, HEAD)
        value = jnp.where(slot == other, here, value)
    return value


def masked_scores(queries, keys, first, length):
    scores = ntdot(queries, keys)
    rows = first + lax.broadcasted_iota(jnp.int32, (scores.shape[0], 1), 0)
    bound = jnp.minimum(rows, length - 1)
    return jnp.where(lax.broadcasted_iota(jnp.int32, scores.shape, 1) <= bound, scores, NEGATIVE)


def attn_fwd_kernel(slot_ref, len_ref, q_ref, k_ref, v_ref, out_ref, lse_ref):
    n, _, length, width = q_ref.shape
    heads, slots = width // HEAD, k_ref.shape[3] // HEAD
    group = 2
    seq_length = len_ref[pl.program_id(0)]
    for i in range(n // group):
        at = slice(i * group, (i + 1) * group)
        for j in range(heads):
            lanes = slice(j * HEAD, (j + 1) * HEAD)
            blocks = (i + 1) * group
            queries = q_ref[at, 0, :, lanes].reshape(group * length, HEAD) * HEAD ** (-0.5)
            keys = pick(k_ref, blocks, slots, slot_ref[j])
            values = pick(v_ref, blocks, slots, slot_ref[j])
            scores = masked_scores(queries.astype(BF), keys, i * group * length, seq_length)
            top = jnp.max(scores, axis=1, keepdims=True)
            probs = jnp.exp(scores - top)
            total = jnp.sum(probs, axis=1, keepdims=True)
            mixed = dot(probs.astype(BF), values) * (slot_ref[heads + j].astype(F32) / total)
            out_ref[at, 0, :, lanes] = mixed.reshape(group, length, HEAD)
            lse_ref[at, 0, :, j : j + 1] = (top + jnp.log(total)).reshape(group, length, 1)


def attn_forward(slot, lengths, q, k, v):
    n, seqs, length, width = q.shape
    big = lambda w: pl.BlockSpec((n, 1, length, w), lambda s: (0, s, 0, 0))
    smem = pl.BlockSpec(memory_space=pltpu.SMEM)
    return pl.pallas_call(
        attn_fwd_kernel,
        grid=(seqs,),
        in_specs=[smem, smem, big(width), big(k.shape[3]), big(k.shape[3])],
        out_specs=[big(width), big(width // HEAD)],
        out_shape=[
            jax.ShapeDtypeStruct(q.shape, F32),
            jax.ShapeDtypeStruct((n, seqs, length, width // HEAD), F32),
        ],
        compiler_params=pltpu.CompilerParams(vmem_limit_bytes=GIANT),
    )(slot, lengths, q, k, v)


def attn_bwd_kernel(slot_ref, len_ref, q_ref, k_ref, v_ref, gh_ref, att_ref, lse_ref,
                    gq_ref, gk_ref, gv_ref, gk_acc, gv_acc):
    n, _, length, width = q_ref.shape
    heads, slots = width // HEAD, k_ref.shape[3] // HEAD
    group = 2
    seq_length = len_ref[pl.program_id(0)]
    gk_acc[...] = jnp.zeros_like(gk_acc)
    gv_acc[...] = jnp.zeros_like(gv_acc)
    for i in range(n // group):
        at = slice(i * group, (i + 1) * group)
        blocks = (i + 1) * group
        for j in range(heads):
            lanes = slice(j * HEAD, (j + 1) * HEAD)
            slot = slot_ref[j]
            queries = q_ref[at, 0, :, lanes].reshape(group * length, HEAD) * HEAD ** (-0.5)
            queries = queries.astype(BF)
            keys = pick(k_ref, blocks, slots, slot)
            values = pick(v_ref, blocks, slots, slot)
            grad = gh_ref[at, 0, :, lanes].reshape(group * length, HEAD)
            attended = att_ref[at, 0, :, lanes].reshape(group * length, HEAD)
            delta = jnp.sum(grad.astype(F32) * attended, axis=1, keepdims=True)
            lse = lse_ref[at, 0, :, j : j + 1].reshape(group * length, 1)
            scores = masked_scores(queries, keys, i * group * length, seq_length)
            probs = jnp.exp(scores - lse)
            grad_scores = (probs * (ntdot(grad, values) - delta)).astype(BF)
            gq = dot(grad_scores, keys) * HEAD ** (-0.5)
            gq_ref[at, 0, :, lanes] = gq.astype(BF).reshape(group, length, HEAD)
            rows = slice(0, blocks * length)
            gk_acc[slot, rows] += tndot(grad_scores, queries)
            gv_acc[slot, rows] += tndot(probs.astype(BF), grad)
    for other in range(slots):
        lanes = slice(other * HEAD, (other + 1) * HEAD)
        gk_ref[:, 0, :, lanes] = gk_acc[other].astype(BF).reshape(n, length, HEAD)
        gv_ref[:, 0, :, lanes] = gv_acc[other].astype(BF).reshape(n, length, HEAD)


def attn_backward(slot, lengths, q, k, v, gh, att, lse):
    n, seqs, length, width = q.shape
    big = lambda w: pl.BlockSpec((n, 1, length, w), lambda s: (0, s, 0, 0))
    smem = pl.BlockSpec(memory_space=pltpu.SMEM)
    kw = k.shape[3]
    return pl.pallas_call(
        attn_bwd_kernel,
        grid=(seqs,),
        in_specs=[smem, smem, big(width), big(kw), big(kw), big(width), big(width), big(width // HEAD)],
        out_specs=[big(width), big(kw), big(kw)],
        out_shape=[jax.ShapeDtypeStruct(x.shape, BF) for x in (q, k, v)],
        scratch_shapes=[pltpu.VMEM((kw // HEAD, n * length, HEAD), F32)] * 2,
        compiler_params=pltpu.CompilerParams(vmem_limit_bytes=GIANT),
    )(slot, lengths, q, k, v, gh, att, lse)


def greet(peers, axis="seq"):
    barrier = pltpu.get_barrier_semaphore()
    for peer in peers:
        pl.semaphore_signal(barrier, inc=1, device_id={axis: peer}, device_id_type=MESH)
    pl.semaphore_wait(barrier, len(peers))

def send(src, dst, send_sem, recv_sem, peer, axis="seq"):
    return pltpu.make_async_remote_copy(src_ref=src, dst_ref=dst, send_sem=send_sem, recv_sem=recv_sem,
        device_id={axis: peer}, device_id_type=MESH)

def ag_parts(n, x_ref, o_ref, local_sem, far_send, far_recv, near_send, near_recv):
    me = lax.axis_index("seq")
    core, chip, chips = me % 2, me // 2, n // 2
    sib = me + 1 - 2 * core
    far = [((chip + d) % chips) * 2 + core for d in range(1, chips)]
    mine = pltpu.make_async_copy(x_ref, o_ref.at[me], local_sem)
    out = [
        send(x_ref, o_ref.at[me], far_send.at[d], far_recv.at[d], far[d - 1]) for d in range(1, chips)
    ]
    near = [send(x_ref, o_ref.at[me], near_send.at[0], near_recv.at[0], sib)]

    def begin():
        for c in [mine] + out + near:
            c.start()

    def finish():
        for d in range(1, chips):
            out[d - 1].wait_recv()
            block = ((chip + chips - d) % chips) * 2 + core
            c = send(o_ref.at[block], o_ref.at[block], near_send.at[d], near_recv.at[d], sib)
            c.start()
            near.append(c)
        mine.wait()
        for c in near:
            c.wait()
        for c in out:
            c.wait_send()

    return begin, finish


def ag_kernel(n, x_ref, o_ref, *sems):
    me = lax.axis_index("seq")
    core, chip, chips = me % 2, me // 2, n // 2
    greet([me + 1 - 2 * core] + [((chip + d) % chips) * 2 + core for d in range(1, chips)])
    begin, finish = ag_parts(n, x_ref, o_ref, *sems)
    begin()
    finish()


def all_gather_any(x, n, cid):
    chips = n // 2
    return pl.pallas_call(functools.partial(ag_kernel, n),
        out_shape=jax.ShapeDtypeStruct((n,) + x.shape, x.dtype),
        in_specs=[pl.BlockSpec(memory_space=pl.ANY)],
        out_specs=pl.BlockSpec(memory_space=pl.ANY),
        scratch_shapes=[pltpu.SemaphoreType.DMA] + [pltpu.SemaphoreType.DMA((chips,))] * 4,
        compiler_params=pltpu.CompilerParams(collective_id=cid, has_side_effects=True),
    )(x)

def rs_kernel(n, p_ref, after_ref, o_ref, own, near, sums, got, local_sem, near_send, near_recv, far_send, far_recv):
    me = lax.axis_index("seq")
    core, chip, chips = me % 2, me // 2, n // 2
    sib = me + 1 - 2 * core
    step = lambda d: (chip + d) % chips
    far = [step(d) * 2 + core for d in range(1, chips)]
    greet([sib] + far)
    order = list(range(1, chips)) + [0]
    loads, nears, fars = {}, {}, {}
    for d in order:
        nears[d] = send(p_ref.at[step(d) * 2 + 1 - core], near.at[d], near_send.at[d], near_recv.at[d], sib)
        nears[d].start()
        loads[d] = pltpu.make_async_copy(p_ref.at[step(d) * 2 + core], own.at[d], local_sem.at[d])
        loads[d].start()
    rows = own.shape[1]
    slab = 16
    def each(body):
        def run(i, _):
            body(pl.ds(pl.multiple_of(i * slab, slab), slab))
            return 0
        lax.fori_loop(0, rows // slab, run, 0, unroll=2)
    for d in order:
        loads[d].wait()
        nears[d].wait_recv()
        if d:
            def add(at):
                sums[d - 1, at] = (own[d, at].astype(F32) + near[d, at].astype(F32)).astype(BF)
            each(add)
            fars[d] = send(sums.at[d - 1], got.at[d - 1], far_send.at[d - 1], far_recv.at[d - 1], far[d - 1])
            fars[d].start()
        else:
            def add(at):
                o_ref[at] = own[0, at].astype(F32) + near[0, at].astype(F32)
            each(add)
    for d in range(1, chips):
        fars[d].wait_recv()
        def add(at):
            o_ref[at] = o_ref[at] + got[d - 1, at].astype(F32)
        each(add)
    for d in order:
        nears[d].wait_send()
        if d: fars[d].wait_send()

def reduce_scatter_any(p, after, n, cid):
    chips = n // 2
    blk = p.shape[1:]
    return pl.pallas_call(functools.partial(rs_kernel, n),
        out_shape=jax.ShapeDtypeStruct(blk, F32),
        in_specs=[pl.BlockSpec(memory_space=pl.ANY)] * 2,
        out_specs=pl.BlockSpec(memory_space=pltpu.VMEM),
        scratch_shapes=[pltpu.VMEM((chips,) + blk, p.dtype), pltpu.VMEM((chips,) + blk, p.dtype),
            pltpu.VMEM((chips-1,) + blk, p.dtype), pltpu.VMEM((chips-1,) + blk, p.dtype),
            pltpu.SemaphoreType.DMA((chips,)), pltpu.SemaphoreType.DMA((chips,)), pltpu.SemaphoreType.DMA((chips,)),
            pltpu.SemaphoreType.DMA((chips-1,)), pltpu.SemaphoreType.DMA((chips-1,))],
        compiler_params=pltpu.CompilerParams(collective_id=cid, has_side_effects=True, vmem_limit_bytes=GIANT),
    )(p, after)

def stat_kernel(n, axis, x_ref, o_ref, got, send_sem, recv_sem):
    me = lax.axis_index(axis)
    peers = [(me + d) % n for d in range(1, n)]
    greet(peers, axis)
    copies = []
    for d in range(1, n):
        c = send(x_ref, got.at[d - 1], send_sem.at[d - 1], recv_sem.at[d - 1], peers[d - 1], axis)
        c.start()
        copies.append(c)
    total = x_ref[...]
    for d in range(1, n):
        copies[d - 1].wait_recv()
        total = total + got[d - 1]
    o_ref[...] = total
    for c in copies:
        c.wait_send()


def small_sum(x, n, cid, axis="seq"):
    return pl.pallas_call(
        functools.partial(stat_kernel, n, axis),
        out_shape=jax.ShapeDtypeStruct(x.shape, F32),
        in_specs=[pl.BlockSpec(memory_space=pltpu.VMEM)],
        out_specs=pl.BlockSpec(memory_space=pltpu.VMEM),
        scratch_shapes=[pltpu.VMEM((n - 1,) + x.shape, F32)] + [pltpu.SemaphoreType.DMA((n - 1,))] * 2,
        compiler_params=pltpu.CompilerParams(collective_id=cid, has_side_effects=True, vmem_limit_bytes=GIANT),
    )(x)


def square(me):
    core, x, y = me % 2, (me // 2) % 2, me // 4
    seat = lambda yy, xx, cc: (yy * 2 + xx) * 2 + cc
    return core, (seat(y, x, 1 - core), seat(y, 1 - x, core), seat(1 - y, x, core), seat(1 - y, 1 - x, core))

def ag4_parts(n, x_ref, o_ref, local_sem, far_send, far_recv, near_send, near_recv):
    me = lax.axis_index("seq")
    core, (sib, east, north, across) = square(me)
    half = x_ref.shape[0] // 2
    cut = (pl.ds(0, half), pl.ds(half, half))
    mine = pltpu.make_async_copy(x_ref, o_ref.at[me], local_sem)
    far, near = {}, []
    for slot, h, peer in ((0, 0, east), (2, 1, north), (1, 1, east), (3, 0, north)):
        far[slot] = send(x_ref.at[cut[h]], o_ref.at[me, cut[h]], far_send.at[slot], far_recv.at[slot], peer)
    near.append(send(x_ref, o_ref.at[me], near_send.at[6], near_recv.at[6], sib))

    def begin():
        mine.start()
        for slot in (0, 2, 1, 3):
            far[slot].start()
        near[0].start()

    def pass_on(slot, block, h):
        ref = o_ref.at[block, cut[h]]
        c = send(ref, ref, near_send.at[slot], near_recv.at[slot], sib)
        c.start()
        near.append(c)

    def finish():
        for slot, block, h, relay, to in (
            (0, east, 0, 4, north), (2, north, 1, 5, east), (1, east, 1, None, None), (3, north, 0, None, None)
        ):
            far[slot].wait_recv()
            if relay is not None:
                ref = o_ref.at[block, cut[h]]
                far[relay] = send(ref, ref, far_send.at[relay], far_recv.at[relay], to)
                far[relay].start()
            pass_on(slot, block, h)
        for slot, h in ((4, 0), (5, 1)):
            far[slot].wait_recv()
            pass_on(slot, across, h)
        mine.wait()
        for c in near:
            c.wait()
        for c in far.values():
            c.wait_send()

    return begin, finish


def ag4_kernel(x_ref, o_ref, *sems):
    core, (sib, east, north, across) = square(lax.axis_index("seq"))
    greet([sib, east, north])
    begin, finish = ag4_parts(8, x_ref, o_ref, *sems)
    begin()
    finish()


def all_gather4(x, n, cid):
    return pl.pallas_call(ag4_kernel,
        out_shape=jax.ShapeDtypeStruct((n,) + x.shape, x.dtype),
        in_specs=[pl.BlockSpec(memory_space=pl.ANY)],
        out_specs=pl.BlockSpec(memory_space=pl.ANY),
        scratch_shapes=[pltpu.SemaphoreType.DMA] + [pltpu.SemaphoreType.DMA((6,))] * 2 + [pltpu.SemaphoreType.DMA((7,))] * 2,
        compiler_params=pltpu.CompilerParams(collective_id=cid, has_side_effects=True),
    )(x)

def rs4_kernel(p_ref, after_ref, o_ref, own, near, got, local_sem, near_send, near_recv, far_send, far_recv):
    me = lax.axis_index("seq")
    core, (sib, east, north, across) = square(me)
    greet([sib, east, north])
    rows = own.shape[1]
    half = rows // 2
    cut = (pl.ds(0, half), pl.ds(half, half))
    seats = (across, east, north, me)
    loads, nears, far = [], [], {}
    for i, seat in enumerate(seats):
        other = seat + 1 - 2 * core
        c = send(p_ref.at[other], near.at[i], near_send.at[i], near_recv.at[i], sib)
        c.start(); nears.append(c)
        c = pltpu.make_async_copy(p_ref.at[seat], own.at[i], local_sem.at[i])
        c.start(); loads.append(c)
    slab = 16
    def each(first, count, body):
        def run(i, _):
            body(pl.ds(pl.multiple_of(first + i * slab, slab), slab), pl.ds(pl.multiple_of(i * slab, slab), slab))
            return 0
        lax.fori_loop(0, count // slab, run, 0, unroll=2)
    def fold(i):
        loads[i].wait(); nears[i].wait_recv()
        def add(at, _):
            own[i, at] = (own[i, at].astype(F32) + near[i, at].astype(F32)).astype(own.dtype)
        each(0, rows, add)
    def go(slot, i, h, peer):
        far[slot] = send(own.at[i, cut[h]], got.at[slot], far_send.at[slot], far_recv.at[slot], peer)
        far[slot].start()
    fold(0)
    go(0, 0, 0, east)
    go(1, 0, 1, north)
    fold(1)
    go(2, 1, 0, east)
    fold(2)
    go(3, 2, 1, north)
    def join(i, h, slot):
        far[slot].wait_recv()
        def add(at, src):
            own[i, at] = (own[i, at].astype(F32) + got[slot, src].astype(F32)).astype(own.dtype)
        each(h * half, half, add)
    join(2, 0, 0)
    go(4, 2, 0, north)
    join(1, 1, 1)
    go(5, 1, 1, east)
    loads[3].wait(); nears[3].wait_recv()
    def first(h, slot):
        far[slot].wait_recv()
        def add(at, src):
            o_ref[at] = own[3, at].astype(F32) + near[3, at].astype(F32) + got[slot, src].astype(F32)
        each(h * half, half, add)
    first(0, 2)
    first(1, 3)
    def last(h, slot):
        far[slot].wait_recv()
        def add(at, src):
            o_ref[at] = o_ref[at] + got[slot, src].astype(F32)
        each(h * half, half, add)
    last(0, 4)
    last(1, 5)
    for c in nears: c.wait_send()
    for c in far.values(): c.wait_send()

def reduce_scatter4(p, after, n, cid):
    blk = p.shape[1:]
    return pl.pallas_call(rs4_kernel,
        out_shape=jax.ShapeDtypeStruct(blk, F32),
        in_specs=[pl.BlockSpec(memory_space=pl.ANY)] * 2,
        out_specs=pl.BlockSpec(memory_space=pltpu.VMEM),
        scratch_shapes=[pltpu.VMEM((4,) + blk, p.dtype), pltpu.VMEM((4,) + blk, p.dtype),
            pltpu.VMEM((6, blk[0] // 2) + blk[1:], p.dtype)] + [pltpu.SemaphoreType.DMA((4,))] * 3 + [pltpu.SemaphoreType.DMA((6,))] * 2,
        compiler_params=pltpu.CompilerParams(collective_id=cid, has_side_effects=True, vmem_limit_bytes=GIANT),
    )(p, after)


def start_kernel(n, x_ref, w_ref, o_ref, c_ref, swap_sem, swap_send, swap_recv, *sems):
    me = lax.axis_index("seq")
    others = [(me + d) % n for d in range(1, n)]
    greet(others)
    own = pltpu.make_async_copy(w_ref.at[me], c_ref.at[me], swap_sem)
    own.start()
    gather_start, gather_end = (ag4_parts if n == 8 else ag_parts)(n, x_ref, o_ref, *sems)
    gather_start()
    swaps = []
    for d in range(1, n):
        c = send(w_ref.at[others[d - 1]], c_ref.at[me], swap_send.at[d - 1], swap_recv.at[d - 1], others[d - 1])
        c.start()
        swaps.append(c)
    gather_end()
    own.wait()
    for c in swaps:
        c.wait()


def gather_and_exchange(x, w, n, cid):
    chips = n // 2
    far, near = (6, 7) if n == 8 else (chips, chips)
    anywhere = pl.BlockSpec(memory_space=pl.ANY)
    dma = pltpu.SemaphoreType.DMA
    return pl.pallas_call(
        functools.partial(start_kernel, n),
        out_shape=[jax.ShapeDtypeStruct((n,) + x.shape, x.dtype), jax.ShapeDtypeStruct(w.shape, w.dtype)],
        in_specs=[anywhere] * 2,
        out_specs=[anywhere] * 2,
        scratch_shapes=[dma, dma((n - 1,)), dma((n - 1,)), dma, dma((far,)), dma((far,)), dma((near,)), dma((near,))],
        compiler_params=pltpu.CompilerParams(collective_id=cid, has_side_effects=True),
    )(x, w)


def all_gather(x, n, cid):
    return (all_gather4 if n == 8 else all_gather_any)(x, n, cid)


def reduce_scatter(p, n, cid, after=None):
    after = jnp.zeros((8, 128), F32) if after is None else after
    return (reduce_scatter4 if n == 8 else reduce_scatter_any)(p, after, n, cid)


def mm_rs4_kernel(turned, *refs):
    terms = len(turned)
    a_refs, b_refs = refs[:terms], refs[terms : 2 * terms]
    after_ref, o_ref, part, near, got, near_send, near_recv, far_send, far_recv = refs[2 * terms :]
    me = lax.axis_index("seq")
    core, (sib, east, north, across) = square(me)
    x, y = (me // 2) % 2, me // 4
    greet([sib, east, north])
    rows = part.shape[2]
    half = rows // 2
    cut = (pl.ds(0, half), pl.ds(half, half))
    slab = 16
    own = part.at[1]

    def near_copy(i):
        return send(part.at[0, i], near.at[i], near_send.at[i], near_recv.at[i], sib)

    hops = ((0, 0, east), (0, 1, north), (1, 0, east), (2, 1, north), (2, 0, north), (1, 1, east))

    def far_copy(slot):
        i, h, peer = hops[slot]
        return send(own.at[i, cut[h]], got.at[slot], far_send.at[slot], far_recv.at[slot], peer)

    def each(first, count, body):
        def run(i, _):
            at = pl.multiple_of(i * slab, slab)
            body(pl.ds(pl.multiple_of(first + at, slab), slab), pl.ds(at, slab))
            return 0

        lax.fori_loop(0, count // slab, run, 0, unroll=2)

    def fold(i):
        near_copy(i).wait_recv()

        def add(at, _):
            own[i, at] = (own[i, at].astype(F32) + near[i, at].astype(F32)).astype(BF)

        each(0, rows, add)

    def step(s, _):
        i, mine = s // 2, s % 2
        yy, xx = (y + (i + 1) % 2) % 2, (x + 1 - i // 2) % 2
        seat = (yy * 2 + xx) * 2 + (core + 1 - mine) % 2
        total = None
        for a, b, t in zip(a_refs, b_refs, turned):
            term = (ntdot if t else dot)(a[seat], b[...])
            total = term if total is None else total + term
        part[mine, i] = total.astype(BF)

        @pl.when(mine == 0)
        def _():
            near_copy(i).start()

        @pl.when(s == 3)
        def _():
            fold(0)
            far_copy(0).start()
            far_copy(1).start()

        @pl.when(s == 5)
        def _():
            fold(1)
            far_copy(2).start()

        @pl.when(s == 6)
        def _():
            fold(2)
            far_copy(3).start()

        return 0

    lax.fori_loop(0, 8, step, 0)

    def join(i, h, slot):
        far_copy(slot).wait_recv()

        def add(at, src):
            own[i, at] = (own[i, at].astype(F32) + got[slot, src].astype(F32)).astype(BF)

        each(h * half, half, add)

    join(2, 0, 0)
    far_copy(4).start()
    join(1, 1, 1)
    far_copy(5).start()
    near_copy(3).wait_recv()

    def first(h, slot):
        far_copy(slot).wait_recv()

        def add(at, src):
            o_ref[at] = own[3, at].astype(F32) + near[3, at].astype(F32) + got[slot, src].astype(F32)

        each(h * half, half, add)

    first(0, 2)
    first(1, 3)

    def last(h, slot):
        far_copy(slot).wait_recv()

        def add(at, src):
            o_ref[at] = o_ref[at] + got[slot, src].astype(F32)

        each(h * half, half, add)

    last(0, 4)
    last(1, 5)
    for i in range(4):
        near_copy(i).wait_send()
    for slot in range(6):
        far_copy(slot).wait_send()


def product_scatter(pairs, n, cid, after=None):
    after = jnp.zeros((8, 128), F32) if after is None else after
    rows = pairs[0][0].shape[0] // n
    cols = pairs[0][1].shape[0 if pairs[0][2] else 1]
    if n != 8:
        total = sum((ntdot if t else dot)(a, b) for a, b, t in pairs)
        return reduce_scatter(total.astype(BF).reshape(n, rows, cols), n, cid, after)
    vmem = pl.BlockSpec(memory_space=pltpu.VMEM)
    dma = pltpu.SemaphoreType.DMA
    return pl.pallas_call(
        functools.partial(mm_rs4_kernel, tuple(t for _, _, t in pairs)),
        out_shape=jax.ShapeDtypeStruct((rows, cols), F32),
        in_specs=[vmem] * (2 * len(pairs)) + [pl.BlockSpec(memory_space=pl.ANY)],
        out_specs=vmem,
        scratch_shapes=[
            pltpu.VMEM((2, 4, rows, cols), BF),
            pltpu.VMEM((4, rows, cols), BF),
            pltpu.VMEM((6, rows // 2, cols), BF),
            dma((4,)), dma((4,)), dma((6,)), dma((6,)),
        ],
        compiler_params=pltpu.CompilerParams(collective_id=cid, has_side_effects=True, vmem_limit_bytes=GIANT),
    )(*(a.reshape(n, rows, a.shape[1]) for a, _, _ in pairs), *(b for _, b, _ in pairs), after)


class HeadPlan:
    def __init__(self, n):
        self.n = n
        self.per = -(-HEADS // n)
        group = HEADS // KVH
        self.first_kv, self.slots = [], 1
        for i in range(n):
            low, high = i * self.per, min((i + 1) * self.per, HEADS) - 1
            if low >= HEADS:
                self.first_kv.append(KVH)
            else:
                self.first_kv.append(low // group)
                self.slots = max(self.slots, high // group - low // group + 1)
        self.width = self.per * HEAD
        self.kv_width = self.slots * HEAD

    def head_table(self):
        group = HEADS // KVH
        rows = []
        for i in range(self.n):
            heads = [i * self.per + j for j in range(self.per)]
            rows.append(
                [h // group - self.first_kv[i] if h < HEADS else 0 for h in heads]
                + [int(h < HEADS) for h in heads]
            )
        return jnp.array(rows, jnp.int32)

    def kv_used(self, i):
        group = HEADS // KVH
        heads = range(i * self.per, min((i + 1) * self.per, HEADS))
        return sorted({h // group for h in heads})

    def split_columns(self, w):
        rows = w.shape[0]
        q = jnp.pad(w[:, : HEADS * HEAD], ((0, 0), (0, self.n * self.width - HEADS * HEAD)))
        parts = []
        for i in range(self.n):
            pieces = [q[:, i * self.width : (i + 1) * self.width]]
            for kind in range(2):
                start = HEADS * HEAD + kind * KVH * HEAD
                used = self.kv_used(i)
                for slot in range(self.slots):
                    g = self.first_kv[i] + slot
                    if g in used:
                        pieces.append(w[:, start + g * HEAD : start + (g + 1) * HEAD])
                    else:
                        pieces.append(jnp.zeros((rows, HEAD), w.dtype))
            parts.append(jnp.concatenate(pieces, axis=1))
        return jnp.stack(parts)

    def join_columns(self, g):
        q = [g[i, :, : self.width] for i in range(self.n)]
        q = jnp.concatenate(q, axis=1)[:, : HEADS * HEAD].astype(F32)
        kv = []
        for kind in range(2):
            for head in range(KVH):
                total = 0.0
                for i in range(self.n):
                    if head in self.kv_used(i):
                        at = self.width + kind * self.kv_width + (head - self.first_kv[i]) * HEAD
                        total = total + g[i, :, at : at + HEAD].astype(F32)
                kv.append(total)
        return jnp.concatenate([q] + kv, axis=1)


def reblock(rows, have, want, total):
    n, me = lax.axis_size("seq"), lax.axis_index("seq")
    result = jnp.zeros((want,) + rows.shape[1:], rows.dtype)
    pad = jnp.pad(rows, ((want, want), (0, 0)))
    for shift in range(-(n - 1), n):
        pairs = []
        for i in range(n):
            j = i + shift
            if 0 <= j < n:
                low = max(i * have, j * want)
                high = min((i + 1) * have, (j + 1) * want, total)
                if low < high:
                    pairs.append((i, j))
        if not pairs:
            continue
        start = want + (me + shift) * want - me * have
        piece = lax.dynamic_slice_in_dim(pad, jnp.clip(start, 0, have + want), want, 0)
        if shift:
            piece = lax.ppermute(piece, "seq", pairs)
        else:
            ok = jnp.array([(i, i) in pairs for i in range(n)])[me]
            piece = jnp.where(ok, piece, jnp.zeros_like(piece))
        result = result + piece
    return result


def per_device(tokens, lengths, cotangent, w_qkv, w_ao, w_in, w_xp, w_dt, w_so, w_gu, w_down,
               norm_in, norm_attn, norm_ssm, norm_ffn, conv_w, conv_b, dt_bias, a_log, d_skip):
    seqs, slot_len, width = tokens.shape
    n, me, replicas = lax.axis_size("seq"), lax.axis_index("seq"), lax.axis_size("dp")
    local, rows = seqs * slot_len, seqs * slot_len * n
    cols = INNER // n
    plan = HeadPlan(n)
    w_rows, ao_rows = w_qkv.shape[0], w_ao.shape[0]
    pos = me * slot_len + jnp.arange(slot_len, dtype=jnp.int32)
    is_valid = pos[None, :] < lengths[:, None]
    table = plan.head_table()[me]
    tie = lax.optimization_barrier
    flat = lambda v: v.reshape(rows, v.shape[-1])
    gather = lambda v, cid: flat(all_gather(v, n, cid))
    scatter = lambda v, cid, after=None: reduce_scatter(
        v.astype(BF).reshape(n, local, v.shape[-1]), n, cid, after
    )
    later = lambda g, zero: g + zero.astype(g.dtype)
    exchange = lambda v: lax.all_to_all(v, "seq", 0, 0, tiled=True)
    blocks = lambda v: v.reshape(n, seqs, slot_len, v.shape[-1])
    mine = lambda v: lax.dynamic_slice_in_dim(v, me * cols, cols, v.ndim - 1)
    over = lambda g: lax.psum(g, "dp")

    def row_sums(a, b, cid):
        both = jnp.stack([a, b]).reshape(-1, 128)
        return small_sum(both, n, cid).reshape(2, rows)

    wdt = mine(w_dt)
    taps, bias, dtb, skip = mine(conv_w), mine(conv_b), mine(dt_bias), mine(d_skip)
    rate = -jnp.exp(mine(a_log))
    ssm_gain = mine(norm_ssm)
    attn_gain = lax.dynamic_slice_in_dim(
        jnp.pad(norm_attn, (0, n * plan.width - HEADS * HEAD)), me * plan.width, plan.width, 0
    )

    x = tokens.astype(F32).reshape(local, width)
    scale_in = lax.rsqrt(jnp.mean(x * x, axis=-1, keepdims=True) + EPSILON)
    normed, qkv_cols = gather_and_exchange(
        (x * scale_in * norm_in).astype(BF), plan.split_columns(w_qkv), n, 1
    )
    normed, qkv_cols = flat(normed), qkv_cols.reshape(n * w_rows, -1)
    qkv = dot(normed, qkv_cols).astype(BF)
    behind = 0.0 * normed[0, 0].astype(F32)
    in_parts = later(jnp.transpose(w_in.reshape(w_rows, 2, n, cols), (1, 2, 0, 3)), behind)
    wx = exchange(in_parts[0]).reshape(n * w_rows, cols)
    wz = exchange(in_parts[1]).reshape(n * w_rows, cols)
    behind = 0.0 * qkv[0, 0].astype(F32)
    ao_all = lax.all_gather(later(w_ao, behind), "seq", axis=0, tiled=True)
    ao_mine = lax.dynamic_slice_in_dim(
        jnp.pad(ao_all, ((0, n * plan.width - HEADS * HEAD), (0, 0))), me * plan.width, plan.width, 0
    )
    upstream = (cotangent.astype(F32) * is_valid[..., None]).reshape(local, width)
    upstream_all = lax.all_gather(later(upstream.astype(BF), behind), "seq", axis=0, tiled=True)
    q = blocks(qkv[:, : plan.width])
    k = blocks(qkv[:, plan.width : plan.width + plan.kv_width])
    v = blocks(qkv[:, plan.width + plan.kv_width :])
    attended, lse = attn_forward(table, lengths, q, k, v)
    attended_rows = flat(attended)

    x_conv = blocks(dot(normed, wx).astype(BF))
    z_gate = dot(normed, wz)
    edge = KCONV - 1
    before = jnp.concatenate(
        [jnp.zeros((1, seqs, edge, cols), BF), x_conv[:-1, :, slot_len - edge :]], axis=0
    )
    padded = jnp.concatenate([before, x_conv], axis=2).astype(F32)
    conv_pre = bias + sum(taps[o] * padded[:, :, o : o + slot_len] for o in range(KCONV))
    mixer_in = jax.nn.silu(conv_pre)
    mixer_low = flat(mixer_in).astype(BF)
    projected = lax.psum(dot(mixer_low, w_xp), "seq")
    step_low = projected[:, :DTR].astype(BF)
    b_input, c_output = projected[:, DTR : DTR + NST], projected[:, DTR + NST :]
    step_pre = blocks(dot(step_low, wdt) + dtb)
    turn = lambda m: jnp.swapaxes(m.reshape(n, seqs, slot_len // CHUNK, CHUNK, NST), 3, 4)
    bt, ct = turn(b_input), turn(c_output)
    core, start = scan_forward(step_pre, mixer_in, bt, blocks(c_output), rate, skip[None])
    core = flat(core)
    gated = core * jax.nn.silu(z_gate)
    squares = row_sums(
        jnp.sum(attended_rows * attended_rows, axis=1), jnp.sum(gated * gated, axis=1), 2
    )
    r_attn = lax.rsqrt(squares[0] / (HEADS * HEAD) + EPSILON)[:, None]
    r_ssm = lax.rsqrt(squares[1] / INNER + EPSILON)[:, None]
    attn_low = (attended_rows * r_attn * attn_gain).astype(BF)
    ssm_low = (gated * r_ssm * ssm_gain).astype(BF)
    mixed = product_scatter(((attn_low, ao_mine, False), (ssm_low, w_so, False)), n, 3)
    residual = x + 0.5 * mixed
    r_ffn = lax.rsqrt(jnp.mean(residual * residual, axis=-1, keepdims=True) + EPSILON)
    normed_two = gather((residual * r_ffn * norm_ffn).astype(BF), 4)
    w_gate, w_up = w_gu[:, 0], w_gu[:, 1]
    gate, up = dot(normed_two, w_gate), dot(normed_two, w_up)
    activated = (jax.nn.silu(gate) * up).astype(BF)

    grad_act = ntdot(upstream_all, w_down)
    grad_gate = (grad_act * up * silu_grad(gate)).astype(BF)
    grad_up = (grad_act * jax.nn.silu(gate)).astype(BF)
    g_down = tndot(activated, upstream_all).astype(BF)
    g_gate, g_up = tndot(normed_two, grad_gate).astype(BF), tndot(normed_two, grad_up).astype(BF)
    s_down, s_gate, s_up = over((g_down, g_gate, g_up))
    grad_two = product_scatter(((grad_gate, w_gate, True), (grad_up, w_up, True)), n, 5)
    def norm_pull(grad, values, r, gain):
        dotted = jnp.mean(grad * gain * values, axis=-1, keepdims=True)
        return r * (grad * gain - values * (r * r * dotted)), jnp.sum(grad * values * r, axis=0)

    add, g_norm_ffn = norm_pull(grad_two, residual, r_ffn, norm_ffn)
    grad_residual = upstream + add
    mix_low = gather(grad_residual.astype(BF), 7)
    d_attn = 0.5 * ntdot(mix_low, ao_mine)
    d_ssm = 0.5 * ntdot(mix_low, w_so)
    inner = row_sums(
        jnp.sum(d_attn * attn_gain * attended_rows, axis=1),
        jnp.sum(d_ssm * ssm_gain * gated, axis=1),
        8,
    )
    t_attn = (inner[0] / (HEADS * HEAD))[:, None] * r_attn * r_attn
    t_ssm = (inner[1] / INNER)[:, None] * r_ssm * r_ssm
    grad_heads = (r_attn * (d_attn * attn_gain - attended_rows * t_attn)).astype(BF)
    grad_gated = r_ssm * (d_ssm * ssm_gain - gated * t_ssm)
    g_norm_attn = jnp.sum(d_attn * attended_rows * r_attn, axis=0)
    g_norm_ssm = jnp.sum(d_ssm * gated * r_ssm, axis=0)

    gq, gk, gv = attn_backward(table, lengths, q, k, v, blocks(grad_heads), attended, lse)
    grad_qkv = flat(jnp.concatenate([gq, gk, gv], axis=3))
    grad_core = grad_gated * jax.nn.silu(z_gate)
    grad_z = (grad_gated * core * silu_grad(z_gate)).astype(BF)
    g_ao = reblock((0.5 * tndot(attn_low, mix_low)).astype(BF), plan.width, ao_rows, HEADS * HEAD)
    g_so = (0.5 * tndot(ssm_low, mix_low)).astype(BF)
    g_z = exchange(tndot(normed, grad_z).astype(BF).reshape(n, w_rows, cols))
    g_qkv = exchange(tndot(normed, grad_qkv).astype(BF).reshape(n, w_rows, -1))
    g_qkv = plan.join_columns(g_qkv).astype(BF)
    grad_core, grad_z, grad_qkv = tie((grad_core, grad_z, grad_qkv))
    gpre, gmix, gb, gc, grate, gskip = scan_backward(
        step_pre, mixer_in, blocks(grad_core), start, bt, ct, blocks(b_input), rate, skip[None]
    )
    gpre = flat(gpre)
    nothing = lambda *sums: 0.0 * sum(g.reshape(-1)[0].astype(F32) for g in sums)
    after_one = nothing(s_down, s_gate, s_up, grate)
    s_ao, s_so, s_z, s_qkv = over(tuple(later(g, after_one) for g in (g_ao, g_so, g_z, g_qkv)))
    g_dt_bias = jnp.sum(gpre, axis=0)
    grad_step = gpre.astype(BF)
    grad_projected = jnp.concatenate([ntdot(grad_step, wdt), flat(gb), flat(gc)], axis=1)
    grad_projected = gather(scatter(grad_projected, 9, jnp.full((8, 128), after_one)).astype(BF), 10)
    grad_mixer = gmix + blocks(ntdot(grad_projected, w_xp))
    grad_conv = grad_mixer * silu_grad(conv_pre)
    g_conv_b = jnp.sum(grad_conv, axis=(0, 1, 2))
    g_conv_w = jnp.stack(
        [jnp.sum(grad_conv * padded[:, :, o : o + slot_len], axis=(0, 1, 2)) for o in range(KCONV)]
    )
    after = jnp.concatenate(
        [grad_conv[1:, :, :edge], jnp.zeros((1, seqs, edge, cols), F32)], axis=0
    )
    extended = jnp.concatenate([grad_conv, after], axis=2)
    grad_x = sum(taps[o] * extended[:, :, edge - o : edge - o + slot_len] for o in range(KCONV))
    grad_x = flat(grad_x).astype(BF)
    g_x = exchange(tndot(normed, grad_x).astype(BF).reshape(n, w_rows, cols))
    g_xp = tndot(mixer_low, grad_projected).astype(BF)
    g_wdt = tndot(step_low, grad_step).astype(BF)
    after_two = nothing(s_ao, s_so, s_z, s_qkv)
    s_x, s_xp, s_wdt = over(tuple(later(g, after_two) for g in (g_x, g_xp, g_wdt)))
    grad_normed = product_scatter(
        ((grad_x, wx, True), (grad_z, wz, True), (grad_qkv, qkv_cols, True)), n, 11, jnp.full((8, 128), after_two)
    )
    block_out = residual + product_scatter(((activated, w_down, False),), n, 6, grad_normed[:8, :128])
    add_in, g_norm_in = norm_pull(grad_normed, x, scale_in, norm_in)
    grad_tokens = grad_residual + add_in

    s_in = jnp.stack([s_x, s_z])
    s_in = jnp.transpose(s_in, (2, 0, 1, 3)).reshape(w_rows, 2 * INNER)
    s_gu = jnp.stack([s_gate, s_up], axis=1)

    place = lambda g: lax.dynamic_update_slice_in_dim(
        jnp.zeros((n * plan.width,), F32), g, me * plan.width, 0
    )[: HEADS * HEAD]

    def pad_rows(v):
        v = v.reshape(-1)
        return jnp.pad(v, (0, -v.size % 1024)).reshape(-1, 128)

    shared = jnp.stack([g_norm_in, place(g_norm_attn), g_norm_ffn])
    total = small_sum(pad_rows(shared), n, 12).reshape(-1)[: shared.size].reshape(shared.shape)
    shared = lax.dynamic_slice_in_dim(total, me * w_rows, w_rows, 1)
    owned = jnp.concatenate(
        [g_norm_ssm[None], g_conv_w, g_conv_b[None], g_dt_bias[None], grate * rate, gskip], axis=0
    )
    small = pad_rows(jnp.concatenate([shared.reshape(-1), owned.reshape(-1)]))
    small = small_sum(small, replicas, 13, "dp").reshape(-1)
    s_shared = small[: shared.size].reshape(shared.shape)
    s_owned = small[shared.size : shared.size + owned.size].reshape(owned.shape)
    full = lambda g: g.astype(F32)

    return (
        block_out.astype(BF).reshape(seqs, slot_len, width),
        grad_tokens.reshape(seqs, slot_len, width),
        full(s_qkv),
        full(s_ao),
        full(s_in),
        full(s_xp),
        full(s_wdt),
        full(s_so),
        full(s_gu),
        full(s_down),
        s_shared[0],
        s_shared[1],
        s_owned[0],
        s_shared[2],
        s_owned[1 : 1 + KCONV],
        s_owned[1 + KCONV],
        s_owned[2 + KCONV],
        s_owned[3 + KCONV : 3 + KCONV + NST],
        s_owned[3 + KCONV + NST],
    )


def solution(mesh):
    rows, cols, flat = P("seq", None), P(None, "seq"), P("seq")
    act = P("dp", "seq", None)
    hid = P(None, None, "seq")
    in_specs = (act, P("dp"), act, rows, rows, rows, rows, P(), rows, hid, rows) + (P(),) * 9
    out_specs = (act, act, rows, rows, rows, rows, cols, rows, hid, rows,
                 flat, flat, flat, flat, cols, flat, flat, cols, flat)
    return jax.shard_map(per_device, mesh=mesh, in_specs=in_specs, out_specs=out_specs, check_vma=False)
```

time: 3150 us -> 1230 us (0.39)
  waiting for transfers between devices: 1220 us -> 193 us
  other arithmetic: 876 us -> 103 us
  Pallas kernels: 0 us -> 518 us
  local copies, waits for them, and re-layouts: 551 us -> 198 us
  blocking collectives: 151 us -> 0 us
  matrix products: 280 us -> 156 us
    unnamed x42 -> x6, waiting for transfers between devices: 603 us -> 0.1 us
    pallas_call x0 -> x17, Pallas kernels: none -> 518 us  [the longest x4 164 us: product_scatter(): pl.pallas_call(functools.partial(mm_rs4_kernel, tuple((t for _, _, t in p...]
    all_gather x14 -> x2, waiting for transfers between devices: 370 us -> 0.01 us  [the longest x1 0.01 us: per_device(): ao_all = lax.all_gather(later(w_ao, behind), 'seq', axis=0, tiled=True)]
    reduce_scatter x7 -> x0, waiting for transfers between devices: 247 us -> none  [the longest x1 68 us: per_device(): lax.psum_scatter(grad_qkv.astype(jnp.bfloat16), 'seq', scatter_dimension=...]
    mul x196 -> x7, other arithmetic: 246 us -> 3.74 us  [the longest x1 1.27 us: per_device(): cotangent.astype(F32) * is_valid[..., None]]
    reduce_sum x107 -> x7, other arithmetic: 225 us -> 14.9 us  [the longest x2 4.52 us: norm_pull(): jnp.sum(grad * values * r, axis=0)]
    dynamic_update_slice x192 -> x0, other arithmetic: 207 us -> none  [run_block(): return lax.scan(advance, carried, block_series, unroll=4)]
    psum x0 -> x4, waiting for transfers between devices: none -> 173 us  [the longest x3 173 us: per_device(): over = lambda g: lax.psum(g, 'dp')]
  transfers between devices with their start and end apart: 34 -> 13, of which waited for: 22 -> 4; matrix products, arithmetic and copies ran while one was open for 22% -> 24% of each run, Pallas kernels for 0% -> 31%
where the time goes in v1:
time: 1230 us; the launch traced here: 1220 us
  Pallas kernels  518 us (42%)
  local copies, waits for them, and re-layouts  198 us (16%)
  waiting for transfers between devices  193 us (16%)
  matrix products  156 us (13%)
  other arithmetic  103 us (8%)
  starting transfers between devices  27.2 us (2%)
  between operations  22 us (2%)
    psum x3, waiting for transfers between devices, per_device(): over = lambda g: lax.psum(g, 'dp')  173 us
    pallas_call x4, Pallas kernels, product_scatter(): pl.pallas_call(functools.partial(mm_rs4_kernel, tuple((t for _, _, t in p...  164 us
    pallas_call x1, Pallas kernels, scan_backward(): pl.pallas_call(scan_bwd_kernel, grid=(seqs, n), in_specs=[big(cols), big(...  87.1 us
    pallas_call x3, Pallas kernels, all_gather4(): pl.pallas_call(ag4_kernel, out_shape=jax.ShapeDtypeStruct((n,) + x.shape,...  75.7 us
    dot_general x10, matrix products, tndot(): return lax.dot_general(a, b, TN, preferred_element_type=F32)  72.1 us
    pallas_call x1, Pallas kernels, gather_and_exchange(): pl.pallas_call(functools.partial(start_kernel, n), out_shape=[jax.ShapeDt...  53.5 us
    dot_general x7, matrix products, dot(): return jnp.dot(a, b, preferred_element_type=F32)  49.6 us
    pallas_call x1, Pallas kernels, attn_backward(): pl.pallas_call(attn_bwd_kernel, grid=(seqs,), in_specs=[smem, smem, big(w...  36.8 us
  transfers between devices with their start and end apart: 13, of which 4 were waited for; matrix products, arithmetic and copies ran while one was open for 24% of the time, Pallas kernels for 31%

profile of v1, /device:TPU:0, one launch (start us, length us, event | category | flops | bytes accessed | tf_op | source)
XLA Modules:
  0.0 1217.4 jit_solution(14736441358312935591)
XLA Ops:
  26.8 53.5 %shard_map.357 = (bf16[8,256,1600]{2,1,0:T(8,128)(2,1)}, bf16[8,200,512]{2,1,0:T(8,128)(2,1)}) custom-call(bf16[256,1600]{1,0:T(8,128)(2,1)} %fusion.26.x_ref, bf16[8,200,512]{2,1,0:T(8,128)(2,1)} %bitcast_dynamic-update-slice_fusion.w_ref), custom_call_target="tpu_custom_call" | custom-call | tf_op jit(solution)/shard_map/pallas_call | solution.py:665
  84.0 8.3 add.377
  103.5 19.8 %all-to-all-done = bf16[8,200,400]{2,1,0:T(8,128)(2,1)S(1)} async-done(((bf16[8,200,400]{2,1,0:T(8,128)(2,1)}), bf16[8,200,400]{2,1,0:T(8,128)(2,1)S(1)}, u32[]{:S(2)}, u32[]{:S(2)}) %all-to-all-start) | async-done | bytes 1280032 | tf_op jit(solution)/shard_map/all_to_all | solution.py:931
  124.5 7.3 convolution_convert_fusion.7
  135.4 4.8 fusion.76
  143.9 7.2 convolution_convert_fusion.4
  159.3 4.3 all-to-all-start.1
  168.3 29.4 %shard_map.358 = (f32[8,2,128,256]{3,2,1,0:T(8,128)}, f32[8,2,128,4]{3,2,1,0:T(8,128)}) custom-call(s32[8]{0:T(128)} %fusion.70.slot_ref, s32[2]{0:T(128)} %len_ref.3, bf16[8,2,128,256]{3,2,1,0:T(8,128)(2,1)} %bitcast.303, bf16[8,2,128,128]{3,2,1,0:T(8,128)(2,1)} %bitcast.328, bf16[8,2,128,128]{3,2,1,0:T(8,128)(2,1)} %bitcast.326), custom_call_target="tpu_custom_call" | custom-call | tf_op jit(solution)/shard_map/pallas_call | solution.py:288
  202.0 4.1 fusion.78
  208.3 4.5 copy.140
  212.8 5.6 copy.141
  227.1 5.0 copy.103
  234.7 31.6 %shard_map.359 = (f32[8,2,128,400]{3,2,1,0:T(8,128)}, f32[8,2,16,400]{3,2,1,0:T(8,128)}) custom-call(f32[8,2,128,400]{3,2,1,0:T(8,128)} %bitcast.290, f32[8,2,128,400]{3,2,1,0:T(8,128)} %get-tuple-element.146.mix_ref, f32[8,2,8,16,16]{4,3,2,1,0:T(8,128)} %get-tuple-element.215.bt_ref, f32[8,2,128,16]{3,2,1,0:T(8,128)} %bitcast.332, ...), custom_call_target="tpu_custom_call" | custom-call | tf_op jit(solution)/shard_map/pallas_call | solution.py:97
  266.3 5.2 copy.106
  271.6 10.9 multiply_reduce_fusion.6
  283.1 8.4 shard_map.360
  305.2 38.9 %shard_map.361 = f32[256,1600]{1,0:T(8,128)} custom-call(bf16[8,256,256]{2,1,0:T(8,128)(2,1)} %fusion.24.refs_0_, bf16[8,256,400]{2,1,0:T(8,128)(2,1)} %bitcast.312, bf16[256,1600]{1,0:T(8,128)(2,1)} %pad_dynamic-slice_fusion.refs_2_, bf16[400,1600]{1,0:T(8,128)(2,1)} %refs_3_.1, f32[8,128]{1,0:T(8,128)} %broadcast_21_refs_4_.2.refs_4_), custom_call_target="tpu_custom_call" | custom-call | tf_op jit(solution)/shard_map/pallas_call | solution.py:807
  348.7 32.7 %shard_map.362 = bf16[8,256,1600]{2,1,0:T(8,128)(2,1)} custom-call(bf16[256,1600]{1,0:T(8,128)(2,1)} %multiply_convert_fusion.6.x_ref), custom_call_target="tpu_custom_call" | custom-call | tf_op jit(solution)/shard_map/pallas_call | solution.py:558
  381.5 10.0 fusion.11
  391.5 8.7 fusion.13
  400.2 14.6 %multiply_convert_fusion = (bf16[2048,688]{0,1:T(8,128)(2,1)}, bf16[2048,688]{0,1:T(8,128)(2,1)}, bf16[2048,688]{0,1:T(8,128)(2,1)}) fusion(f32[2048,688]{0,1:T(8,128)} %fusion.13, f32[2048,688]{0,1:T(8,128)} %fusion.11, bf16[2048,1600]{1,0:T(8,128)(2,1)} %all-gather.5.cloned.1.call-done, bf16[688,1600]{1,0:T(8,128)(2,1)} %refs_1_.1), kind=kOutput, calls=%fused_computation.2 | convolution fusion | flops 4530012160 | bytes 28481536 | tf_op jit(solution)/shard_map/dot_general | solution.py:33
  414.8 4.6 copy.113
  419.4 9.8 convolution_convert_fusion
  429.2 4.6 copy.112
  433.8 9.9 convolution_convert_fusion.1
  443.7 43.5 %shard_map.363 = f32[256,1600]{1,0:T(8,128)} custom-call(bf16[8,256,688]{2,1,0:T(8,128)(2,1)} %bitcast.300, bf16[8,256,688]{2,1,0:T(8,128)(2,1)} %bitcast.299, bf16[1600,688]{1,0:T(8,128)(2,1)} %bitcast.301, bf16[1600,688]{1,0:T(8,128)(2,1)} %bitcast.302, f32[8,128]{1,0:T(8,128)} %broadcast_21_refs_4_.2.refs_4_), custom_call_target="tpu_custom_call" | custom-call | tf_op jit(solution)/shard_map/pallas_call | solution.py:807
  493.5 32.6 %shard_map.364 = bf16[8,256,1600]{2,1,0:T(8,128)(2,1)} custom-call(bf16[256,1600]{1,0:T(8,128)(2,1)} %get-tuple-element.139.x_ref), custom_call_target="tpu_custom_call" | custom-call | tf_op jit(solution)/shard_map/pallas_call | solution.py:558
  526.1 9.4 multiply_reduce_fusion.4
  535.6 3.9 fusion.22
  540.1 6.2 shard_map.365
  547.1 9.8 convolution_convert_fusion.2
  559.8 36.8 %shard_map.366 = (bf16[8,2,128,256]{3,2,1,0:T(8,128)(2,1)}, bf16[8,2,128,128]{3,2,1,0:T(8,128)(2,1)}, bf16[8,2,128,128]{3,2,1,0:T(8,128)(2,1)}) custom-call(s32[8]{0:T(128)} %fusion.70.slot_ref, s32[2]{0:T(128)} %len_ref.3, bf16[8,2,128,256]{3,2,1,0:T(8,128)(2,1)} %bitcast.304, bf16[8,2,128,128]{3,2,1,0:T(8,128)(2,1)} %bitcast.329, ...), custom_call_target="tpu_custom_call" | custom-call | tf_op jit(solution)/shard_map/pallas_call | solution.py:342
  598.4 8.6 convolution_convert_fusion.3
  610.6 7.3 multiply_convert_fusion.3
  617.8 5.0 copy.115
  622.8 87.1 %shard_map.367 = (f32[8,2,128,400]{3,2,1,0:T(8,128)}, f32[8,2,128,400]{3,2,1,0:T(8,128)}, f32[8,2,128,16]{3,2,1,0:T(8,128)}, f32[8,2,128,16]{3,2,1,0:T(8,128)}, f32[16,400]{1,0:T(8,128)}, /*index=5*/f32[1,400]{1,0:T(1,128)}) custom-call(f32[8,2,128,400]{3,2,1,0:T(8,128)} %bitcast.291, f32[8,2,128,400]{3,2,1,0:T(8,128)} %get-tuple-element.146.mix_ref, ...), custom_call_target="tpu_custom_call" | custom-call | tf_op jit(solution)/shard_map/pallas_call | solution.py:220
  711.3 7.7 convolution_convert_fusion.5
  722.5 5.2 fusion.9
  741.8 5.6 all-to-all-start.2
  750.1 50.0 %all-reduce.22.cloned.1.call-done = (bf16[688,1600]{1,0:T(8,128)(2,1)}, bf16[1600,688]{0,1:T(8,128)(2,1)}, bf16[1600,688]{0,1:T(8,128)(2,1)}) async-done(((bf16[688,1600]{1,0:T(8,128)(2,1)}, bf16[1600,688]{0,1:T(8,128)(2,1)}, bf16[1600,688]{0,1:T(8,128)(2,1)}), (bf16[688,1600]{1,0:T(8,128)(2,1)}, bf16[1600,688]{0,1:T(8,128)(2,1)}, bf16[1600,688]{0,1:T(8,128)(2,1)})) %all-reduce.22.cloned.1.call-update) | async-done | bytes 6604816 | tf_op jit(solution)/shard_map/psum | solution.py:934
  800.1 4.5 copy.121
  804.6 5.6 reshape.530
  811.4 4.4 reshape.529
  816.3 4.6 copy.122
  821.0 5.6 reshape.531
  830.4 7.6 fusion.10
  851.3 3.9 copy.125
  859.4 11.1 shard_map.368
  872.1 10.4 shard_map.369
  882.4 5.4 multiply_multiply_fusion
  890.1 4.5 multiply_reduce_fusion
  895.0 7.7 convolution_convert_fusion.6
  906.1 4.4 all-to-all-start.4
  910.6 5.9 maximum_convert_fusion
  916.5 95.8 %all-reduce.20.cloned.1.call-done = (bf16[200,1600]{1,0:T(8,128)(2,1)}, bf16[400,1600]{1,0:T(8,128)(2,1)}, bf16[8,200,400]{2,1,0:T(8,128)(2,1)}, bf16[200,2240]{1,0:T(8,128)(2,1)}) async-done(((bf16[200,1600]{1,0:T(8,128)(2,1)}, bf16[400,1600]{1,0:T(8,128)(2,1)}, bf16[8,200,400]{2,1,0:T(8,128)(2,1)}, bf16[200,2240]{1,0:T(8,128)(2,1)}), (bf16[200,1600]{1,0:T(8,128)(2,1)}, bf16[400,1600]{1,0:T(8,128)(2,1)}, ...) | async-done | bytes 4096016 | tf_op jit(solution)/shard_map/psum | solution.py:934
  1012.3 4.3 reshape.536
  1021.8 4.4 reshape.538
  1032.2 43.5 %shard_map.370 = f32[256,1600]{1,0:T(8,128)} custom-call(bf16[8,256,400]{2,1,0:T(8,128)(2,1)} %bitcast.311, bf16[8,256,400]{2,1,0:T(8,128)(2,1)} %bitcast.309, bf16[8,256,512]{2,1,0:T(8,128)(2,1)} %bitcast.314, bf16[1600,400]{1,0:T(8,128)(2,1)} %bitcast.325, bf16[1600,400]{1,0:T(8,128)(2,1)} %bitcast.34.refs_4_, bf16[1600,512]{1,0:T(8,128)(2,1)} %bitcast.338, ...), custom_call_target="tpu_custom_call" | custom-call | tf_op jit(solution)/shard_map/pallas_call | solution.py:807
  1078.4 6.3 shard_map.372
  1086.3 7.9 shard_map.373
  1118.9 38.5 %shard_map.371 = f32[256,1600]{1,0:T(8,128)} custom-call(bf16[8,256,688]{2,1,0:T(8,128)(2,1)} %bitcast.298, bf16[688,1600]{1,0:T(8,128)(2,1)} %refs_1_.1, f32[8,128]{1,0:T(8,128)} %slice.436.refs_2_), custom_call_target="tpu_custom_call" | custom-call | tf_op jit(solution)/shard_map/pallas_call | solution.py:807
  1165.3 27.1 %all-reduce.18.cloned.1.call-done = (bf16[1,8,200,400]{3,2,1,0:T(8,128)(2,1)}, bf16[400,132]{0,1:T(8,128)(2,1)}, bf16[100,400]{0,1:T(8,128)(2,1)}) async-done(((bf16[1,8,200,400]{3,2,1,0:T(8,128)(2,1)}, bf16[400,132]{0,1:T(8,128)(2,1)}, bf16[100,400]{0,1:T(8,128)(2,1)}), (bf16[1,8,200,400]{3,2,1,0:T(8,128)(2,1)}, bf16[400,132]{0,1:T(8,128)(2,1)}, bf16[100,400]{0,1:T(8,128)(2,1)})) %all-reduce.18.cloned.1.call-update) | async-done | bytes 1465616 | tf_op jit(solution)/shard_map/psum | solution.py:934
  1194.3 6.5 copy.129
  1200.8 8.1 reshape.557
  (317 shorter events, 204.7 us)
Async XLA Ops:
  7.2 216.4 %copy-start = (bf16[100,3200]{1,0:T(8,128)(2,1)S(1)}, bf16[100,3200]{1,0:T(8,128)(2,1)}, u32[]{:S(2)}) copy-start(bf16[100,3200]{1,0:T(8,128)(2,1)} %param.29) | copy-start | bytes 1920004
  7.2 6.1 copy-start.63
  7.2 5.1 copy-start.30
  12.3 13.4 %copy-start.4 = (f32[2,128,1600]{2,1,0:T(8,128)}, f32[2,128,1600]{2,1,0:T(8,128)S(1)}, u32[]{:S(2)}) copy-start(f32[2,128,1600]{2,1,0:T(8,128)S(1)} %copy.99) | copy-start | bytes 4915204
  13.3 3.9 copy-start.59
  16.2 9.5 copy-start.47
  17.2 9.7 copy-start.57
  98.0 25.3 %all-to-all-start = ((bf16[8,200,400]{2,1,0:T(8,128)(2,1)}), bf16[8,200,400]{2,1,0:T(8,128)(2,1)S(1)}, u32[]{:S(2)}, u32[]{:S(2)}) async-start(bf16[8,200,400]{2,1,0:T(8,128)(2,1)} %get-tuple-element.159), calls=%async_computation | async-start | bytes 3276800 | tf_op jit(solution)/shard_map/all_to_all | solution.py:931
  101.6 117.4 %all-reduce.16.cloned.1.call-start = ((), (), s32[]{:S(2)}) async-start(), calls=%async_computation.5 | async-start | bytes 2228224 | tf_op jit(solution)/shard_map/psum | solution.py:982
  103.4 31.9 %copy-start.49 = (f32[1,400]{1,0:T(1,128)}, f32[1,400]{1,0:T(1,128)S(1)}, u32[]{:S(2)}) copy-start(f32[1,400]{1,0:T(1,128)S(1)} %get-tuple-element.195) | copy-start | bytes 4804
  103.4 31.9 %copy-start.51 = (f32[1,400]{1,0:T(1,128)}, f32[1,400]{1,0:T(1,128)S(1)}, u32[]{:S(2)}) copy-start(f32[1,400]{1,0:T(1,128)S(1)} %get-tuple-element.196) | copy-start | bytes 4804
  103.4 31.9 %copy-start.53 = (f32[1,400]{1,0:T(1,128)}, f32[1,400]{1,0:T(1,128)S(1)}, u32[]{:S(2)}) copy-start(f32[1,400]{1,0:T(1,128)S(1)} %get-tuple-element.197) | copy-start | bytes 4804
  103.4 31.9 %copy-start.55 = (f32[1,400]{1,0:T(1,128)}, f32[1,400]{1,0:T(1,128)S(1)}, u32[]{:S(2)}) copy-start(f32[1,400]{1,0:T(1,128)S(1)} %get-tuple-element.198) | copy-start | bytes 4804
  135.3 4.8 copy-start.1
  135.4 6.1 copy-start.41
  143.4 158.9 %all-gather.3.cloned.1.call-start = ((), (), s32[]{:S(2)}) async-start(), calls=%async_computation.6 | async-start | bytes 5990400 | tf_op jit(solution)/shard_map/all_gather | solution.py:960
  143.9 9.7 copy-start.38
  143.9 10.7 copy-start.62
  154.5 245.6 %all-gather.5.cloned.1.call-start = ((), (), s32[]{:S(2)}) async-start(), calls=%async_computation.7 | async-start | bytes 7667712 | tf_op jit(solution)/shard_map/all_gather | solution.py:965
  159.3 112.3 %all-to-all-start.1 = ((bf16[8,200,400]{2,1,0:T(8,128)(2,1)}), bf16[8,200,400]{2,1,0:T(8,128)(2,1)}, u32[]{:S(2)}, u32[]{:S(2)}) async-start(bf16[8,200,400]{2,1,0:T(8,128)(2,1)} %get-tuple-element.158), calls=%async_computation.1 | async-start | bytes 3276800 | tf_op jit(solution)/shard_map/all_to_all | solution.py:931
  163.6 3.7 copy-start.34
  163.6 636.6 %all-reduce.22.cloned.1.call-start = ((), (), s32[]{:S(2)}) async-start(), calls=%async_computation.10 | async-start | bytes 13737984 | tf_op jit(solution)/shard_map/psum | solution.py:934
  202.0 4.1 copy-start.61
  212.8 5.6 copy-start.65
  295.7 3.9 copy-start.2
  344.1 3.5 copy-start.46
  381.5 10.0 copy-start.21
  487.1 2.6 copy-start.7
  487.2 3.0 copy-start.13
  526.1 9.4 copy-start.3
  526.1 9.4 copy-start.29
  535.6 10.8 copy-start.40
  598.4 8.6 copy-start.17
  607.0 134.8 %all-to-all-start.3 = ((bf16[8,200,512]{2,1,0:T(8,128)(2,1)}), bf16[8,200,512]{2,1,0:T(8,128)(2,1)S(1)}, u32[]{:S(2)}, u32[]{:S(2)}) async-start(bf16[8,200,512]{2,1,0:T(8,128)(2,1)} %bitcast.337), calls=%async_computation.3 | async-start | bytes 3276800 | tf_op jit(solution)/shard_map/all_to_all | solution.py:931
  719.0 3.5 copy-start.18
  722.5 12.1 copy-start.25
  727.7 6.9 copy-start.19
  729.5 112.3 %collective-permute-start = (bf16[200,1600]{1,0:T(8,128)(2,1)}, bf16[200,1600]{1,0:T(8,128)(2,1)}, u32[]{:S(2)}, u32[]{:S(2)}) collective-permute-start(bf16[200,1600]{1,0:T(8,128)(2,1)} %get-tuple-element.185), channel_id=1, source_target_pairs={{0,1},{1,2},{2,3},{3,4},{4,5},{5,6},{6,7},{8,9},{9,10},{10,11},{11... | collective-permute-start | bytes 1920008 | tf_op jit(solution)/shard_map/ppermute | solution.py:905
  732.7 109.2 %collective-permute-start.1 = (bf16[200,1600]{1,0:T(8,128)(2,1)}, bf16[200,1600]{1,0:T(8,128)(2,1)}, u32[]{:S(2)}, u32[]{:S(2)}) collective-permute-start(bf16[200,1600]{1,0:T(8,128)(2,1)} %get-tuple-element.186), channel_id=1, source_target_pairs={{3,5},{4,6},{5,7},{11,13},{12,14},{13,15},{19,21},{20,22},{21,23},... | collective-permute-start | bytes 1920008 | tf_op jit(solution)/shard_map/ppermute | solution.py:905
  741.8 96.2 %all-to-all-start.2 = ((bf16[8,200,400]{2,1,0:T(8,128)(2,1)}), bf16[8,200,400]{2,1,0:T(8,128)(2,1)}, u32[]{:S(2)}, u32[]{:S(2)}) async-start(bf16[8,200,400]{2,1,0:T(8,128)(2,1)} %bitcast.322), calls=%async_computation.2 | async-start | bytes 3276800 | tf_op jit(solution)/shard_map/all_to_all | solution.py:931
  747.4 264.9 %all-reduce.20.cloned.1.call-start = ((), (), s32[]{:S(2)}) async-start(), calls=%async_computation.9 | async-start | bytes 9113600 | tf_op jit(solution)/shard_map/psum | solution.py:934
  838.0 2.8 copy-start.26
  838.0 3.9 copy-start.20
  845.2 3.3 copy-start.31
  851.3 4.1 copy-start.44
  851.3 5.0 copy-start.15
  858.8 23.7 %copy-start.42 = (bf16[400,132]{0,1:T(8,128)(2,1)S(1)}, bf16[400,132]{0,1:T(8,128)(2,1)}, u32[]{:S(2)}) copy-start(bf16[400,132]{0,1:T(8,128)(2,1)} %param.28) | copy-start | bytes 316804
  890.1 4.5 copy-start.64
  894.6 8.0 copy-start.16
  906.1 4.5 copy-start.14
  906.1 203.6 %all-to-all-start.4 = ((bf16[8,200,400]{2,1,0:T(8,128)(2,1)}), bf16[8,200,400]{2,1,0:T(8,128)(2,1)}, u32[]{:S(2)}, u32[]{:S(2)}) async-start(bf16[8,200,400]{2,1,0:T(8,128)(2,1)} %bitcast.323), calls=%async_computation.4 | async-start | bytes 3276800 | tf_op jit(solution)/shard_map/all_to_all | solution.py:931
  910.5 281.8 %all-reduce.18.cloned.1.call-start = ((), (), s32[]{:S(2)}) async-start(), calls=%async_computation.8 | async-start | bytes 3760128 | tf_op jit(solution)/shard_map/psum | solution.py:934
  1012.3 9.5 copy-start.22
  1016.6 10.8 copy-start.27
  1032.2 43.5 %copy-start.5 = (f32[2,128,1600]{2,1,0:T(8,128)S(1)}, f32[2,128,1600]{2,1,0:T(8,128)}, u32[]{:S(2)}) copy-start(f32[2,128,1600]{2,1,0:T(8,128)} %copy-done.4) | copy-start | bytes 4915204
  1032.2 43.5 %copy-start.48 = (f32[1600]{0:T(1024)S(1)}, f32[1600]{0:T(1024)}, u32[]{:S(2)}) copy-start(f32[1600]{0:T(1024)} %param.33) | copy-start | bytes 19204
  1032.2 43.5 %copy-start.58 = (f32[256]{0:T(256)S(1)}, f32[256]{0:T(256)}, u32[]{:S(2)}) copy-start(f32[256]{0:T(256)} %copy-done.57) | copy-start | bytes 3076
  1100.1 3.9 copy-start.60
  1101.5 2.5 copy-start.28
  1104.0 3.3 copy-start.11
  1118.9 38.5 %copy-start.8 = (f32[256,1600]{1,0:T(8,128)S(1)}, f32[256,1600]{1,0:T(8,128)}, u32[]{:S(2)}) copy-start(f32[256,1600]{1,0:T(8,128)} %copy-done.6) | copy-start | bytes 4915204
  1157.5 34.9 %copy-start.23 = (bf16[8,200,400]{2,1,0:T(8,128)(2,1)S(1)}, bf16[8,200,400]{2,1,0:T(8,128)(2,1)}, u32[]{:S(2)}) copy-start(bf16[8,200,400]{2,1,0:T(8,128)(2,1)} %get-tuple-element.130) | copy-start | bytes 3840004
  1200.8 8.1 copy-start.43
  1200.8 8.8 copy-start.45
  (17 other events, 31.0 us)
Sparse Core Ops, SparseCore 0:
  143.5 62.7 all-reduce.15
  208.7 40.6 all-gather.2
  251.3 49.1 all-gather.4
  557.1 242.9 all-reduce.21
  845.3 166.9 all-reduce.19
  1112.6 79.6 all-reduce.17

commit v2 on v1

--- a/solution.py
+++ b/solution.py
@@ -55,9 +55,18 @@
     return own, tile
 
 
-def scan_fwd_kernel(pre_ref, mix_ref, bt_ref, c_ref, rate_ref, skip_ref, core_ref, start_ref,
-                    h_ref, dt_ref, u_ref, wide_ref, hs_ref):
-    length, cols = pre_ref.shape[2:]
+def turn_chunks(proj, bt_ref, ct_ref):
+    turned = jnp.swapaxes(proj[:, : 8 * NST], 0, 1)
+    for k in range(proj.shape[0] // CHUNK):
+        at = slice(k * CHUNK, (k + 1) * CHUNK)
+        bt_ref[k] = turned[:NST, at]
+        if ct_ref is not None:
+            ct_ref[k] = turned[NST : 2 * NST, at]
+
+
+def scan_fwd_kernel(proj_ref, mix_ref, rows_ref, wz_ref, wdt_ref, dtb_ref, rate_ref, skip_ref,
+                    core_ref, z_ref, sq_ref, start_ref, h_ref, dt_ref, u_ref, wide_ref, hs_ref, bt_ref):
+    length, cols = mix_ref.shape[2:]
     own, tile = chunk_masks()
 
     @pl.when(pl.program_id(1) == 0)
@@ -67,7 +76,10 @@
         wide_ref[:, :cols] = rate_ref[...] * LOG2E
 
     start_ref[0, 0] = h_ref[:, :cols]
-    dt = jax.nn.softplus(pre_ref[0, 0])
+    proj = proj_ref[0, 0]
+    turn_chunks(proj, bt_ref, None)
+    pre = dot(proj[:, 2 * NST :].astype(BF), wdt_ref[...]) + dtb_ref[...]
+    dt = jax.nn.softplus(pre)
     dt_ref[:, :cols] = dt
     u_ref[:, :cols] = dt * mix_ref[0, 0]
     rate = wide_ref[...]
@@ -75,7 +87,7 @@
 
     def chunk(k, h):
         base = pl.multiple_of(k * CHUNK, CHUNK)
-        bt = bt_ref[0, 0, k]
+        bt = bt_ref[k]
         for t in range(CHUNK):
             a = jnp.exp2(dt_ref[pl.ds(base + t, 1), :] * rate)
             h = a * h + bt[:, t : t + 1] * u_ref[pl.ds(base + t, 1), :]
@@ -83,44 +95,47 @@
         return h
 
     h_ref[...] = lax.fori_loop(0, length // CHUNK, chunk, h_ref[...])
-    crep = dot(c_ref[0, 0].astype(BF), tile)
+    z = dot(rows_ref[0, 0], wz_ref[...])
+    z_ref[0, 0] = z
+    crep = dot(proj[:, NST : 2 * NST].astype(BF), tile)
     for k in range(length // CHUNK):
         at = slice(k * CHUNK, (k + 1) * CHUNK)
         cb = (crep[at] * own).astype(BF)
-        core_ref[0, 0, at, :] = dot(cb, hs_ref[k * spread : (k + 1) * spread])[:, :cols] + skip_ref[...] * mix_ref[0, 0, at, :]
-
-def scan_forward(pre, mix, bt, c, rate, skip):
-    n, seqs, length, cols = pre.shape
+        core_ref[0, 0, at, :] = (
+            dot(cb, hs_ref[k * spread : (k + 1) * spread])[:, :cols] + skip_ref[...] * mix_ref[0, 0, at, :]
+        )
+    gated = core_ref[0, 0] * (z * jax.nn.sigmoid(z))
+    sq_ref[0, 0] = jnp.sum(gated * gated, axis=1, keepdims=True)
+
+
+def scan_forward(proj, mix, rows, wz, wdt, dtb, rate, skip):
+    n, seqs, length, cols = mix.shape
     wide = -(-cols // 128) * 128
     big = lambda w: pl.BlockSpec((1, 1, length, w), lambda s, i: (i, s, 0, 0))
-    whole = lambda r: pl.BlockSpec((r, cols), lambda s, i: (0, 0))
+    whole = lambda a: pl.BlockSpec(a.shape, lambda s, i: (0, 0))
+    shape = lambda w: jax.ShapeDtypeStruct((n, seqs, length, w), F32)
     return pl.pallas_call(
         scan_fwd_kernel,
         grid=(seqs, n),
-        in_specs=[
-            big(cols), big(cols),
-            pl.BlockSpec((1, 1) + bt.shape[2:], lambda s, i: (i, s, 0, 0, 0)),
-            big(NST), whole(NST), whole(1),
-        ],
-        out_specs=[big(cols), pl.BlockSpec((1, 1, NST, cols), lambda s, i: (i, s, 0, 0))],
-        out_shape=[
-            jax.ShapeDtypeStruct(pre.shape, F32),
-            jax.ShapeDtypeStruct((n, seqs, NST, cols), F32),
-        ],
+        in_specs=[big(proj.shape[3]), big(cols), big(rows.shape[3])] + [whole(a) for a in (wz, wdt, dtb, rate, skip)],
+        out_specs=[big(cols), big(cols), big(1), pl.BlockSpec((1, 1, NST, cols), lambda s, i: (i, s, 0, 0))],
+        out_shape=[shape(cols), shape(cols), shape(1), jax.ShapeDtypeStruct((n, seqs, NST, cols), F32)],
         scratch_shapes=[
             pltpu.VMEM((NST, wide), F32),
             pltpu.VMEM((length, wide), F32),
             pltpu.VMEM((length, wide), F32),
             pltpu.VMEM((NST, wide), F32),
             pltpu.VMEM((NST * length, wide), BF),
+            pltpu.VMEM((length // CHUNK, NST, CHUNK), F32),
         ],
         compiler_params=pltpu.CompilerParams(vmem_limit_bytes=GIANT),
-    )(pre, mix, bt, c, rate, skip)
-
-def scan_bwd_kernel(pre_ref, mix_ref, gin_ref, start_ref, bt_ref, ct_ref, b_ref, rate_ref, skip_ref,
-                    gpre_ref, gmix_ref, gb_ref, gc_ref, grate_ref, gskip_ref,
-                    carry_ref, dt_ref, u_ref, gy_ref, wide_ref, hs_ref, gs_ref, q_ref):
-    length, cols = pre_ref.shape[2:]
+    )(proj, mix, rows, wz, wdt, dtb, rate, skip)
+
+
+def scan_bwd_kernel(proj_ref, mix_ref, d_ref, core_ref, z_ref, stat_ref, start_ref, wdt_ref, dtb_ref, rate_ref, skip_ref,
+                    gain_ref, gpre_ref, gmix_ref, gz_ref, gb_ref, gc_ref, grate_ref, sums_ref,
+                    carry_ref, dt_ref, u_ref, gy_ref, wide_ref, hs_ref, gs_ref, q_ref, bt_ref, ct_ref):
+    length, cols = mix_ref.shape[2:]
     own, tile = chunk_masks()
     spread = NST * CHUNK
     half = NST // 2
@@ -134,23 +149,33 @@
     @pl.when((pl.program_id(1) == 0) & (pl.program_id(0) == 0))
     def _():
         grate_ref[...] = jnp.zeros_like(grate_ref)
-        gskip_ref[...] = jnp.zeros_like(gskip_ref)
+        sums_ref[...] = jnp.zeros_like(sums_ref)
         for ref in (dt_ref, u_ref, gy_ref, wide_ref):
             ref[...] = jnp.zeros_like(ref)
         wide_ref[0:NST, :cols] = rate_ref[...] * LOG2E
 
-    dt = jax.nn.softplus(pre_ref[0, 0])
+    scale, shift = stat_ref[0, 0][:, 2:3], stat_ref[0, 0][:, 3:4]
+    d, core, z = d_ref[0, 0], core_ref[0, 0], z_ref[0, 0]
+    logistic = jax.nn.sigmoid(z)
+    gated = core * (z * logistic)
+    grad_gated = scale * (d * gain_ref[...] - gated * shift)
+    gy_ref[:, :cols] = grad_gated * (z * logistic)
+    gz_ref[0, 0] = (grad_gated * core * (logistic * (1.0 + z * (1.0 - logistic)))).astype(BF)
+    sums_ref[0:1] += jnp.sum(d * gated * scale, axis=0, keepdims=True)
+    sums_ref[1:2] += jnp.sum(gy_ref[:, :cols] * mix_ref[0, 0], axis=0, keepdims=True)
+    proj = proj_ref[0, 0]
+    turn_chunks(proj, bt_ref, ct_ref)
+    pre = dot(proj[:, 2 * NST :].astype(BF), wdt_ref[...]) + dtb_ref[...]
+    dt = jax.nn.softplus(pre)
     dt_ref[:, :cols] = dt
     u_ref[:, :cols] = dt * mix_ref[0, 0]
-    gy_ref[:, :cols] = gin_ref[0, 0]
     wide_ref[NST:, :cols] = start_ref[0, 0]
-    gskip_ref[...] += jnp.sum(gin_ref[0, 0] * mix_ref[0, 0], axis=0, keepdims=True)
     rate = wide_ref[0:NST]
     hs_ref[0:NST] = wide_ref[NST:].astype(BF)
 
     def ahead(k, h):
         base = pl.multiple_of(k * CHUNK, CHUNK)
-        bt = bt_ref[0, 0, k]
+        bt = bt_ref[k]
         for t in range(CHUNK):
             a = jnp.exp2(dt_ref[pl.ds(base + t, 1), :] * rate)
             h = a * h + bt[:, t : t + 1] * u_ref[pl.ds(base + t, 1), :]
@@ -163,7 +188,7 @@
         carry, grate = state
         k = length // CHUNK - 1 - r
         base = pl.multiple_of(k * CHUNK, CHUNK)
-        ct = ct_ref[0, 0, k]
+        ct = ct_ref[k]
         qr_late = None
         for t in reversed(range(CHUNK)):
             at = pl.ds(pl.multiple_of((base + t) * NST, NST), NST)
@@ -188,7 +213,7 @@
     )
     carry_ref[...] = carry
     grate_ref[...] += grate[:, :cols]
-    brep = dot(b_ref[0, 0].astype(BF), tile)
+    brep = dot(proj[:, :NST].astype(BF), tile)
     gy_low = gy_ref[...].astype(BF)
     u_low = u_ref[...].astype(BF)
     gcs, gbs = [], []
@@ -197,11 +222,13 @@
         for k in (2 * pair, 2 * pair + 1):
             rows = slice(k * CHUNK, (k + 1) * CHUNK)
             deep = slice(k * spread, (k + 1) * spread)
-            mix, dt_now, gy = mix_ref[0, 0, rows, :], dt_ref[rows, :cols], gin_ref[0, 0, rows, :]
+            mix, dt_now, gy = mix_ref[0, 0, rows, :], dt_ref[rows, :cols], gy_ref[rows, :cols]
             gs = gs_ref[deep]
             gu = dot((brep[rows] * own).astype(BF), gs)[:, :cols]
             gdt = gdts[(k % 2) * CHUNK : (k % 2 + 1) * CHUNK, :cols] + gu * mix
-            gpre_ref[0, 0, rows, :] = gdt * jax.nn.sigmoid(pre_ref[0, 0, rows, :])
+            gpre = gdt * jax.nn.sigmoid(pre[rows])
+            gpre_ref[0, 0, rows, :] = gpre.astype(BF)
+            sums_ref[2:3] += jnp.sum(gpre, axis=0, keepdims=True)
             gmix_ref[0, 0, rows, :] = gu * dt_now + skip_ref[...] * gy
             hs = hs_ref[k * spread + NST : (k + 1) * spread + NST]
             gcs.append((ntdot(gy_low[rows], hs) * own).astype(BF))
@@ -209,26 +236,24 @@
     gc_ref[0, 0] = ntdot(jnp.concatenate(gcs, axis=0), tile)
     gb_ref[0, 0] = ntdot(jnp.concatenate(gbs, axis=0), tile)
 
-def scan_backward(pre, mix, gy, start, bt, ct, b, rate, skip):
-    n, seqs, length, cols = pre.shape
+def scan_backward(proj, mix, d, core, z, stats, start, wdt, dtb, rate, skip, gain):
+    n, seqs, length, cols = mix.shape
     wide = -(-cols // 128) * 128
     at = lambda s, i: (n - 1 - i, s, 0, 0)
     big = lambda w: pl.BlockSpec((1, 1, length, w), at)
-    whole = lambda r: pl.BlockSpec((r, cols), lambda s, i: (0, 0))
-    turned = pl.BlockSpec((1, 1) + bt.shape[2:], lambda s, i: (n - 1 - i, s, 0, 0, 0))
-    shape = lambda w: jax.ShapeDtypeStruct((n, seqs, length, w), F32)
+    whole = lambda a: pl.BlockSpec(a.shape, lambda s, i: (0, 0))
+    shape = lambda w, t: jax.ShapeDtypeStruct((n, seqs, length, w), t)
     return pl.pallas_call(
         scan_bwd_kernel,
         grid=(seqs, n),
-        in_specs=[
-            big(cols), big(cols), big(cols), pl.BlockSpec((1, 1, NST, cols), at),
-            turned, turned, big(NST), whole(NST), whole(1),
-        ],
-        out_specs=[big(cols), big(cols), big(NST), big(NST), whole(NST), whole(1)],
+        in_specs=[big(proj.shape[3]), big(cols), big(cols), big(cols), big(cols), big(stats.shape[3]),
+                  pl.BlockSpec((1, 1, NST, cols), at)] + [whole(a) for a in (wdt, dtb, rate, skip, gain)],
+        out_specs=[big(cols), big(cols), big(cols), big(NST), big(NST), whole(rate),
+                   pl.BlockSpec((8, cols), lambda s, i: (0, 0))],
         out_shape=[
-            shape(cols), shape(cols), shape(NST), shape(NST),
+            shape(cols, BF), shape(cols, F32), shape(cols, BF), shape(NST, F32), shape(NST, F32),
             jax.ShapeDtypeStruct((NST, cols), F32),
-            jax.ShapeDtypeStruct((1, cols), F32),
+            jax.ShapeDtypeStruct((8, cols), F32),
         ],
         scratch_shapes=[
             pltpu.VMEM((NST, wide), F32),
@@ -239,9 +264,11 @@
             pltpu.VMEM((length * NST + NST, wide), BF),
             pltpu.VMEM((length * NST, wide), BF),
             pltpu.VMEM((length * NST // 2, wide), BF),
+            pltpu.VMEM((length // CHUNK, NST, CHUNK), F32),
+            pltpu.VMEM((length // CHUNK, NST, CHUNK), F32),
         ],
         compiler_params=pltpu.CompilerParams(vmem_limit_bytes=GIANT),
-    )(pre, mix, gy, start, bt, ct, b, rate, skip)
+    )(proj, mix, d, core, z, stats, start, wdt, dtb, rate, skip, gain)
 
 
 def pick(ref, blocks, slots, slot):
@@ -259,11 +286,12 @@
     return jnp.where(lax.broadcasted_iota(jnp.int32, scores.shape, 1) <= bound, scores, NEGATIVE)
 
 
-def attn_fwd_kernel(slot_ref, len_ref, q_ref, k_ref, v_ref, out_ref, lse_ref):
+def attn_fwd_kernel(seq, slot_ref, len_ref, q_ref, k_ref, v_ref, *refs):
+    out_ref, lse_ref = refs[-2:]
     n, _, length, width = q_ref.shape
     heads, slots = width // HEAD, k_ref.shape[3] // HEAD
     group = 2
-    seq_length = len_ref[pl.program_id(0)]
+    seq_length = len_ref[seq]
     for i in range(n // group):
         at = slice(i * group, (i + 1) * group)
         for j in range(heads):
@@ -281,29 +309,40 @@
             lse_ref[at, 0, :, j : j + 1] = (top + jnp.log(total)).reshape(group, length, 1)
 
 
-def attn_forward(slot, lengths, q, k, v):
+def attn_forward(seq, slot, lengths, q, k, v, before=()):
     n, seqs, length, width = q.shape
-    big = lambda w: pl.BlockSpec((n, 1, length, w), lambda s: (0, s, 0, 0))
+    big = lambda w: pl.BlockSpec((n, 1, length, w), lambda s: (0, seq, 0, 0))
     smem = pl.BlockSpec(memory_space=pltpu.SMEM)
     return pl.pallas_call(
-        attn_fwd_kernel,
-        grid=(seqs,),
-        in_specs=[smem, smem, big(width), big(k.shape[3]), big(k.shape[3])],
+        functools.partial(attn_fwd_kernel, seq),
+        grid=(1,),
+        in_specs=[smem, smem, big(width), big(k.shape[3]), big(k.shape[3])]
+        + [pl.BlockSpec(memory_space=pl.ANY)] * len(before),
         out_specs=[big(width), big(width // HEAD)],
         out_shape=[
             jax.ShapeDtypeStruct(q.shape, F32),
             jax.ShapeDtypeStruct((n, seqs, length, width // HEAD), F32),
         ],
+        input_output_aliases={5: 0, 6: 1} if before else {},
         compiler_params=pltpu.CompilerParams(vmem_limit_bytes=GIANT),
-    )(slot, lengths, q, k, v)
-
-
-def attn_bwd_kernel(slot_ref, len_ref, q_ref, k_ref, v_ref, gh_ref, att_ref, lse_ref,
-                    gq_ref, gk_ref, gv_ref, gk_acc, gv_acc):
+    )(slot, lengths, q, k, v, *before)
+
+
+def attn_bwd_kernel(slot_ref, len_ref, q_ref, k_ref, v_ref, d_ref, att_ref, lse_ref, stat_ref, gain_ref,
+                    gq_ref, gk_ref, gv_ref, sums_ref, gk_acc, gv_acc, gh_ref):
     n, _, length, width = q_ref.shape
     heads, slots = width // HEAD, k_ref.shape[3] // HEAD
     group = 2
     seq_length = len_ref[pl.program_id(0)]
+    @pl.when(pl.program_id(0) == 0)
+    def _():
+        sums_ref[...] = jnp.zeros_like(sums_ref)
+
+    for i in range(n):
+        scale, shift = stat_ref[i, 0][:, 0:1], stat_ref[i, 0][:, 1:2]
+        d, attended = d_ref[i, 0], att_ref[i, 0]
+        gh_ref[i] = (scale * (d * gain_ref[...] - attended * shift)).astype(BF)
+        sums_ref[0:1] += jnp.sum(d * attended * scale, axis=0, keepdims=True)
     gk_acc[...] = jnp.zeros_like(gk_acc)
     gv_acc[...] = jnp.zeros_like(gv_acc)
     for i in range(n // group):
@@ -316,7 +355,7 @@
             queries = queries.astype(BF)
             keys = pick(k_ref, blocks, slots, slot)
             values = pick(v_ref, blocks, slots, slot)
-            grad = gh_ref[at, 0, :, lanes].reshape(group * length, HEAD)
+            grad = gh_ref[at, :, lanes].reshape(group * length, HEAD)
             attended = att_ref[at, 0, :, lanes].reshape(group * length, HEAD)
             delta = jnp.sum(grad.astype(F32) * attended, axis=1, keepdims=True)
             lse = lse_ref[at, 0, :, j : j + 1].reshape(group * length, 1)
@@ -334,20 +373,155 @@
         gv_ref[:, 0, :, lanes] = gv_acc[other].astype(BF).reshape(n, length, HEAD)
 
 
-def attn_backward(slot, lengths, q, k, v, gh, att, lse):
+def attn_backward(slot, lengths, q, k, v, d, att, lse, stats, gain):
     n, seqs, length, width = q.shape
     big = lambda w: pl.BlockSpec((n, 1, length, w), lambda s: (0, s, 0, 0))
+    whole = lambda r: pl.BlockSpec((r, width), lambda s: (0, 0))
     smem = pl.BlockSpec(memory_space=pltpu.SMEM)
     kw = k.shape[3]
     return pl.pallas_call(
         attn_bwd_kernel,
         grid=(seqs,),
-        in_specs=[smem, smem, big(width), big(kw), big(kw), big(width), big(width), big(width // HEAD)],
-        out_specs=[big(width), big(kw), big(kw)],
-        out_shape=[jax.ShapeDtypeStruct(x.shape, BF) for x in (q, k, v)],
-        scratch_shapes=[pltpu.VMEM((kw // HEAD, n * length, HEAD), F32)] * 2,
+        in_specs=[smem, smem, big(width), big(kw), big(kw), big(width), big(width), big(width // HEAD),
+                  big(stats.shape[3]), whole(1)],
+        out_specs=[big(width), big(kw), big(kw), whole(8)],
+        out_shape=[jax.ShapeDtypeStruct(x.shape, BF) for x in (q, k, v)]
+        + [jax.ShapeDtypeStruct((8, width), F32)],
+        scratch_shapes=[pltpu.VMEM((kw // HEAD, n * length, HEAD), F32)] * 2 + [pltpu.VMEM((n, length, width), BF)],
         compiler_params=pltpu.CompilerParams(vmem_limit_bytes=GIANT),
-    )(slot, lengths, q, k, v, gh, att, lse)
+    )(slot, lengths, q, k, v, d, att, lse, stats, gain)
+
+
+def signal_fwd_kernel(rows_ref, wx_ref, taps_ref, bias_ref, xp_ref, x_ref, pre_ref, mix_ref, low_ref, part_ref, xs_ref):
+    length = rows_ref.shape[2]
+
+    @pl.when(pl.program_id(1) == 0)
+    def _():
+        xs_ref[0:8] = jnp.zeros((8, xs_ref.shape[1]), F32)
+
+    x = dot(rows_ref[0, 0], wx_ref[...]).astype(BF)
+    x_ref[0, 0] = x
+    xs_ref[8:] = x.astype(F32)
+    first = 8 - (KCONV - 1)
+    pre = bias_ref[...]
+    for o in range(KCONV):
+        pre = pre + taps_ref[o : o + 1] * xs_ref[first + o : first + o + length]
+    xs_ref[0:8] = xs_ref[length : length + 8]
+    pre_ref[0, 0] = pre
+    mix = pre * jax.nn.sigmoid(pre)
+    mix_ref[0, 0] = mix
+    low_ref[0, 0] = mix.astype(BF)
+    part_ref[0, 0] = ntdot(mix.astype(BF), xp_ref[...])
+
+
+def signal_forward(rows, wx, taps, bias, xp):
+    n, seqs, length, width = rows.shape
+    cols = wx.shape[1]
+    big = lambda w: pl.BlockSpec((1, 1, length, w), lambda s, i: (i, s, 0, 0))
+    whole = lambda a: pl.BlockSpec(a.shape, lambda s, i: (0, 0))
+    shape = lambda w, t: jax.ShapeDtypeStruct((n, seqs, length, w), t)
+    return pl.pallas_call(
+        signal_fwd_kernel,
+        grid=(seqs, n),
+        in_specs=[big(width), whole(wx), whole(taps), whole(bias), whole(xp)],
+        out_specs=[big(cols)] * 4 + [big(xp.shape[0])],
+        out_shape=[shape(cols, BF), shape(cols, F32), shape(cols, F32), shape(cols, BF), shape(xp.shape[0], F32)],
+        scratch_shapes=[pltpu.VMEM((length + 8, cols), F32)],
+        compiler_params=pltpu.CompilerParams(vmem_limit_bytes=GIANT),
+    )(rows, wx, taps, bias, xp)
+
+
+def signal_bwd_kernel(gmix_ref, gproj_ref, xp_ref, pre_ref, x_ref, last_ref, taps_ref, gx_ref, sums_ref, gs_ref, xs_ref):
+    length = gmix_ref.shape[2]
+    edge = KCONV - 1
+    i = pl.program_id(1)
+
+    @pl.when((i == 0) & (pl.program_id(0) == 0))
+    def _():
+        sums_ref[...] = jnp.zeros_like(sums_ref)
+
+    @pl.when(i == 0)
+    def _():
+        gs_ref[length:] = jnp.zeros((8, gs_ref.shape[1]), F32)
+
+    grad = gmix_ref[0, 0] + dot(gproj_ref[0, 0], xp_ref[...])
+    grad = grad * silu_grad(pre_ref[0, 0])
+    gs_ref[:length] = grad
+    first_block = (i == pl.num_programs(1) - 1).astype(F32)
+    xs_ref[0:16] = last_ref[0, 0].astype(F32) * (1.0 - first_block)
+    xs_ref[16:] = x_ref[0, 0].astype(F32)
+    total = None
+    for o in range(KCONV):
+        term = taps_ref[o : o + 1] * gs_ref[edge - o : edge - o + length]
+        total = term if total is None else total + term
+        at = 16 - edge + o
+        sums_ref[o : o + 1] += jnp.sum(grad * xs_ref[at : at + length], axis=0, keepdims=True)
+    sums_ref[KCONV : KCONV + 1] += jnp.sum(grad, axis=0, keepdims=True)
+    gx_ref[0, 0] = total.astype(BF)
+    gs_ref[length:] = gs_ref[0:8]
+
+
+def signal_backward(gmix, gproj, xp, pre, x, taps):
+    n, seqs, length, cols = gmix.shape
+    at = lambda s, i: (n - 1 - i, s, 0, 0)
+    big = lambda w: pl.BlockSpec((1, 1, length, w), at)
+    whole = lambda a: pl.BlockSpec(a.shape, lambda s, i: (0, 0))
+    before = lambda s, i: (jnp.maximum(n - 2 - i, 0), s, length // 16 - 1, 0)
+    return pl.pallas_call(
+        signal_bwd_kernel,
+        grid=(seqs, n),
+        in_specs=[big(cols), big(xp.shape[0]), whole(xp), big(cols), big(cols),
+                  pl.BlockSpec((1, 1, 16, cols), before), whole(taps)],
+        out_specs=[big(cols), pl.BlockSpec((8, cols), lambda s, i: (0, 0))],
+        out_shape=[jax.ShapeDtypeStruct(gmix.shape, BF), jax.ShapeDtypeStruct((8, cols), F32)],
+        scratch_shapes=[pltpu.VMEM((length + 8, cols), F32), pltpu.VMEM((length + 16, cols), F32)],
+        compiler_params=pltpu.CompilerParams(vmem_limit_bytes=GIANT),
+    )(gmix, gproj, xp, pre, x, x, taps)
+
+
+def norm_kernel(sq_ref, att_ref, again_ref, core_ref, z_ref, sgain_ref, attn_ref, ssm_ref):
+    sq = sq_ref[0]
+    r_attn = lax.rsqrt(sq[:, 0:1] / (HEADS * HEAD) + EPSILON)
+    r_ssm = lax.rsqrt(sq[:, 1:2] / INNER + EPSILON)
+    attn_ref[0] = (att_ref[0] * r_attn * again_ref[...]).astype(BF)
+    z = z_ref[0]
+    ssm_ref[0] = (core_ref[0] * (z * jax.nn.sigmoid(z)) * r_ssm * sgain_ref[...]).astype(BF)
+
+
+def norm_both(squares, attended, attn_gain, core, z, ssm_gain):
+    n, rows, _ = squares.shape
+    block = lambda c: pl.BlockSpec((1, rows, c), lambda i: (i, 0, 0))
+    whole = lambda a: pl.BlockSpec(a.shape, lambda i: (0, 0))
+    aw, sw = attended.shape[2], core.shape[2]
+    return pl.pallas_call(
+        norm_kernel,
+        grid=(n,),
+        in_specs=[block(2), block(aw), whole(attn_gain), block(sw), block(sw), whole(ssm_gain)],
+        out_specs=[block(aw), block(sw)],
+        out_shape=[jax.ShapeDtypeStruct((n, rows, w), BF) for w in (aw, sw)],
+        compiler_params=pltpu.CompilerParams(vmem_limit_bytes=GIANT),
+    )(squares, attended, attn_gain, core, z, ssm_gain)
+
+
+def ffn_bwd_kernel(u_ref, down_ref, gate_ref, up_ref, ggate_ref, gup_ref):
+    grad = ntdot(u_ref[0], down_ref[...])
+    gate, up = gate_ref[0].astype(F32), up_ref[0].astype(F32)
+    logistic = jax.nn.sigmoid(gate)
+    ggate_ref[0] = (grad * up * (logistic * (1.0 + gate * (1.0 - logistic)))).astype(BF)
+    gup_ref[0] = (grad * (gate * logistic)).astype(BF)
+
+
+def ffn_backward(upstream, w_down, gate, up):
+    n, rows, hidden = gate.shape
+    block = lambda c: pl.BlockSpec((1, rows, c), lambda i: (i, 0, 0))
+    return pl.pallas_call(
+        ffn_bwd_kernel,
+        grid=(n,),
+        in_specs=[block(upstream.shape[2]), pl.BlockSpec(w_down.shape, lambda i: (0, 0)), block(hidden), block(hidden)],
+        out_specs=[block(hidden)] * 2,
+        out_shape=[jax.ShapeDtypeStruct(gate.shape, BF)] * 2,
+        compiler_params=pltpu.CompilerParams(vmem_limit_bytes=GIANT),
+    )(upstream, w_down, gate, up)
 
 
 def greet(peers, axis="seq"):
@@ -638,38 +812,58 @@
     )(p, after)
 
 
-def start_kernel(n, x_ref, w_ref, o_ref, c_ref, swap_sem, swap_send, swap_recv, *sems):
+def start_kernel(n, moves, x_ref, gain_ref, w_ref, in_ref, o_ref, c_ref, first_ref, second_ref,
+                 normed_ref, cols_ref, swap_sem, swap_send, swap_recv, *sems):
     me = lax.axis_index("seq")
     others = [(me + d) % n for d in range(1, n)]
-    greet(others)
-    own = pltpu.make_async_copy(w_ref.at[me], c_ref.at[me], swap_sem)
+    barrier = pltpu.get_barrier_semaphore()
+    for peer in others:
+        pl.semaphore_signal(barrier, inc=1, device_id={"seq": peer}, device_id_type=MESH)
+    x = x_ref[...].astype(F32)
+    scale = lax.rsqrt(jnp.mean(x * x, axis=-1, keepdims=True) + EPSILON)
+    normed_ref[...] = (x * scale * gain_ref[...]).astype(BF)
+    pl.semaphore_wait(barrier, n - 1)
+    gather_start, gather_end = (ag4_parts if n == 8 else ag_parts)(n, normed_ref, o_ref, *sems)
+    gather_start()
+    for i in range(n):
+        if sum(size for _, _, size in moves[i]) < cols_ref.shape[2]:
+            cols_ref[i] = jnp.zeros(cols_ref.shape[1:], BF)
+        for dst, src, size in moves[i]:
+            cols_ref[i, :, dst : dst + size] = w_ref[:, src : src + size]
+    own = pltpu.make_async_copy(cols_ref.at[me], c_ref.at[me], swap_sem)
     own.start()
-    gather_start, gather_end = (ag4_parts if n == 8 else ag_parts)(n, x_ref, o_ref, *sems)
-    gather_start()
     swaps = []
     for d in range(1, n):
-        c = send(w_ref.at[others[d - 1]], c_ref.at[me], swap_send.at[d - 1], swap_recv.at[d - 1], others[d - 1])
+        peer = others[d - 1]
+        c = send(cols_ref.at[peer], c_ref.at[me], swap_send.at[d - 1], swap_recv.at[d - 1], peer)
         c.start()
         swaps.append(c)
+    width = first_ref.shape[2]
+    for i in range(n):
+        first_ref[i] = in_ref[:, i * width : (i + 1) * width]
+        second_ref[i] = in_ref[:, (n + i) * width : (n + i + 1) * width]
     gather_end()
     own.wait()
     for c in swaps:
         c.wait()
 
 
-def gather_and_exchange(x, w, n, cid):
-    chips = n // 2
-    far, near = (6, 7) if n == 8 else (chips, chips)
+def gather_and_exchange(x, gain, w, moves, width, w_in, n, cid):
+    far, near = (6, 7) if n == 8 else (n // 2, n // 2)
     anywhere = pl.BlockSpec(memory_space=pl.ANY)
+    vmem = pl.BlockSpec(memory_space=pltpu.VMEM)
     dma = pltpu.SemaphoreType.DMA
+    cols = jax.ShapeDtypeStruct((n, w.shape[0], width), BF)
+    part = jax.ShapeDtypeStruct((n, w_in.shape[0], w_in.shape[1] // (2 * n)), BF)
     return pl.pallas_call(
-        functools.partial(start_kernel, n),
-        out_shape=[jax.ShapeDtypeStruct((n,) + x.shape, x.dtype), jax.ShapeDtypeStruct(w.shape, w.dtype)],
-        in_specs=[anywhere] * 2,
-        out_specs=[anywhere] * 2,
-        scratch_shapes=[dma, dma((n - 1,)), dma((n - 1,)), dma, dma((far,)), dma((far,)), dma((near,)), dma((near,))],
-        compiler_params=pltpu.CompilerParams(collective_id=cid, has_side_effects=True),
-    )(x, w)
+        functools.partial(start_kernel, n, moves),
+        out_shape=[jax.ShapeDtypeStruct((n,) + x.shape, BF), cols, part, part],
+        in_specs=[vmem] * 4,
+        out_specs=[anywhere] * 2 + [vmem] * 2,
+        scratch_shapes=[pltpu.VMEM(x.shape, BF), pltpu.VMEM(cols.shape, BF), dma, dma((n - 1,)), dma((n - 1,)),
+                        dma, dma((far,)), dma((far,)), dma((near,)), dma((near,))],
+        compiler_params=pltpu.CompilerParams(collective_id=cid, has_side_effects=True, vmem_limit_bytes=GIANT),
+    )(x, gain[None], w, w_in)
 
 
 def all_gather(x, n, cid):
@@ -819,6 +1013,246 @@
     )(*(a.reshape(n, rows, a.shape[1]) for a, _, _ in pairs), *(b for _, b, _ in pairs), after)
 
 
+def chain_kernel(axis, count, cuts, *refs):
+    arrays = len(cuts)
+    x_refs, after_ref, o_refs = refs[:arrays], refs[arrays], refs[arrays + 1 : 2 * arrays + 1]
+    rest = refs[2 * arrays + 1 :]
+    up_in, up_out, down_in, down_out = (rest[k * arrays : (k + 1) * arrays] for k in range(4))
+    up_send, up_recv, down_send, down_recv = rest[4 * arrays :]
+    me = lax.axis_index(axis)
+    first, last = me == 0, me == count - 1
+    above, below = (me + 1) % count, (me + count - 1) % count
+    barrier = pltpu.get_barrier_semaphore()
+
+    @pl.when(me > 0)
+    def _():
+        pl.semaphore_signal(barrier, inc=1, device_id={axis: below}, device_id_type=MESH)
+
+    @pl.when(me < count - 1)
+    def _():
+        pl.semaphore_signal(barrier, inc=1, device_id={axis: above}, device_id_type=MESH)
+
+    @pl.when((me > 0) & (me < count - 1))
+    def _():
+        pl.semaphore_wait(barrier, 2)
+
+    @pl.when(first | last)
+    def _():
+        pl.semaphore_wait(barrier, 1)
+
+    pieces = [(k, c) for k in range(arrays) for c in range(cuts[k])]
+    lane = lambda k: x_refs[k].shape[1] // cuts[k]
+    at = lambda k, c: slice(c * lane(k), (c + 1) * lane(k))
+
+    def up(s, k, c):
+        return send(up_out[k].at[c], up_in[k].at[c], up_send.at[s], up_recv.at[s], above, axis)
+
+    def down(s, k, c):
+        return send(down_out[k].at[c], down_in[k].at[c], down_send.at[s], down_recv.at[s], below, axis)
+
+    for s, (k, c) in enumerate(pieces):
+        own = x_refs[k][:, at(k, c)]
+
+        @pl.when(first)
+        def _():
+            up_out[k][c] = own
+            up(s, k, c).start()
+
+        @pl.when(last)
+        def _():
+            down_out[k][c] = own
+            down(s, k, c).start()
+
+    own = lambda s: x_refs[pieces[s][0]][:, at(*pieces[s])].astype(F32)
+
+    def serve_up(s):
+        k, c = pieces[s]
+
+        @pl.when(me > 0)
+        def _():
+            up(s, k, c).wait_recv()
+
+            @pl.when(me < count - 1)
+            def _():
+                up_out[k][c] = (own(s) + up_in[k][c].astype(F32)).astype(BF)
+                up(s, k, c).start()
+
+    def serve_down(s):
+        k, c = pieces[s]
+
+        @pl.when(me < count - 1)
+        def _():
+            down(s, k, c).wait_recv()
+
+            @pl.when(me > 0)
+            def _():
+                down_out[k][c] = (own(s) + down_in[k][c].astype(F32)).astype(BF)
+                down(s, k, c).start()
+
+    def finish(s):
+        k, c = pieces[s]
+        put = lambda value: o_refs[k].__setitem__((slice(None), at(k, c)), value)
+
+        @pl.when(first)
+        def _():
+            put(own(s) + down_in[k][c].astype(F32))
+
+        @pl.when(last)
+        def _():
+            put(own(s) + up_in[k][c].astype(F32))
+
+        @pl.when((me > 0) & (me < count - 1))
+        def _():
+            put(own(s) + up_in[k][c].astype(F32) + down_in[k][c].astype(F32))
+
+    for s in range(len(pieces) + 1):
+        for side, early, late in ((me * 2 < count, serve_up, serve_down), (me * 2 >= count, serve_down, serve_up)):
+            @pl.when(side)
+            def _():
+                if s < len(pieces):
+                    early(s)
+                if s:
+                    late(s - 1)
+
+        if s:
+            finish(s - 1)
+
+    for s, (k, c) in enumerate(pieces):
+        @pl.when(me < count - 1)
+        def _():
+            up(s, k, c).wait_send()
+
+        @pl.when(me > 0)
+        def _():
+            down(s, k, c).wait_send()
+
+
+def chain_sum(arrays, cuts, count, cid, after, axis="dp"):
+    vmem = pl.BlockSpec(memory_space=pltpu.VMEM)
+    total = sum(cuts)
+    slots = [pltpu.VMEM((c, a.shape[0], a.shape[1] // c), BF) for a, c in zip(arrays, cuts)]
+    return pl.pallas_call(
+        functools.partial(chain_kernel, axis, count, tuple(cuts)),
+        out_shape=[jax.ShapeDtypeStruct(a.shape, F32) for a in arrays],
+        in_specs=[vmem] * len(arrays) + [pl.BlockSpec(memory_space=pl.ANY)],
+        out_specs=[vmem] * len(arrays),
+        scratch_shapes=slots * 4 + [pltpu.SemaphoreType.DMA((total,))] * 4,
+        compiler_params=pltpu.CompilerParams(collective_id=cid, has_side_effects=True, vmem_limit_bytes=GIANT),
+    )(*arrays, after)
+
+
+def gather_product4_kernel(body, weights, aligned, x_ref, *refs):
+    w_refs, refs = refs[:weights], refs[weights:]
+    row_refs, o_ref = refs[:aligned], refs[aligned]
+    results, (mine_sem, far_send, far_recv, near_send, near_recv) = refs[aligned + 1 : -5], refs[-5:]
+    me = lax.axis_index("seq")
+    core, (sib, east, north, across) = square(me)
+    x, y = (me // 2) % 2, me // 4
+    greet([sib, east, north])
+    half = x_ref.shape[0] // 2
+    cut = (pl.ds(0, half), pl.ds(half, half))
+    hops = (
+        (me, 0, east), (me, 1, east), (me, 1, north), (me, 0, north), (east, 0, north), (north, 1, east)
+    )
+    handed = ((east, 0), (east, 1), (north, 1), (north, 0), (across, 0), (across, 1))
+
+    def far(slot):
+        block, h, peer = hops[slot]
+        ref = o_ref.at[block, cut[h]]
+        return send(x_ref.at[cut[h]] if slot < 4 else ref, ref, far_send.at[slot], far_recv.at[slot], peer)
+
+    def near(slot):
+        if slot == 6:
+            return send(x_ref, o_ref.at[me], near_send.at[6], near_recv.at[6], sib)
+        block, h = handed[slot]
+        ref = o_ref.at[block, cut[h]]
+        return send(ref, ref, near_send.at[slot], near_recv.at[slot], sib)
+
+    mine = pltpu.make_async_copy(x_ref, o_ref.at[me], mine_sem)
+    mine.start()
+    for slot in (0, 2, 1, 3):
+        far(slot).start()
+    near(6).start()
+
+    def arrive(slot, relay=None):
+        far(slot).wait_recv()
+        if relay is not None:
+            far(relay).start()
+        near(slot).start()
+
+    def step(s, _):
+        @pl.when(s == 0)
+        def _():
+            mine.wait()
+
+        @pl.when(s == 1)
+        def _():
+            near(6).wait_recv()
+
+        @pl.when(s == 2)
+        def _():
+            arrive(0, 4)
+            arrive(2, 5)
+            arrive(1)
+
+        @pl.when(s == 3)
+        def _():
+            near(0).wait_recv()
+            near(1).wait_recv()
+
+        @pl.when(s == 4)
+        def _():
+            arrive(3)
+
+        @pl.when(s == 5)
+        def _():
+            near(2).wait_recv()
+            near(3).wait_recv()
+
+        @pl.when(s == 6)
+        def _():
+            arrive(4)
+            arrive(5)
+
+        @pl.when(s == 7)
+        def _():
+            near(4).wait_recv()
+            near(5).wait_recv()
+
+        pair = s // 2
+        seat = (((y + pair // 2) % 2) * 2 + (x + pair % 2) % 2) * 2 + (core + s) % 2
+        for ref, value in zip(results, body(o_ref[seat], *w_refs, *(ref[seat] for ref in row_refs))):
+            ref[seat] = value.astype(ref.dtype)
+        return 0
+
+    lax.fori_loop(0, 8, step, 0)
+    for slot in range(7):
+        near(slot).wait_send()
+    for slot in range(6):
+        far(slot).wait_send()
+
+
+def gather_product(body, x, weights, outs, n, cid, by_rows=()):
+    rows = x.shape[0]
+    if n != 8:
+        whole = all_gather(x, n, cid)
+        values = body(
+            whole.reshape(n * rows, -1), *weights, *(a.reshape(n * rows, a.shape[2]) for a in by_rows)
+        )
+        return [whole] + [v.astype(t).reshape(n, rows, -1) for v, (_, t) in zip(values, outs)]
+    vmem = pl.BlockSpec(memory_space=pltpu.VMEM)
+    dma = pltpu.SemaphoreType.DMA
+    return pl.pallas_call(
+        functools.partial(gather_product4_kernel, body, len(weights), len(by_rows)),
+        out_shape=[jax.ShapeDtypeStruct((n,) + x.shape, x.dtype)]
+        + [jax.ShapeDtypeStruct((n, rows, c), t) for c, t in outs],
+        in_specs=[vmem] * (1 + len(weights) + len(by_rows)),
+        out_specs=[vmem] * (1 + len(outs)),
+        scratch_shapes=[dma, dma((6,)), dma((6,)), dma((7,)), dma((7,))],
+        compiler_params=pltpu.CompilerParams(collective_id=cid, has_side_effects=True, vmem_limit_bytes=GIANT),
+    )(x, *weights, *by_rows)
+
+
 class HeadPlan:
     def __init__(self, n):
         self.n = n
@@ -851,23 +1285,18 @@
         heads = range(i * self.per, min((i + 1) * self.per, HEADS))
         return sorted({h // group for h in heads})
 
-    def split_columns(self, w):
-        rows = w.shape[0]
-        q = jnp.pad(w[:, : HEADS * HEAD], ((0, 0), (0, self.n * self.width - HEADS * HEAD)))
-        parts = []
+    def moves(self):
+        lists = []
         for i in range(self.n):
-            pieces = [q[:, i * self.width : (i + 1) * self.width]]
+            first = i * self.width
+            mine = [(0, first, min(self.width, HEADS * HEAD - first))] if first < HEADS * HEAD else []
             for kind in range(2):
                 start = HEADS * HEAD + kind * KVH * HEAD
-                used = self.kv_used(i)
-                for slot in range(self.slots):
-                    g = self.first_kv[i] + slot
-                    if g in used:
-                        pieces.append(w[:, start + g * HEAD : start + (g + 1) * HEAD])
-                    else:
-                        pieces.append(jnp.zeros((rows, HEAD), w.dtype))
-            parts.append(jnp.concatenate(pieces, axis=1))
-        return jnp.stack(parts)
+                for g in self.kv_used(i):
+                    slot = g - self.first_kv[i]
+                    mine.append((self.width + kind * self.kv_width + slot * HEAD, start + g * HEAD, HEAD))
+            lists.append(tuple(mine))
+        return tuple(lists)
 
     def join_columns(self, g):
         q = [g[i, :, : self.width] for i in range(self.n)]
@@ -928,10 +1357,17 @@
         v.astype(BF).reshape(n, local, v.shape[-1]), n, cid, after
     )
     later = lambda g, zero: g + zero.astype(g.dtype)
+    nothing = lambda *sums: 0.0 * sum(g.reshape(-1)[0].astype(F32) for g in sums)
+    mark = lambda zero: jnp.full((8, 128), zero)
     exchange = lambda v: lax.all_to_all(v, "seq", 0, 0, tiled=True)
     blocks = lambda v: v.reshape(n, seqs, slot_len, v.shape[-1])
     mine = lambda v: lax.dynamic_slice_in_dim(v, me * cols, cols, v.ndim - 1)
     over = lambda g: lax.psum(g, "dp")
+
+    def one_step(work):
+        shapes = jax.eval_shape(work, 0)
+        none = lambda _: jax.tree.map(lambda t: jnp.zeros(t.shape, t.dtype), shapes)
+        return lax.cond(lengths[0] > 0, work, none, 0)
 
     def row_sums(a, b, cid):
         both = jnp.stack([a, b]).reshape(-1, 128)
@@ -947,15 +1383,12 @@
 
     x = tokens.astype(F32).reshape(local, width)
     scale_in = lax.rsqrt(jnp.mean(x * x, axis=-1, keepdims=True) + EPSILON)
-    normed, qkv_cols = gather_and_exchange(
-        (x * scale_in * norm_in).astype(BF), plan.split_columns(w_qkv), n, 1
+    normed, qkv_cols, in_x, in_z = gather_and_exchange(
+        tokens.reshape(local, width), norm_in, w_qkv, plan.moves(), plan.width + 2 * plan.kv_width, w_in, n, 1
     )
     normed, qkv_cols = flat(normed), qkv_cols.reshape(n * w_rows, -1)
     qkv = dot(normed, qkv_cols).astype(BF)
-    behind = 0.0 * normed[0, 0].astype(F32)
-    in_parts = later(jnp.transpose(w_in.reshape(w_rows, 2, n, cols), (1, 2, 0, 3)), behind)
-    wx = exchange(in_parts[0]).reshape(n * w_rows, cols)
-    wz = exchange(in_parts[1]).reshape(n * w_rows, cols)
+    wx, wz = exchange(in_x), exchange(in_z)
     behind = 0.0 * qkv[0, 0].astype(F32)
     ao_all = lax.all_gather(later(w_ao, behind), "seq", axis=0, tiled=True)
     ao_mine = lax.dynamic_slice_in_dim(
@@ -966,119 +1399,137 @@
     q = blocks(qkv[:, : plan.width])
     k = blocks(qkv[:, plan.width : plan.width + plan.kv_width])
     v = blocks(qkv[:, plan.width + plan.kv_width :])
-    attended, lse = attn_forward(table, lengths, q, k, v)
-    attended_rows = flat(attended)
-
-    x_conv = blocks(dot(normed, wx).astype(BF))
-    z_gate = dot(normed, wz)
-    edge = KCONV - 1
-    before = jnp.concatenate(
-        [jnp.zeros((1, seqs, edge, cols), BF), x_conv[:-1, :, slot_len - edge :]], axis=0
+    attended, lse = attn_forward(0, table, lengths, q, k, v)
+    for seq in range(1, seqs):
+        attended, lse = attn_forward(seq, table, lengths, q, k, v, (attended, lse))
+    wx = later(wx, nothing(lse)).reshape(n * w_rows, cols)
+    wz = wz.reshape(n * w_rows, cols)
+    xp = jnp.swapaxes(w_xp, 0, 1)
+    xp = jnp.concatenate([xp[DTR:], xp[:DTR]], axis=0)
+    x_conv, conv_pre, mixer_in, mixer_low, projected = signal_forward(blocks(normed), wx, taps, bias[None], xp)
+    mixer_low = flat(mixer_low)
+    projected = blocks(gather(scatter(flat(projected), 15).astype(BF), 16)).astype(F32)
+    core, z_gate, ssm_sq, start = scan_forward(
+        projected, mixer_in, blocks(normed), wz, wdt, dtb[None], rate, skip[None]
     )
-    padded = jnp.concatenate([before, x_conv], axis=2).astype(F32)
-    conv_pre = bias + sum(taps[o] * padded[:, :, o : o + slot_len] for o in range(KCONV))
-    mixer_in = jax.nn.silu(conv_pre)
-    mixer_low = flat(mixer_in).astype(BF)
-    projected = lax.psum(dot(mixer_low, w_xp), "seq")
-    step_low = projected[:, :DTR].astype(BF)
-    b_input, c_output = projected[:, DTR : DTR + NST], projected[:, DTR + NST :]
-    step_pre = blocks(dot(step_low, wdt) + dtb)
-    turn = lambda m: jnp.swapaxes(m.reshape(n, seqs, slot_len // CHUNK, CHUNK, NST), 3, 4)
-    bt, ct = turn(b_input), turn(c_output)
-    core, start = scan_forward(step_pre, mixer_in, bt, blocks(c_output), rate, skip[None])
-    core = flat(core)
-    gated = core * jax.nn.silu(z_gate)
-    squares = row_sums(
-        jnp.sum(attended_rows * attended_rows, axis=1), jnp.sum(gated * gated, axis=1), 2
-    )
-    r_attn = lax.rsqrt(squares[0] / (HEADS * HEAD) + EPSILON)[:, None]
-    r_ssm = lax.rsqrt(squares[1] / INNER + EPSILON)[:, None]
-    attn_low = (attended_rows * r_attn * attn_gain).astype(BF)
-    ssm_low = (gated * r_ssm * ssm_gain).astype(BF)
+    by_device = lambda m: m.reshape(n, local, m.shape[-1])
+    squares = row_sums(jnp.sum(attended * attended, axis=3).reshape(rows), ssm_sq.reshape(rows), 2)
+    r_attn = lax.rsqrt(squares[0] / (HEADS * HEAD) + EPSILON)
+    r_ssm = lax.rsqrt(squares[1] / INNER + EPSILON)
+    attn_low, ssm_low = map(flat, norm_both(
+        by_device(squares.T), by_device(attended), attn_gain[None], by_device(core), by_device(z_gate), ssm_gain[None]
+    ))
     mixed = product_scatter(((attn_low, ao_mine, False), (ssm_low, w_so, False)), n, 3)
     residual = x + 0.5 * mixed
     r_ffn = lax.rsqrt(jnp.mean(residual * residual, axis=-1, keepdims=True) + EPSILON)
-    normed_two = gather((residual * r_ffn * norm_ffn).astype(BF), 4)
-    w_gate, w_up = w_gu[:, 0], w_gu[:, 1]
-    gate, up = dot(normed_two, w_gate), dot(normed_two, w_up)
-    activated = (jax.nn.silu(gate) * up).astype(BF)
-
-    grad_act = ntdot(upstream_all, w_down)
-    grad_gate = (grad_act * up * silu_grad(gate)).astype(BF)
-    grad_up = (grad_act * jax.nn.silu(gate)).astype(BF)
+    turned = jnp.transpose(w_gu, (1, 2, 0))
+    w_gate, w_up = turned[0], turned[1]
+    hidden = w_gate.shape[0]
+
+    def gated_units(rows_in, gate_ref, up_ref):
+        gate, up = ntdot(rows_in, gate_ref[...]), ntdot(rows_in, up_ref[...])
+        return gate, up, jax.nn.silu(gate) * up
+
+    normed_two, gate, up, activated = gather_product(
+        gated_units, (residual * r_ffn * norm_ffn).astype(BF), (w_gate, w_up), ((hidden, BF),) * 3, n, 4
+    )
+    normed_two, activated = flat(normed_two), flat(activated)
+
+    grad_gate, grad_up = map(flat, ffn_backward(by_device(upstream_all), w_down, gate, up))
     g_down = tndot(activated, upstream_all).astype(BF)
-    g_gate, g_up = tndot(normed_two, grad_gate).astype(BF), tndot(normed_two, grad_up).astype(BF)
+    g_gate, g_up = tndot(grad_gate, normed_two).astype(BF), tndot(grad_up, normed_two).astype(BF)
+    g_down, g_gate, g_up = tie((g_down, g_gate, g_up))
     s_down, s_gate, s_up = over((g_down, g_gate, g_up))
-    grad_two = product_scatter(((grad_gate, w_gate, True), (grad_up, w_up, True)), n, 5)
+    grad_two = product_scatter(
+        ((grad_gate, w_gate, False), (grad_up, w_up, False)), n, 5, mark(nothing(g_gate, g_up))
+    )
+
     def norm_pull(grad, values, r, gain):
         dotted = jnp.mean(grad * gain * values, axis=-1, keepdims=True)
         return r * (grad * gain - values * (r * r * dotted)), jnp.sum(grad * values * r, axis=0)
 
     add, g_norm_ffn = norm_pull(grad_two, residual, r_ffn, norm_ffn)
     grad_residual = upstream + add
-    mix_low = gather(grad_residual.astype(BF), 7)
-    d_attn = 0.5 * ntdot(mix_low, ao_mine)
-    d_ssm = 0.5 * ntdot(mix_low, w_so)
-    inner = row_sums(
-        jnp.sum(d_attn * attn_gain * attended_rows, axis=1),
-        jnp.sum(d_ssm * ssm_gain * gated, axis=1),
-        8,
+
+    def heads_and_channels(rows_in, ao_ref, so_ref, head_gain, channel_gain, heads_out, core_out, gate_out):
+        of_heads = 0.5 * ntdot(rows_in, ao_ref[...])
+        of_channels = 0.5 * ntdot(rows_in, so_ref[...])
+        gated = core_out * (gate_out * jax.nn.sigmoid(gate_out))
+        sums = [
+            jnp.sum(of_heads * head_gain[...] * heads_out, axis=1, keepdims=True),
+            jnp.sum(of_channels * channel_gain[...] * gated, axis=1, keepdims=True),
+        ]
+        return of_heads, of_channels, jnp.concatenate(sums, axis=1)
+
+    mix_low, d_attn, d_ssm, inner = gather_product(
+        heads_and_channels, grad_residual.astype(BF), (ao_mine, w_so, attn_gain[None], ssm_gain[None]),
+        ((plan.width, F32), (cols, F32), (2, F32)), n, 7, (by_device(attended), by_device(core), by_device(z_gate)),
     )
-    t_attn = (inner[0] / (HEADS * HEAD))[:, None] * r_attn * r_attn
-    t_ssm = (inner[1] / INNER)[:, None] * r_ssm * r_ssm
-    grad_heads = (r_attn * (d_attn * attn_gain - attended_rows * t_attn)).astype(BF)
-    grad_gated = r_ssm * (d_ssm * ssm_gain - gated * t_ssm)
-    g_norm_attn = jnp.sum(d_attn * attended_rows * r_attn, axis=0)
-    g_norm_ssm = jnp.sum(d_ssm * gated * r_ssm, axis=0)
-
-    gq, gk, gv = attn_backward(table, lengths, q, k, v, blocks(grad_heads), attended, lse)
-    grad_qkv = flat(jnp.concatenate([gq, gk, gv], axis=3))
-    grad_core = grad_gated * jax.nn.silu(z_gate)
-    grad_z = (grad_gated * core * silu_grad(z_gate)).astype(BF)
-    g_ao = reblock((0.5 * tndot(attn_low, mix_low)).astype(BF), plan.width, ao_rows, HEADS * HEAD)
-    g_so = (0.5 * tndot(ssm_low, mix_low)).astype(BF)
-    g_z = exchange(tndot(normed, grad_z).astype(BF).reshape(n, w_rows, cols))
-    g_qkv = exchange(tndot(normed, grad_qkv).astype(BF).reshape(n, w_rows, -1))
+    mix_low, inner = flat(mix_low), inner.reshape(rows, 2)
+    inner = row_sums(inner[:, 0], inner[:, 1], 8)
+    stats = blocks(jnp.stack([
+        r_attn, inner[0] / (HEADS * HEAD) * r_attn * r_attn, r_ssm, inner[1] / INNER * r_ssm * r_ssm
+    ], axis=1))
+
+    def mixers_back(_):
+        gq, gk, gv, head_sums = attn_backward(
+            table, lengths, q, k, v, blocks(d_attn), attended, lse, stats, attn_gain[None]
+        )
+        gpre, gmix, gz, gb, gc, grate, channel_sums = scan_backward(
+            projected, mixer_in, blocks(d_ssm), core, z_gate, stats, start, wdt, dtb[None], rate, skip[None],
+            ssm_gain[None],
+        )
+        grad_qkv, grad_z = flat(jnp.concatenate([gq, gk, gv], axis=3)), flat(gz)
+        of_weights = (
+            (0.5 * tndot(attn_low, mix_low)).astype(BF),
+            (0.5 * tndot(ssm_low, mix_low)).astype(BF),
+            tndot(normed, grad_z).astype(BF),
+            tndot(normed, grad_qkv).astype(BF),
+        )
+        return head_sums[0], channel_sums, grad_qkv, grad_z, flat(gpre), gmix, flat(gb), flat(gc), grate, of_weights
+
+    g_norm_attn, channel_sums, grad_qkv, grad_z, grad_step, gmix, gb, gc, grate, of_weights = one_step(mixers_back)
+    g_norm_ssm, gskip, g_dt_bias = channel_sums[0], channel_sums[1:2], channel_sums[2]
+    g_ao, g_so, g_z, g_qkv = of_weights
+    g_ao = reblock(g_ao, plan.width, ao_rows, HEADS * HEAD)
+    g_z = exchange(g_z.reshape(n, w_rows, cols))
+    g_z = jnp.swapaxes(g_z, 0, 1).reshape(w_rows, INNER)
+    g_qkv = exchange(g_qkv.reshape(n, w_rows, -1))
     g_qkv = plan.join_columns(g_qkv).astype(BF)
-    grad_core, grad_z, grad_qkv = tie((grad_core, grad_z, grad_qkv))
-    gpre, gmix, gb, gc, grate, gskip = scan_backward(
-        step_pre, mixer_in, blocks(grad_core), start, bt, ct, blocks(b_input), rate, skip[None]
+    after_one = nothing(s_down, s_gate, s_up, grate)
+    s_ao, s_so, s_qkv, s_z = over(tuple(later(g, after_one) for g in (g_ao, g_so, g_qkv, g_z)))
+    grad_projected = jnp.concatenate([gb, gc, ntdot(grad_step, wdt)], axis=1)
+    grad_projected = gather(scatter(grad_projected, 9, mark(after_one)).astype(BF), 10)
+
+    def signal_back(_):
+        grad_x, sums = signal_backward(gmix, blocks(grad_projected), xp, conv_pre, x_conv, taps)
+        grad_x = flat(grad_x)
+        return (
+            grad_x,
+            sums,
+            tndot(normed, grad_x).astype(BF),
+            tndot(grad_projected, mixer_low).astype(BF),
+            tndot(grad_step, flat(projected)[:, 2 * NST :].astype(BF)).astype(BF),
+        )
+
+    grad_x, tap_sums, g_x, g_xp, g_wdt = one_step(signal_back)
+    g_conv_w, g_conv_b = tap_sums[:KCONV], tap_sums[KCONV]
+    g_x = exchange(g_x.reshape(n, w_rows, cols))
+    g_x = jnp.swapaxes(g_x, 0, 1).reshape(w_rows, INNER)
+    grad_normed = product_scatter(
+        ((grad_x, wx, True), (grad_z, wz, True), (grad_qkv, qkv_cols, True)), n, 11
     )
-    gpre = flat(gpre)
-    nothing = lambda *sums: 0.0 * sum(g.reshape(-1)[0].astype(F32) for g in sums)
-    after_one = nothing(s_down, s_gate, s_up, grate)
-    s_ao, s_so, s_z, s_qkv = over(tuple(later(g, after_one) for g in (g_ao, g_so, g_z, g_qkv)))
-    g_dt_bias = jnp.sum(gpre, axis=0)
-    grad_step = gpre.astype(BF)
-    grad_projected = jnp.concatenate([ntdot(grad_step, wdt), flat(gb), flat(gc)], axis=1)
-    grad_projected = gather(scatter(grad_projected, 9, jnp.full((8, 128), after_one)).astype(BF), 10)
-    grad_mixer = gmix + blocks(ntdot(grad_projected, w_xp))
-    grad_conv = grad_mixer * silu_grad(conv_pre)
-    g_conv_b = jnp.sum(grad_conv, axis=(0, 1, 2))
-    g_conv_w = jnp.stack(
-        [jnp.sum(grad_conv * padded[:, :, o : o + slot_len], axis=(0, 1, 2)) for o in range(KCONV)]
+    block_out = residual + product_scatter(
+        ((activated, w_down, False),), n, 6, mark(nothing(grad_normed))
     )
-    after = jnp.concatenate(
-        [grad_conv[1:, :, :edge], jnp.zeros((1, seqs, edge, cols), F32)], axis=0
-    )
-    extended = jnp.concatenate([grad_conv, after], axis=2)
-    grad_x = sum(taps[o] * extended[:, :, edge - o : edge - o + slot_len] for o in range(KCONV))
-    grad_x = flat(grad_x).astype(BF)
-    g_x = exchange(tndot(normed, grad_x).astype(BF).reshape(n, w_rows, cols))
-    g_xp = tndot(mixer_low, grad_projected).astype(BF)
-    g_wdt = tndot(step_low, grad_step).astype(BF)
-    after_two = nothing(s_ao, s_so, s_z, s_qkv)
-    s_x, s_xp, s_wdt = over(tuple(later(g, after_two) for g in (g_x, g_xp, g_wdt)))
-    grad_normed = product_scatter(
-        ((grad_x, wx, True), (grad_z, wz, True), (grad_qkv, qkv_cols, True)), n, 11, jnp.full((8, 128), after_two)
-    )
-    block_out = residual + product_scatter(((activated, w_down, False),), n, 6, grad_normed[:8, :128])
     add_in, g_norm_in = norm_pull(grad_normed, x, scale_in, norm_in)
     grad_tokens = grad_residual + add_in
 
-    s_in = jnp.stack([s_x, s_z])
-    s_in = jnp.transpose(s_in, (2, 0, 1, 3)).reshape(w_rows, 2 * INNER)
-    s_gu = jnp.stack([s_gate, s_up], axis=1)
+    s_gu = jnp.transpose(jnp.stack([s_gate, s_up]), (2, 0, 1))
+    s_x, s_xp, s_wdt = chain_sum((g_x, g_xp, g_wdt), (5, 1, 1), replicas, 14, mark(nothing(block_out, s_ao, s_so, s_qkv, s_z)))
+    s_in = jnp.concatenate([s_x, s_z.astype(F32)], axis=1)
+    s_xp = jnp.swapaxes(jnp.concatenate([s_xp[2 * NST :], s_xp[: 2 * NST]], axis=0), 0, 1)
+    s_wdt = jnp.swapaxes(s_wdt, 0, 1)
 
     place = lambda g: lax.dynamic_update_slice_in_dim(
         jnp.zeros((n * plan.width,), F32), g, me * plan.width, 0

time: 1230 us -> 1070 us (0.87)
  Pallas kernels: 518 us -> 715 us
  waiting for transfers between devices: 193 us -> 10.8 us
  matrix products: 156 us -> 73.8 us
  local copies, waits for them, and re-layouts: 198 us -> 140 us
  other arithmetic: 103 us -> 69.4 us
    pallas_call x4 -> x12, Pallas kernels: 202 us -> 415 us  [the longest x1 92.6 us: scan_backward(): pl.pallas_call(scan_bwd_kernel, grid=(seqs, n), in_specs=[big(proj.shape[...]
    psum x3 -> x2, waiting for transfers between devices: 173 us -> 0.01 us  [per_device(): over = lambda g: lax.psum(g, 'dp')]
    pallas_call x3 -> x2, Pallas kernels: 75.7 us -> 22.9 us  [all_gather4(): pl.pallas_call(ag4_kernel, out_shape=jax.ShapeDtypeStruct((n,) + x.shape,...]
    dot_general x7 -> x1, matrix products: 49.6 us -> 7.41 us  [dot(): return jnp.dot(a, b, preferred_element_type=F32)]
    convert_element_type x7 -> x0, local copies, waits for them, and re-layouts: 33.3 us -> none  [the longest x2 14.6 us: per_device(): full = lambda g: g.astype(F32)]
    dot_general x5 -> x1, matrix products: 34.1 us -> 2.42 us  [ntdot(): return lax.dot_general(a, b, NT, preferred_element_type=F32)]
    pallas_call x1 -> x2, Pallas kernels: 11.1 us -> 34.5 us  [reduce_scatter4(): pl.pallas_call(rs4_kernel, out_shape=jax.ShapeDtypeStruct(blk, F32), in_s...]
    reshape x8 -> x13, local copies, waits for them, and re-layouts: 28.9 us -> 43.8 us  [per_device(): g.reshape(-1)[0].astype(F32)]
  transfers between devices with their start and end apart: 13 -> 11, of which waited for: 4 -> 2; matrix products, arithmetic and copies ran while one was open for 24% -> 18% of each run, Pallas kernels for 31% -> 56%
where the time goes in v2:
time: 1070 us; the launch traced here: 1060 us
  Pallas kernels  715 us (67%)
  local copies, waits for them, and re-layouts  140 us (13%)
  matrix products  73.8 us (7%)
  other arithmetic  69.4 us (6%)
  starting transfers between devices  26.9 us (3%)
  between operations  23.4 us (2%)
  waiting for transfers between devices  10.8 us (1%)
    pallas_call x4, Pallas kernels, product_scatter(): pl.pallas_call(functools.partial(mm_rs4_kernel, tuple((t for _, _, t in p...  163 us
    pallas_call x1, Pallas kernels, scan_backward(): pl.pallas_call(scan_bwd_kernel, grid=(seqs, n), in_specs=[big(proj.shape[...  92.6 us
    pallas_call x2, Pallas kernels, gather_product(): pl.pallas_call(functools.partial(gather_product4_kernel, body, len(weight...  84.4 us
    dot_general x10, matrix products, tndot(): return lax.dot_general(a, b, TN, preferred_element_type=F32)  64 us
    pallas_call x1, Pallas kernels, gather_and_exchange(): pl.pallas_call(functools.partial(start_kernel, n, moves), out_shape=[jax....  57.3 us
    pallas_call x1, Pallas kernels, chain_sum(): pl.pallas_call(functools.partial(chain_kernel, axis, count, tuple(cuts)),...  52 us
    reshape x13, local copies, waits for them, and re-layouts, per_device(): g.reshape(-1)[0].astype(F32)  43.8 us
    pallas_call x4, Pallas kernels, small_sum(): pl.pallas_call(functools.partial(stat_kernel, n, axis), out_shape=jax.Sha...  42.5 us
  transfers between devices with their start and end apart: 11, of which 2 were waited for; matrix products, arithmetic and copies ran while one was open for 18% of the time, Pallas kernels for 56%

profile of v2, /device:TPU:0, one launch (start us, length us, event | category | flops | bytes accessed | tf_op | source)
XLA Modules:
  0.0 1060.5 jit_solution(6310383917248935082)
XLA Ops:
  10.8 57.3 %shard_map.357 = (bf16[8,256,1600]{2,1,0:T(8,128)(2,1)}, bf16[8,200,512]{2,1,0:T(8,128)(2,1)}, bf16[8,200,400]{2,1,0:T(8,128)(2,1)}, bf16[8,200,400]{2,1,0:T(8,128)(2,1)}) custom-call(bf16[256,1600]{1,0:T(8,128)(2,1)} %bitcast.260, f32[1,1600]{1,0:T(1,128)} %broadcast_in_dim.62.gain_ref, bf16[200,2240]{1,0:T(8,128)(2,1)} %w_ref.1, bf16[200,6400]{1,0:T(8,128)(2,1)} %in_ref.1), custom_call_target="tpu_custom_call" | custom-call | tf_op jit(solution)/shard_map/pallas_call | solution.py:858
  68.1 7.4 convolution_convert_fusion.6
  83.6 4.6 all-to-all-start
  91.4 15.7 %shard_map.358 = (f32[8,2,128,256]{3,2,1,0:T(8,128)S(1)}, f32[8,2,128,4]{3,2,1,0:T(8,128)}) custom-call(s32[8]{0:T(128)S(1)} %fusion.33.slot_ref, s32[2]{0:T(128)S(1)} %copy-done.54, bf16[8,2,128,256]{3,2,1,0:T(8,128)(2,1)} %bitcast.233, bf16[8,2,128,128]{3,2,1,0:T(8,128)(2,1)S(1)} %bitcast.245, bf16[8,2,128,128]{3,2,1,0:T(8,128)(2,1)S(1)} %bitcast.242), custom_call_target="tpu_custom_call" | custom-call | tf_op jit(solution)/shard_map/pallas_call | solution.py:316
  107.2 16.0 %shard_map.359 = (f32[8,2,128,256]{3,2,1,0:T(8,128)S(1)}, f32[8,2,128,4]{3,2,1,0:T(8,128)}) custom-call(s32[8]{0:T(128)S(1)} %fusion.33.slot_ref, s32[2]{0:T(128)S(1)} %copy-done.54, bf16[8,2,128,256]{3,2,1,0:T(8,128)(2,1)} %bitcast.234, bf16[8,2,128,128]{3,2,1,0:T(8,128)(2,1)S(1)} %bitcast.246, ...), custom_call_target="tpu_custom_call", output_to_operand_aliasing={{0}: (5, {}), {1}: (6, {})} | custom-call | tf_op jit(solution)/shard_map/pallas_call | solution.py:316
  126.0 4.6 all-to-all-start.1
  139.8 4.8 slice_bitcast_fusion
  147.3 18.4 %shard_map.360 = (bf16[8,2,128,400]{3,2,1,0:T(8,128)(2,1)}, f32[8,2,128,400]{3,2,1,0:T(8,128)}, f32[8,2,128,400]{3,2,1,0:T(8,128)}, bf16[8,2,128,400]{3,2,1,0:T(8,128)(2,1)}, f32[8,2,128,132]{3,2,1,0:T(8,128)}) custom-call(bf16[8,2,128,1600]{3,2,1,0:T(8,128)(2,1)} %bitcast.227, bf16[1600,400]{1,0:T(8,128)(2,1)} %bitcast.236, ...), custom_call_target="tpu_custom_call" | custom-call | tf_op jit(solution)/shard_map/pallas_call | solution.py:423
  169.0 15.4 %shard_map.361 = f32[256,132]{1,0:T(8,128)} custom-call(bf16[8,256,132]{2,1,0:T(8,128)(2,1)} %bitcast.254, f32[8,128]{1,0:T(8,128)} %broadcast_47_after_ref_refs_4__refs_6_.2.after_ref.refs_4_.refs_6_), custom_call_target="tpu_custom_call" | custom-call | tf_op jit(solution)/shard_map/pallas_call | solution.py:805
  186.0 12.4 %shard_map.362 = bf16[8,256,132]{2,1,0:T(8,128)(2,1)} custom-call(bf16[256,132]{1,0:T(8,128)(2,1)} %convert_element_type.280.x_ref), custom_call_target="tpu_custom_call" | custom-call | tf_op jit(solution)/shard_map/pallas_call | solution.py:732
  198.4 2.8 convert.80.proj_ref
  201.2 41.7 %shard_map.363 = (f32[8,2,128,400]{3,2,1,0:T(8,128)}, f32[8,2,128,400]{3,2,1,0:T(8,128)}, f32[8,2,128,1]{3,2,1,0:T(8,128)}, f32[8,2,16,400]{3,2,1,0:T(8,128)}) custom-call(f32[8,2,128,132]{3,2,1,0:T(8,128)} %convert.80.proj_ref, f32[8,2,128,400]{3,2,1,0:T(8,128)} %get-tuple-element.260.mix_ref, bf16[8,2,128,1600]{3,2,1,0:T(8,128)(2,1)} %bitcast.228, ...), custom_call_target="tpu_custom_call" | custom-call | tf_op jit(solution)/shard_map/pallas_call | solution.py:117
  245.1 6.6 shard_map.364
  253.8 7.8 shard_map.365
  263.8 38.1 %shard_map.366 = f32[256,1600]{1,0:T(8,128)} custom-call(bf16[8,256,256]{2,1,0:T(8,128)(2,1)} %get-tuple-element.265.refs_0_, bf16[8,256,400]{2,1,0:T(8,128)(2,1)} %get-tuple-element.266.refs_1_, bf16[256,1600]{1,0:T(8,128)(2,1)} %pad_dynamic-slice_fusion.refs_2_.refs_0_, bf16[400,1600]{1,0:T(8,128)(2,1)} %refs_1_.2, ...), custom_call_target="tpu_custom_call" | custom-call | tf_op jit(solution)/shard_map/pallas_call | solution.py:1001
  306.4 42.1 %shard_map.367 = (bf16[8,256,1600]{2,1,0:T(8,128)(2,1)}, bf16[8,256,688]{2,1,0:T(8,128)(2,1)}, bf16[8,256,688]{2,1,0:T(8,128)(2,1)}, bf16[8,256,688]{2,1,0:T(8,128)(2,1)}) custom-call(bf16[256,1600]{1,0:T(8,128)(2,1)} %multiply_convert_fusion.x_ref, bf16[688,1600]{1,0:T(8,128)(2,1)} %get-tuple-element.464.refs_0_.refs_2_, ...), custom_call_target="tpu_custom_call" | custom-call | tf_op jit(solution)/shard_map/pallas_call | solution.py:1245
  348.6 13.8 %shard_map.368 = (bf16[8,256,688]{2,1,0:T(8,128)(2,1)}, bf16[8,256,688]{2,1,0:T(8,128)(2,1)}) custom-call(bf16[8,256,1600]{2,1,0:T(8,128)(2,1)} %bitcast.248, bf16[688,1600]{1,0:T(8,128)(2,1)} %refs_1_.3, bf16[8,256,688]{2,1,0:T(8,128)(2,1)} %get-tuple-element.268.gate_ref, bf16[8,256,688]{2,1,0:T(8,128)(2,1)} %get-tuple-element.269.up_ref), custom_call_target="tpu_custom_call" | custom-call | tf_op jit(solution)/shard_map/pallas_call | solution.py:517
  362.4 10.8 %bitcast_convert_fusion.1 = bf16[688,1600]{1,0:T(8,128)(2,1)} fusion(bf16[8,256,688]{2,1,0:T(8,128)(2,1)} %get-tuple-element.270.refs_0_, bf16[8,256,1600]{2,1,0:T(8,128)(2,1)} %get-tuple-element.272), kind=kOutput, calls=%fused_computation.22 | convolution fusion | flops 4509977600 | bytes 11573248 | tf_op jit(solution)/shard_map/dot_general | solution.py:37
  373.2 6.9 bitcast_convert_fusion
  380.1 7.4 convolution_convert_fusion.5
  387.5 5.4 reshape.582
  393.0 5.4 reshape.583
  403.5 43.5 %shard_map.369 = f32[256,1600]{1,0:T(8,128)} custom-call(bf16[8,256,688]{2,1,0:T(8,128)(2,1)} %get-tuple-element.270.refs_0_, bf16[8,256,688]{2,1,0:T(8,128)(2,1)} %get-tuple-element.271.refs_1_, bf16[688,1600]{1,0:T(8,128)(2,1)} %get-tuple-element.464.refs_0_.refs_2_, bf16[688,1600]{1,0:T(8,128)(2,1)} %get-tuple-element.463.refs_1_.refs_3_, ...), custom_call_target="tpu_custom_call" | custom-call | tf_op jit(solution)/shard_map/pallas_call | solution.py:1001
  449.9 3.4 fusion.35
  453.3 42.3 %shard_map.370 = (bf16[8,256,1600]{2,1,0:T(8,128)(2,1)}, f32[8,256,256]{2,1,0:T(8,128)}, f32[8,256,400]{2,1,0:T(8,128)}, f32[8,256,2]{2,1,0:T(8,128)}) custom-call(bf16[256,1600]{1,0:T(8,128)(2,1)} %get-tuple-element.456.x_ref, bf16[256,1600]{1,0:T(8,128)(2,1)} %pad_dynamic-slice_fusion.refs_2_.refs_0_, bf16[400,1600]{1,0:T(8,128)(2,1)} %refs_1_.2, ...), custom_call_target="tpu_custom_call" | custom-call | tf_op jit(solution)/shard_map/pallas_call | solution.py:1245
  495.6 3.3 fusion.38
  502.7 7.0 shard_map.371
  510.5 168.5 %conditional.2 = (f32[256]{0:T(256)S(1)}, bf16[2048,400]{1,0:T(8,128)(2,1)}, f32[8,2,128,400]{3,2,1,0:T(8,128)}, f32[16,400]{1,0:T(8,128)}, bf16[400,1600]{1,0:T...) conditional(s32[]{:T(128)} %bitcast.56, () %tuple.48, ...), branch_computations={%region_3.4_spmd, %region_4.5_spmd} | conditional | flops 10279668736 | bytes 83468040 | solution.py:1370
  511.9 37.5 %branch_1_fun.5 = (bf16[8,2,128,256]{3,2,1,0:T(8,128)(2,1)}, bf16[8,2,128,128]{3,2,1,0:T(8,128)(2,1)}, bf16[8,2,128,128]{3,2,1,0:T(8,128)(2,1)}, f32[8,256]{1,0:T(8,128)}) custom-call(s32[8]{0:T(128)} %get-tuple-element.129.slot_ref, s32[2]{0:T(128)S(1)} %get-tuple-element.130.len_ref, bf16[8,2,128,256]{3,2,1,0:T(8,128)(2,1)} %get-tuple-element.131.q_ref, ...), custom_call_target="tpu_custom_call" | custom-call | tf_op jit(solution)/shard_map/cond/branch_1_fun/pallas_call | solution.py:382
  550.1 92.6 %branch_1_fun.6 = (bf16[8,2,128,400]{3,2,1,0:T(8,128)(2,1)}, f32[8,2,128,400]{3,2,1,0:T(8,128)}, bf16[8,2,128,400]{3,2,1,0:T(8,128)(2,1)}, f32[8,2,128,16]{3,2,1...) custom-call(f32[8,2,128,132]{3,2,1,0:T(8,128)} %get-tuple-element.140.proj_ref, ...), custom_call_target="tpu_custom_call" | custom-call | tf_op jit(solution)/shard_map/cond/branch_1_fun/pallas_call | solution.py:246
  642.7 7.4 fusion.1
  650.1 8.0 fusion.4
  661.0 6.4 fusion.2
  669.9 6.0 fusion.5
  679.0 3.7 all-to-all-start.2
  688.0 3.2 collective-permute-start
  691.1 3.4 copy.124
  694.6 9.9 all-to-all-done.2
  704.4 4.3 all-to-all-start.4
  711.5 5.6 reshape.586
  718.3 4.2 reshape.587
  723.7 4.4 reshape.588
  735.4 3.1 add.356
  739.5 3.5 add_add_fusion
  746.1 2.8 pad_maximum_fusion.1.p_ref
  750.5 19.1 %shard_map.372 = f32[256,132]{1,0:T(8,128)} custom-call(bf16[8,256,132]{2,1,0:T(8,128)(2,1)} %pad_maximum_fusion.1.p_ref, f32[8,128]{1,0:T(8,128)} %broadcast_in_dim.69.after_ref), custom_call_target="tpu_custom_call" | custom-call | tf_op jit(solution)/shard_map/pallas_call | solution.py:805
  771.3 10.5 shard_map.373
  781.8 27.1 %conditional.3 = (bf16[1600,400]{0,1:T(8,128)(2,1)}, bf16[132,400]{1,0:T(8,128)(2,1)S(1)}, bf16[400,100]{1,0:T(8,128)(2,1)S(1)}, bf16[8,256,400]{2,1,0:T(8,128)(2,1)}, f32[5,400]{1,0:T(8,128)S(1)}) conditional(s32[]{:T(128)} %bitcast.56, () %tuple.47, (bf16[8,256,132]{2,1,0:T(8,128)(2,1)}, f32[8,2,128,400]{3,2,1,0:T(8,128)}, ...), branch_computations={%region_8.9_spmd, %region_9.10_spmd} | conditional | flops 3002551808 | bytes 24337760 | solution.py:1370
  782.0 15.6 %branch_1_fun.7 = (bf16[8,2,128,400]{3,2,1,0:T(8,128)(2,1)}, f32[8,400]{1,0:T(8,128)S(1)}) custom-call(f32[8,2,128,400]{3,2,1,0:T(8,128)} %get-tuple-element.165.gmix_ref, bf16[8,2,128,132]{3,2,1,0:T(8,128)(2,1)} %bitcast.238, bf16[132,400]{1,0:T(8,128)(2,1)S(1)} %get-tuple-element.167.xp_ref, f32[8,2,128,400]{3,2,1,0:T(8,128)} %get-tuple-element.168.pre_ref, ...), custom_call_target="tpu_custom_call" | custom-call | tf_op jit(solution)/shard_map/cond/branch_1_fun/pallas_call | solution.py:470
  797.6 8.0 fusion.6
  808.9 43.0 %shard_map.374 = f32[256,1600]{1,0:T(8,128)} custom-call(bf16[8,256,400]{2,1,0:T(8,128)(2,1)} %get-tuple-element.289.refs_0_, bf16[8,256,400]{2,1,0:T(8,128)(2,1)} %get-tuple-element.290.refs_1_, bf16[8,256,512]{2,1,0:T(8,128)(2,1)} %get-tuple-element.291.refs_2_, bf16[1600,400]{1,0:T(8,128)(2,1)} %bitcast.237, bf16[1600,400]{1,0:T(8,128)(2,1)} %bitcast.42.wz_ref.refs_4_, ...), custom_call_target="tpu_custom_call" | custom-call | tf_op jit(solution)/shard_map/pallas_call | solution.py:1001
  855.9 38.0 %shard_map.375 = f32[256,1600]{1,0:T(8,128)} custom-call(bf16[8,256,688]{2,1,0:T(8,128)(2,1)} %get-tuple-element.267.refs_0_, bf16[688,1600]{1,0:T(8,128)(2,1)} %refs_1_.3, f32[8,128]{1,0:T(8,128)} %broadcast_in_dim.70.refs_2_), custom_call_target="tpu_custom_call" | custom-call | tf_op jit(solution)/shard_map/pallas_call | solution.py:1001
  893.9 3.4 copy.122
  897.4 4.8 all-to-all-start.3
  905.5 20.0 %shard_map.377 = f32[40,128]{1,0:T(8,128)} custom-call(f32[40,128]{1,0:T(8,128)} %pad_bitcast_fusion.x_ref), custom_call_target="tpu_custom_call" | custom-call | tf_op jit(solution)/shard_map/pallas_call | solution.py:663
  926.4 3.2 fusion.34
  934.7 8.9 shard_map.378
  948.0 3.2 reshape.595
  956.6 5.9 convert_bitcast_fusion
  964.5 3.1 reshape.594.refs_0_
  976.5 3.8 reshape.600
  981.4 3.8 reshape.597
  992.7 52.0 %shard_map.376 = (f32[200,3200]{1,0:T(8,128)}, f32[132,400]{1,0:T(8,128)}, f32[400,100]{1,0:T(8,128)}) custom-call(bf16[200,3200]{1,0:T(8,128)(2,1)} %reshape.594.refs_0_, bf16[132,400]{1,0:T(8,128)(2,1)S(1)} %get-tuple-element.295.refs_1_, bf16[400,100]{1,0:T(8,128)(2,1)S(1)} %copy-done.38, f32[8,128]{1,0:T(8,128)} %broadcast_in_dim.72.refs_3_), custom_call_target="tpu_custom_call" | custom-call | tf_op jit(solution)/shard_map/pallas_call | solution.py:1134
  1046.5 3.2 convert_element_type.332
  (290 shorter events, 135.5 us)
Async XLA Ops:
  7.2 118.3 %copy-start = (bf16[100,3200]{1,0:T(8,128)(2,1)S(1)}, bf16[100,3200]{1,0:T(8,128)(2,1)}, u32[]{:S(2)}) copy-start(bf16[100,3200]{1,0:T(8,128)(2,1)} %param.33) | copy-start | bytes 1920004
  7.2 254.3 %all-gather.3.cloned.1.call-start = ((), (), s32[]{:S(2)}) async-start(), calls=%async_computation.5 | async-start | bytes 5990400 | tf_op jit(solution)/shard_map/all_gather | solution.py:1393
  68.0 9.9 copy-start.34
  68.1 10.9 %copy-start.54 = (s32[2]{0:T(128)S(1)}, s32[2]{0:T(128)}, u32[]{:S(2)}) copy-start(s32[2]{0:T(128)} %len_ref.3) | copy-start | bytes 28
  78.9 269.6 %all-gather.5.cloned.1.call-start = ((), (), s32[]{:S(2)}) async-start(), calls=%async_computation.6 | async-start | bytes 7667712 | tf_op jit(solution)/shard_map/all_gather | solution.py:1398
  83.6 42.4 %all-to-all-start = ((bf16[8,200,400]{2,1,0:T(8,128)(2,1)}), bf16[8,200,400]{2,1,0:T(8,128)(2,1)}, u32[]{:S(2)}, u32[]{:S(2)}) async-start(bf16[8,200,400]{2,1,0:T(8,128)(2,1)} %get-tuple-element.257), calls=%async_computation | async-start | bytes 3276800 | tf_op jit(solution)/shard_map/all_to_all | solution.py:1362
  88.2 3.1 copy-start.28
  91.3 15.8 %copy-start.55 = (s32[8]{0:T(128)}, s32[8]{0:T(128)S(1)}, u32[]{:S(2)}) copy-start(s32[8]{0:T(128)S(1)} %fusion.33.slot_ref) | copy-start | bytes 100
  91.4 15.8 %copy-start.14 = (bf16[2048,128]{1,0:T(8,128)(2,1)}, bf16[2048,128]{1,0:T(8,128)(2,1)S(1)}, u32[]{:S(2)}) copy-start(bf16[2048,128]{1,0:T(8,128)(2,1)S(1)} %get-tuple-element.468) | copy-start | bytes 1572868
  125.9 4.7 copy-start.53
  125.9 4.7 copy-start.44
  126.0 75.2 %all-to-all-start.1 = ((bf16[8,200,400]{2,1,0:T(8,128)(2,1)}), bf16[8,200,400]{2,1,0:T(8,128)(2,1)}, u32[]{:S(2)}, u32[]{:S(2)}) async-start(bf16[8,200,400]{2,1,0:T(8,128)(2,1)} %get-tuple-element.261), calls=%async_computation.1 | async-start | bytes 3276800 | tf_op jit(solution)/shard_map/all_to_all | solution.py:1362
  186.0 15.2 %copy-start.39 = (f32[16,400]{1,0:T(8,128)S(1)}, f32[16,400]{1,0:T(8,128)}, u32[]{:S(2)}) copy-start(f32[16,400]{1,0:T(8,128)} %exponential_negate_fusion.rate_ref) | copy-start | bytes 76804
  301.8 3.5 copy-start.45
  362.4 10.8 %copy-start.21 = (bf16[8,256,688]{2,1,0:T(8,128)(2,1)S(1)}, bf16[8,256,688]{2,1,0:T(8,128)(2,1)}, u32[]{:S(2)}) copy-start(bf16[8,256,688]{2,1,0:T(8,128)(2,1)} %get-tuple-element.271.refs_1_) | copy-start | bytes 8454148
  362.4 10.8 %copy-start.58 = (bf16[8,256,1600]{2,1,0:T(8,128)(2,1)S(1)}, bf16[8,256,1600]{2,1,0:T(8,128)(2,1)}, u32[]{:S(2)}) copy-start(bf16[8,256,1600]{2,1,0:T(8,128)(2,1)} %get-tuple-element.272) | copy-start | bytes 19660804
  362.4 17.7 %slice-start.2 = ((s8[6815744]{0:T(1024)(128)(4,1)}), s8[4194304]{0:T(1024)(128)(4,1)S(1)}, s32[]{:S(2)}) async-start(s8[6815744]{0:T(1024)(128)(4,1)} %bitcast.249), calls=%async_computation.11 | async-start | bytes 8388608
  373.2 6.9 slice-start.3
  373.2 6.9 copy-start.20
  398.4 313.1 %all-reduce.13.cloned.1.call-start = ((), (), s32[]{:S(2)}) async-start(), calls=%async_computation.8 | async-start | bytes 13737984 | tf_op jit(solution)/shard_map/psum | solution.py:1365
  446.9 2.6 copy-start.3
  446.9 3.0 copy-start.8
  498.9 11.6 %copy-start.15 = (bf16[2048,128]{1,0:T(8,128)(2,1)S(1)}, bf16[2048,128]{1,0:T(8,128)(2,1)}, u32[]{:S(2)}) copy-start(bf16[2048,128]{1,0:T(8,128)(2,1)} %copy-done.14) | copy-start | bytes 1572868
  550.1 92.6 %copy-start.29 = (bf16[8,256,400]{2,1,0:T(8,128)(2,1)S(1)}, bf16[8,256,400]{2,1,0:T(8,128)(2,1)}, u32[]{:S(2)}) copy-start(bf16[8,256,400]{2,1,0:T(8,128)(2,1)} %get-tuple-element.419) | copy-start | bytes 4915204 | tf_op jit(solution)/shard_map/cond
  642.7 25.6 %copy-start.40 = (f32[16,400]{1,0:T(8,128)}, f32[16,400]{1,0:T(8,128)S(1)}, u32[]{:S(2)}) copy-start(f32[16,400]{1,0:T(8,128)S(1)} %get-tuple-element.516) | copy-start | bytes 76804 | tf_op jit(solution)/shard_map/cond
  642.7 18.3 %slice-start = ((s8[6815744]{0:T(1024)(128)(4,1)}), s8[4194304]{0:T(1024)(128)(4,1)S(1)}, s32[]{:S(2)}) async-start(s8[6815744]{0:T(1024)(128)(4,1)} %bitcast.231), calls=%async_computation.9 | async-start | bytes 8388608 | tf_op jit(solution)/shard_map/cond
  650.1 8.0 copy-start.32
  650.1 10.9 %slice-start.1 = ((s8[6815744]{0:T(1024)(128)(4,1)}), s8[2621440]{0:T(1024)(128)(4,1)S(1)}, s32[]{:S(2)}) async-start(s8[6815744]{0:T(1024)(128)(4,1)} %bitcast.231), calls=%async_computation.10 | async-start | bytes 5242880 | tf_op jit(solution)/shard_map/cond
  661.0 7.9 copy-start.31
  679.0 7.4 copy-start.24
  679.0 7.4 copy-start.47
  679.0 7.4 copy-start.49
  679.0 7.4 copy-start.51
  679.0 7.4 copy-start.56
  679.0 3.8 copy-start.59
  679.0 4.5 copy-start.16
  679.0 25.4 %all-to-all-start.2 = ((bf16[8,200,512]{2,1,0:T(8,128)(2,1)}), bf16[8,200,512]{2,1,0:T(8,128)(2,1)S(1)}, u32[]{:S(2)}, u32[]{:S(2)}) async-start(bf16[8,200,512]{2,1,0:T(8,128)(2,1)} %bitcast.77), calls=%async_computation.2 | async-start | bytes 3276800 | tf_op jit(solution)/shard_map/all_to_all | solution.py:1362
  686.4 53.1 %collective-permute-start.1 = (bf16[200,1600]{1,0:T(8,128)(2,1)}, bf16[200,1600]{1,0:T(8,128)(2,1)}, u32[]{:S(2)}, u32[]{:S(2)}) collective-permute-start(bf16[200,1600]{1,0:T(8,128)(2,1)} %get-tuple-element.466), channel_id=1, source_target_pairs={{3,5},{4,6},{5,7},{11,13},{12,14},{13,15},{19,21},{20,22},{21,23},... | collective-permute-start | bytes 1920008 | tf_op jit(solution)/shard_map/ppermute | solution.py:1334
  688.0 51.6 %collective-permute-start = (bf16[200,1600]{1,0:T(8,128)(2,1)}, bf16[200,1600]{1,0:T(8,128)(2,1)}, u32[]{:S(2)}, u32[]{:S(2)}) collective-permute-start(bf16[200,1600]{1,0:T(8,128)(2,1)} %get-tuple-element.465), channel_id=1, source_target_pairs={{0,1},{1,2},{2,3},{3,4},{4,5},{5,6},{6,7},{8,9},{9,10},{10,11},{11... | collective-permute-start | bytes 1920008 | tf_op jit(solution)/shard_map/ppermute | solution.py:1334
  704.4 28.9 %all-to-all-start.4 = ((bf16[8,200,400]{2,1,0:T(8,128)(2,1)}), bf16[8,200,400]{2,1,0:T(8,128)(2,1)}, u32[]{:S(2)}, u32[]{:S(2)}) async-start(bf16[8,200,400]{2,1,0:T(8,128)(2,1)} %bitcast.252), calls=%async_computation.4 | async-start | bytes 3276800 | tf_op jit(solution)/shard_map/all_to_all | solution.py:1362
  708.7 258.8 %all-reduce.11.cloned.1.call-start = ((), (), s32[]{:S(2)}) async-start(), calls=%async_computation.7 | async-start | bytes 8396800 | tf_op jit(solution)/shard_map/psum | solution.py:1365
  711.5 6.8 copy-start.11
  735.4 3.1 copy-start.18
  743.0 2.8 copy-start.57
  743.0 3.1 copy-start.25
  745.5 3.4 copy-start.41
  748.9 32.9 %copy-start.5 = (f32[8,2,128,132]{3,2,1,0:T(8,128)S(1)}, f32[8,2,128,132]{3,2,1,0:T(8,128)}, u32[]{:S(2)}) copy-start(f32[8,2,128,132]{3,2,1,0:T(8,128)} %convert.80.proj_ref) | copy-start | bytes 3244036
  797.6 8.0 copy-start.10
  797.6 8.0 copy-start.26
  808.9 43.1 %copy-start.37 = (bf16[400,100]{1,0:T(8,128)(2,1)}, bf16[400,100]{1,0:T(8,128)(2,1)S(1)}, u32[]{:S(2)}) copy-start(bf16[400,100]{1,0:T(8,128)(2,1)S(1)} %get-tuple-element.296.refs_2_) | copy-start | bytes 240004
  897.4 4.8 copy-start.46
  897.4 65.2 %all-to-all-start.3 = ((bf16[8,200,400]{2,1,0:T(8,128)(2,1)}), bf16[8,200,400]{2,1,0:T(8,128)(2,1)}, u32[]{:S(2)}, u32[]{:S(2)}) async-start(bf16[8,200,400]{2,1,0:T(8,128)(2,1)} %bitcast.96), calls=%async_computation.3 | async-start | bytes 3276800 | tf_op jit(solution)/shard_map/all_to_all | solution.py:1362
  902.2 24.1 %copy-start.4 = (f32[256,1600]{1,0:T(8,128)S(1)}, f32[256,1600]{1,0:T(8,128)}, u32[]{:S(2)}) copy-start(f32[256,1600]{1,0:T(8,128)} %copy-done.2) | copy-start | bytes 4915204
  926.3 3.2 copy-start.6
  926.3 3.2 copy-start.7
  926.3 3.2 copy-start.17
  931.2 2.4 copy-start.50
  931.2 2.4 copy-start.52
  948.0 8.6 copy-start.12
  967.6 4.0 copy-start.19
  976.5 16.2 %copy-start.38 = (bf16[400,100]{1,0:T(8,128)(2,1)S(1)}, bf16[400,100]{1,0:T(8,128)(2,1)}, u32[]{:S(2)}) copy-start(bf16[400,100]{1,0:T(8,128)(2,1)} %copy-done.37) | copy-start | bytes 240004
  1046.5 3.2 copy-start.23
  1049.7 3.4 copy-start.42
  1049.7 4.1 copy-start.1
  (11 other events, 18.2 us)
Sparse Core Ops, SparseCore 0:
  79.0 57.0 all-gather.2
  138.0 59.7 all-gather.4
  401.8 242.8 all-reduce.12
  743.1 165.8 all-reduce.10

commit v3 on v2

--- a/solution.py
+++ b/solution.py
@@ -76,7 +76,7 @@
         wide_ref[:, :cols] = rate_ref[...] * LOG2E
 
     start_ref[0, 0] = h_ref[:, :cols]
-    proj = proj_ref[0, 0]
+    proj = proj_ref[0, 0].astype(F32)
     turn_chunks(proj, bt_ref, None)
     pre = dot(proj[:, 2 * NST :].astype(BF), wdt_ref[...]) + dtb_ref[...]
     dt = jax.nn.softplus(pre)
@@ -132,7 +132,7 @@
     )(proj, mix, rows, wz, wdt, dtb, rate, skip)
 
 
-def scan_bwd_kernel(proj_ref, mix_ref, d_ref, core_ref, z_ref, stat_ref, start_ref, wdt_ref, dtb_ref, rate_ref, skip_ref,
+def scan_bwd_kernel(len_ref, proj_ref, mix_ref, d_ref, core_ref, z_ref, stat_ref, start_ref, wdt_ref, dtb_ref, rate_ref, skip_ref,
                     gain_ref, gpre_ref, gmix_ref, gz_ref, gb_ref, gc_ref, grate_ref, sums_ref,
                     carry_ref, dt_ref, u_ref, gy_ref, wide_ref, hs_ref, gs_ref, q_ref, bt_ref, ct_ref):
     length, cols = mix_ref.shape[2:]
@@ -154,89 +154,99 @@
             ref[...] = jnp.zeros_like(ref)
         wide_ref[0:NST, :cols] = rate_ref[...] * LOG2E
 
-    scale, shift = stat_ref[0, 0][:, 2:3], stat_ref[0, 0][:, 3:4]
-    d, core, z = d_ref[0, 0], core_ref[0, 0], z_ref[0, 0]
-    logistic = jax.nn.sigmoid(z)
-    gated = core * (z * logistic)
-    grad_gated = scale * (d * gain_ref[...] - gated * shift)
-    gy_ref[:, :cols] = grad_gated * (z * logistic)
-    gz_ref[0, 0] = (grad_gated * core * (logistic * (1.0 + z * (1.0 - logistic)))).astype(BF)
-    sums_ref[0:1] += jnp.sum(d * gated * scale, axis=0, keepdims=True)
-    sums_ref[1:2] += jnp.sum(gy_ref[:, :cols] * mix_ref[0, 0], axis=0, keepdims=True)
-    proj = proj_ref[0, 0]
-    turn_chunks(proj, bt_ref, ct_ref)
-    pre = dot(proj[:, 2 * NST :].astype(BF), wdt_ref[...]) + dtb_ref[...]
-    dt = jax.nn.softplus(pre)
-    dt_ref[:, :cols] = dt
-    u_ref[:, :cols] = dt * mix_ref[0, 0]
-    wide_ref[NST:, :cols] = start_ref[0, 0]
-    rate = wide_ref[0:NST]
-    hs_ref[0:NST] = wide_ref[NST:].astype(BF)
-
-    def ahead(k, h):
-        base = pl.multiple_of(k * CHUNK, CHUNK)
-        bt = bt_ref[k]
-        for t in range(CHUNK):
-            a = jnp.exp2(dt_ref[pl.ds(base + t, 1), :] * rate)
-            h = a * h + bt[:, t : t + 1] * u_ref[pl.ds(base + t, 1), :]
-            hs_ref[pl.ds(pl.multiple_of((base + t + 1) * NST, NST), NST), :] = h.astype(BF)
-        return h
-
-    lax.fori_loop(0, length // CHUNK, ahead, wide_ref[NST:])
-
-    def back(r, state):
-        carry, grate = state
-        k = length // CHUNK - 1 - r
-        base = pl.multiple_of(k * CHUNK, CHUNK)
-        ct = ct_ref[k]
-        qr_late = None
-        for t in reversed(range(CHUNK)):
-            at = pl.ds(pl.multiple_of((base + t) * NST, NST), NST)
-            dt_row = dt_ref[pl.ds(base + t, 1), :]
-            a = jnp.exp2(dt_row * rate)
-            g = ct[:, t : t + 1] * gy_ref[pl.ds(base + t, 1), :] + carry
-            carry = a * g
-            q = carry * hs_ref[at, :].astype(F32)
-            grate = grate + q * dt_row
-            gs_ref[at, :] = g.astype(BF)
-            qr = q * rate
-            qr = qr[:half] + qr[half:]
-            if t % 2:
-                qr_late = qr
-            else:
-                both = jnp.concatenate([qr, qr_late], axis=0).astype(BF)
-                q_ref[pl.ds(pl.multiple_of((base + t) * half, NST), NST), :] = both
-        return carry, grate
-
-    carry, grate = lax.fori_loop(
-        0, length // CHUNK, back, (carry_ref[...], jnp.zeros(carry_ref.shape, F32))
-    )
-    carry_ref[...] = carry
-    grate_ref[...] += grate[:, :cols]
-    brep = dot(proj[:, :NST].astype(BF), tile)
-    gy_low = gy_ref[...].astype(BF)
-    u_low = u_ref[...].astype(BF)
-    gcs, gbs = [], []
-    for pair in range(length // CHUNK // 2):
-        gdts = dot(folded, q_ref[pair * spread : (pair + 1) * spread]) * LN2
-        for k in (2 * pair, 2 * pair + 1):
-            rows = slice(k * CHUNK, (k + 1) * CHUNK)
-            deep = slice(k * spread, (k + 1) * spread)
-            mix, dt_now, gy = mix_ref[0, 0, rows, :], dt_ref[rows, :cols], gy_ref[rows, :cols]
-            gs = gs_ref[deep]
-            gu = dot((brep[rows] * own).astype(BF), gs)[:, :cols]
-            gdt = gdts[(k % 2) * CHUNK : (k % 2 + 1) * CHUNK, :cols] + gu * mix
-            gpre = gdt * jax.nn.sigmoid(pre[rows])
-            gpre_ref[0, 0, rows, :] = gpre.astype(BF)
-            sums_ref[2:3] += jnp.sum(gpre, axis=0, keepdims=True)
-            gmix_ref[0, 0, rows, :] = gu * dt_now + skip_ref[...] * gy
-            hs = hs_ref[k * spread + NST : (k + 1) * spread + NST]
-            gcs.append((ntdot(gy_low[rows], hs) * own).astype(BF))
-            gbs.append((ntdot(u_low[rows], gs) * own).astype(BF))
-    gc_ref[0, 0] = ntdot(jnp.concatenate(gcs, axis=0), tile)
-    gb_ref[0, 0] = ntdot(jnp.concatenate(gbs, axis=0), tile)
-
-def scan_backward(proj, mix, d, core, z, stats, start, wdt, dtb, rate, skip, gain):
+    filled = (pl.num_programs(1) - 1 - pl.program_id(1)) * length < len_ref[pl.program_id(0)]
+
+    @pl.when(jnp.logical_not(filled))
+    def _():
+        for ref in (gpre_ref, gmix_ref, gz_ref, gb_ref, gc_ref):
+            ref[...] = jnp.zeros_like(ref)
+
+    @pl.when(filled)
+    def _():
+        scale, shift = stat_ref[0, 0][:, 2:3], stat_ref[0, 0][:, 3:4]
+        d, core, z = d_ref[0, 0], core_ref[0, 0], z_ref[0, 0]
+        logistic = jax.nn.sigmoid(z)
+        gated = core * (z * logistic)
+        grad_gated = scale * (d * gain_ref[...] - gated * shift)
+        gy_ref[:, :cols] = grad_gated * (z * logistic)
+        gz_ref[0, 0] = (grad_gated * core * (logistic * (1.0 + z * (1.0 - logistic)))).astype(BF)
+        sums_ref[0:1] += jnp.sum(d * gated * scale, axis=0, keepdims=True)
+        sums_ref[1:2] += jnp.sum(gy_ref[:, :cols] * mix_ref[0, 0], axis=0, keepdims=True)
+        proj = proj_ref[0, 0].astype(F32)
+        turn_chunks(proj, bt_ref, ct_ref)
+        pre = dot(proj[:, 2 * NST :].astype(BF), wdt_ref[...]) + dtb_ref[...]
+        dt = jax.nn.softplus(pre)
+        dt_ref[:, :cols] = dt
+        u_ref[:, :cols] = dt * mix_ref[0, 0]
+        wide_ref[NST:, :cols] = start_ref[0, 0]
+        rate = wide_ref[0:NST]
+        hs_ref[0:NST] = wide_ref[NST:].astype(BF)
+
+        def ahead(k, h):
+            base = pl.multiple_of(k * CHUNK, CHUNK)
+            bt = bt_ref[k]
+            for t in range(CHUNK):
+                a = jnp.exp2(dt_ref[pl.ds(base + t, 1), :] * rate)
+                h = a * h + bt[:, t : t + 1] * u_ref[pl.ds(base + t, 1), :]
+                hs_ref[pl.ds(pl.multiple_of((base + t + 1) * NST, NST), NST), :] = h.astype(BF)
+            return h
+
+        lax.fori_loop(0, length // CHUNK, ahead, wide_ref[NST:])
+
+        def back(r, state):
+            carry, grate = state
+            k = length // CHUNK - 1 - r
+            base = pl.multiple_of(k * CHUNK, CHUNK)
+            ct = ct_ref[k]
+            qr_late = None
+            for t in reversed(range(CHUNK)):
+                at = pl.ds(pl.multiple_of((base + t) * NST, NST), NST)
+                dt_row = dt_ref[pl.ds(base + t, 1), :]
+                a = jnp.exp2(dt_row * rate)
+                g = ct[:, t : t + 1] * gy_ref[pl.ds(base + t, 1), :] + carry
+                carry = a * g
+                q = carry * hs_ref[at, :].astype(F32)
+                grate = grate + q * dt_row
+                gs_ref[at, :] = g.astype(BF)
+                qr = q * rate
+                qr = qr[:half] + qr[half:]
+                if t % 2:
+                    qr_late = qr
+                else:
+                    both = jnp.concatenate([qr, qr_late], axis=0).astype(BF)
+                    q_ref[pl.ds(pl.multiple_of((base + t) * half, NST), NST), :] = both
+            return carry, grate
+
+        carry, grate = lax.fori_loop(
+            0, length // CHUNK, back, (carry_ref[...], jnp.zeros(carry_ref.shape, F32))
+        )
+        carry_ref[...] = carry
+        grate_ref[...] += grate[:, :cols]
+        brep = dot(proj[:, :NST].astype(BF), tile)
+        gy_low = gy_ref[...].astype(BF)
+        u_low = u_ref[...].astype(BF)
+        gcs, gbs = [], []
+        for pair in range(length // CHUNK // 2):
+            gdts = dot(folded, q_ref[pair * spread : (pair + 1) * spread]) * LN2
+            for k in (2 * pair, 2 * pair + 1):
+                rows = slice(k * CHUNK, (k + 1) * CHUNK)
+                deep = slice(k * spread, (k + 1) * spread)
+                mix, dt_now, gy = mix_ref[0, 0, rows, :], dt_ref[rows, :cols], gy_ref[rows, :cols]
+                gs = gs_ref[deep]
+                gu = dot((brep[rows] * own).astype(BF), gs)[:, :cols]
+                gdt = gdts[(k % 2) * CHUNK : (k % 2 + 1) * CHUNK, :cols] + gu * mix
+                gpre = gdt * jax.nn.sigmoid(pre[rows])
+                gpre_ref[0, 0, rows, :] = gpre.astype(BF)
+                sums_ref[2:3] += jnp.sum(gpre, axis=0, keepdims=True)
+                gmix_ref[0, 0, rows, :] = gu * dt_now + skip_ref[...] * gy
+                hs = hs_ref[k * spread + NST : (k + 1) * spread + NST]
+                gcs.append((ntdot(gy_low[rows], hs) * own).astype(BF))
+                gbs.append((ntdot(u_low[rows], gs) * own).astype(BF))
+        gc_ref[0, 0] = ntdot(jnp.concatenate(gcs, axis=0), tile)
+        gb_ref[0, 0] = ntdot(jnp.concatenate(gbs, axis=0), tile)
+
+
+def scan_backward(lengths, proj, mix, d, core, z, stats, start, wdt, dtb, rate, skip, gain):
     n, seqs, length, cols = mix.shape
     wide = -(-cols // 128) * 128
     at = lambda s, i: (n - 1 - i, s, 0, 0)
@@ -246,7 +256,8 @@
     return pl.pallas_call(
         scan_bwd_kernel,
         grid=(seqs, n),
-        in_specs=[big(proj.shape[3]), big(cols), big(cols), big(cols), big(cols), big(stats.shape[3]),
+        in_specs=[pl.BlockSpec(memory_space=pltpu.SMEM),
+                  big(proj.shape[3]), big(cols), big(cols), big(cols), big(cols), big(stats.shape[3]),
                   pl.BlockSpec((1, 1, NST, cols), at)] + [whole(a) for a in (wdt, dtb, rate, skip, gain)],
         out_specs=[big(cols), big(cols), big(cols), big(NST), big(NST), whole(rate),
                    pl.BlockSpec((8, cols), lambda s, i: (0, 0))],
@@ -268,7 +279,7 @@
             pltpu.VMEM((length // CHUNK, NST, CHUNK), F32),
         ],
         compiler_params=pltpu.CompilerParams(vmem_limit_bytes=GIANT),
-    )(proj, mix, d, core, z, stats, start, wdt, dtb, rate, skip, gain)
+    )(lengths, proj, mix, d, core, z, stats, start, wdt, dtb, rate, skip, gain)
 
 
 def pick(ref, blocks, slots, slot):
@@ -286,12 +297,22 @@
     return jnp.where(lax.broadcasted_iota(jnp.int32, scores.shape, 1) <= bound, scores, NEGATIVE)
 
 
-def attn_fwd_kernel(seq, slot_ref, len_ref, q_ref, k_ref, v_ref, *refs):
-    out_ref, lse_ref = refs[-2:]
+def attn_fwd_kernel(seq, slot_ref, len_ref, rows_ref, w_ref, *refs):
+    out_ref, lse_ref, q_ref, k_ref, v_ref = refs[-5:]
     n, _, length, width = q_ref.shape
     heads, slots = width // HEAD, k_ref.shape[3] // HEAD
     group = 2
     seq_length = len_ref[seq]
+    kv_width = k_ref.shape[3]
+
+    def project(i, _):
+        y = dot(rows_ref[i, 0], w_ref[...]).astype(BF)
+        q_ref[i, 0] = y[:, :width]
+        k_ref[i, 0] = y[:, width : width + kv_width]
+        v_ref[i, 0] = y[:, width + kv_width :]
+        return 0
+
+    lax.fori_loop(0, n, project, 0)
     for i in range(n // group):
         at = slice(i * group, (i + 1) * group)
         for j in range(heads):
@@ -309,23 +330,22 @@
             lse_ref[at, 0, :, j : j + 1] = (top + jnp.log(total)).reshape(group, length, 1)
 
 
-def attn_forward(seq, slot, lengths, q, k, v, before=()):
-    n, seqs, length, width = q.shape
+def attn_forward(seq, slot, lengths, rows, w, width, before=()):
+    n, seqs, length, depth = rows.shape
+    kv_width = (w.shape[1] - width) // 2
     big = lambda w: pl.BlockSpec((n, 1, length, w), lambda s: (0, seq, 0, 0))
     smem = pl.BlockSpec(memory_space=pltpu.SMEM)
+    outs = ((width, F32), (width // HEAD, F32), (width, BF), (kv_width, BF), (kv_width, BF))
     return pl.pallas_call(
         functools.partial(attn_fwd_kernel, seq),
         grid=(1,),
-        in_specs=[smem, smem, big(width), big(k.shape[3]), big(k.shape[3])]
+        in_specs=[smem, smem, big(depth), pl.BlockSpec(w.shape, lambda s: (0, 0))]
         + [pl.BlockSpec(memory_space=pl.ANY)] * len(before),
-        out_specs=[big(width), big(width // HEAD)],
-        out_shape=[
-            jax.ShapeDtypeStruct(q.shape, F32),
-            jax.ShapeDtypeStruct((n, seqs, length, width // HEAD), F32),
-        ],
-        input_output_aliases={5: 0, 6: 1} if before else {},
+        out_specs=[big(c) for c, _ in outs],
+        out_shape=[jax.ShapeDtypeStruct((n, seqs, length, c), t) for c, t in outs],
+        input_output_aliases={4 + i: i for i in range(len(before))},
         compiler_params=pltpu.CompilerParams(vmem_limit_bytes=GIANT),
-    )(slot, lengths, q, k, v, *before)
+    )(slot, lengths, rows, w, *before)
 
 
 def attn_bwd_kernel(slot_ref, len_ref, q_ref, k_ref, v_ref, d_ref, att_ref, lse_ref, stat_ref, gain_ref,
@@ -345,7 +365,7 @@
         sums_ref[0:1] += jnp.sum(d * attended * scale, axis=0, keepdims=True)
     gk_acc[...] = jnp.zeros_like(gk_acc)
     gv_acc[...] = jnp.zeros_like(gv_acc)
-    for i in range(n // group):
+    def block(i):
         at = slice(i * group, (i + 1) * group)
         blocks = (i + 1) * group
         for j in range(heads):
@@ -367,6 +387,14 @@
             rows = slice(0, blocks * length)
             gk_acc[slot, rows] += tndot(grad_scores, queries)
             gv_acc[slot, rows] += tndot(probs.astype(BF), grad)
+
+    for i in range(n // group):
+        pl.when(i * group * length < seq_length)(functools.partial(block, i))
+
+        @pl.when(i * group * length >= seq_length)
+        def _():
+            gq_ref[i * group : (i + 1) * group] = jnp.zeros((group,) + gq_ref.shape[1:], BF)
+
     for other in range(slots):
         lanes = slice(other * HEAD, (other + 1) * HEAD)
         gk_ref[:, 0, :, lanes] = gk_acc[other].astype(BF).reshape(n, length, HEAD)
@@ -411,7 +439,7 @@
     mix = pre * jax.nn.sigmoid(pre)
     mix_ref[0, 0] = mix
     low_ref[0, 0] = mix.astype(BF)
-    part_ref[0, 0] = ntdot(mix.astype(BF), xp_ref[...])
+    part_ref[0, 0] = ntdot(mix.astype(BF), xp_ref[...]).astype(BF)
 
 
 def signal_forward(rows, wx, taps, bias, xp):
@@ -425,7 +453,7 @@
         grid=(seqs, n),
         in_specs=[big(width), whole(wx), whole(taps), whole(bias), whole(xp)],
         out_specs=[big(cols)] * 4 + [big(xp.shape[0])],
-        out_shape=[shape(cols, BF), shape(cols, F32), shape(cols, F32), shape(cols, BF), shape(xp.shape[0], F32)],
+        out_shape=[shape(cols, BF), shape(cols, F32), shape(cols, F32), shape(cols, BF), shape(xp.shape[0], BF)],
         scratch_shapes=[pltpu.VMEM((length + 8, cols), F32)],
         compiler_params=pltpu.CompilerParams(vmem_limit_bytes=GIANT),
     )(rows, wx, taps, bias, xp)
@@ -1387,28 +1415,25 @@
         tokens.reshape(local, width), norm_in, w_qkv, plan.moves(), plan.width + 2 * plan.kv_width, w_in, n, 1
     )
     normed, qkv_cols = flat(normed), qkv_cols.reshape(n * w_rows, -1)
-    qkv = dot(normed, qkv_cols).astype(BF)
     wx, wz = exchange(in_x), exchange(in_z)
-    behind = 0.0 * qkv[0, 0].astype(F32)
+    heads = attn_forward(0, table, lengths, blocks(normed), qkv_cols, plan.width)
+    behind = nothing(heads[1])
+    for seq in range(1, seqs):
+        heads = attn_forward(seq, table, lengths, blocks(normed), qkv_cols, plan.width, heads)
+    attended, lse, q, k, v = heads
     ao_all = lax.all_gather(later(w_ao, behind), "seq", axis=0, tiled=True)
     ao_mine = lax.dynamic_slice_in_dim(
         jnp.pad(ao_all, ((0, n * plan.width - HEADS * HEAD), (0, 0))), me * plan.width, plan.width, 0
     )
     upstream = (cotangent.astype(F32) * is_valid[..., None]).reshape(local, width)
     upstream_all = lax.all_gather(later(upstream.astype(BF), behind), "seq", axis=0, tiled=True)
-    q = blocks(qkv[:, : plan.width])
-    k = blocks(qkv[:, plan.width : plan.width + plan.kv_width])
-    v = blocks(qkv[:, plan.width + plan.kv_width :])
-    attended, lse = attn_forward(0, table, lengths, q, k, v)
-    for seq in range(1, seqs):
-        attended, lse = attn_forward(seq, table, lengths, q, k, v, (attended, lse))
     wx = later(wx, nothing(lse)).reshape(n * w_rows, cols)
     wz = wz.reshape(n * w_rows, cols)
     xp = jnp.swapaxes(w_xp, 0, 1)
     xp = jnp.concatenate([xp[DTR:], xp[:DTR]], axis=0)
     x_conv, conv_pre, mixer_in, mixer_low, projected = signal_forward(blocks(normed), wx, taps, bias[None], xp)
     mixer_low = flat(mixer_low)
-    projected = blocks(gather(scatter(flat(projected), 15).astype(BF), 16)).astype(F32)
+    projected = blocks(gather(scatter(flat(projected), 15).astype(BF), 16))
     core, z_gate, ssm_sq, start = scan_forward(
         projected, mixer_in, blocks(normed), wz, wdt, dtb[None], rate, skip[None]
     )
@@ -1476,7 +1501,7 @@
             table, lengths, q, k, v, blocks(d_attn), attended, lse, stats, attn_gain[None]
         )
         gpre, gmix, gz, gb, gc, grate, channel_sums = scan_backward(
-            projected, mixer_in, blocks(d_ssm), core, z_gate, stats, start, wdt, dtb[None], rate, skip[None],
+            lengths, projected, mixer_in, blocks(d_ssm), core, z_gate, stats, start, wdt, dtb[None], rate, skip[None],
             ssm_gain[None],
         )
         grad_qkv, grad_z = flat(jnp.concatenate([gq, gk, gv], axis=3)), flat(gz)
@@ -1496,10 +1521,11 @@
     g_z = jnp.swapaxes(g_z, 0, 1).reshape(w_rows, INNER)
     g_qkv = exchange(g_qkv.reshape(n, w_rows, -1))
     g_qkv = plan.join_columns(g_qkv).astype(BF)
-    after_one = nothing(s_down, s_gate, s_up, grate)
+    first_sums = nothing(s_down, s_gate, s_up)
+    grad_projected = jnp.concatenate([gb, gc, ntdot(grad_step, wdt)], axis=1)
+    grad_projected = gather(scatter(grad_projected, 9, mark(first_sums)).astype(BF), 10)
+    after_one = first_sums + nothing(grad_projected)
     s_ao, s_so, s_qkv, s_z = over(tuple(later(g, after_one) for g in (g_ao, g_so, g_qkv, g_z)))
-    grad_projected = jnp.concatenate([gb, gc, ntdot(grad_step, wdt)], axis=1)
-    grad_projected = gather(scatter(grad_projected, 9, mark(after_one)).astype(BF), 10)
 
     def signal_back(_):
         grad_x, sums = signal_backward(gmix, blocks(grad_projected), xp, conv_pre, x_conv, taps)
@@ -1509,7 +1535,7 @@
             sums,
             tndot(normed, grad_x).astype(BF),
             tndot(grad_projected, mixer_low).astype(BF),
-            tndot(grad_step, flat(projected)[:, 2 * NST :].astype(BF)).astype(BF),
+            tndot(grad_step, flat(projected)[:, 2 * NST :]).astype(BF),
         )
 
     grad_x, tap_sums, g_x, g_xp, g_wdt = one_step(signal_back)

time: 1070 us -> 1070 us (level)
  matrix products: 73.8 us -> 61.4 us
    pallas_call x4, Pallas kernels: 42.5 us -> 66.2 us  [small_sum(): pl.pallas_call(functools.partial(stat_kernel, n, axis), out_shape=jax.Sha...]
    pallas_call x1, Pallas kernels: 92.6 us -> 74.3 us  [scan_backward(): pl.pallas_call(scan_bwd_kernel, grid=(seqs, n), in_specs=[pl.BlockSpec(me...]
    pallas_call x2, Pallas kernels: 34.5 us -> 23.6 us  [reduce_scatter4(): pl.pallas_call(rs4_kernel, out_shape=jax.ShapeDtypeStruct(blk, F32), in_s...]
  transfers between devices with their start and end apart: 11 -> 11, of which waited for: 2 -> 2; matrix products, arithmetic and copies ran while one was open for 18% -> 19% of each run, Pallas kernels for 56% -> 54%
where the time goes in v3:
time: 1070 us; the launch traced here: 1060 us
  Pallas kernels  711 us (66%)
  local copies, waits for them, and re-layouts  150 us (14%)
  other arithmetic  72.8 us (7%)
  matrix products  61.4 us (6%)
  starting transfers between devices  27.3 us (3%)
  between operations  23.9 us (2%)
    pallas_call x4, Pallas kernels, product_scatter(): pl.pallas_call(functools.partial(mm_rs4_kernel, tuple((t for _, _, t in p...  164 us
    pallas_call x2, Pallas kernels, gather_product(): pl.pallas_call(functools.partial(gather_product4_kernel, body, len(weight...  85 us
    pallas_call x1, Pallas kernels, scan_backward(): pl.pallas_call(scan_bwd_kernel, grid=(seqs, n), in_specs=[pl.BlockSpec(me...  74.3 us
    pallas_call x4, Pallas kernels, small_sum(): pl.pallas_call(functools.partial(stat_kernel, n, axis), out_shape=jax.Sha...  66.2 us
    dot_general x10, matrix products, tndot(): return lax.dot_general(a, b, TN, preferred_element_type=F32)  60.6 us
    pallas_call x1, Pallas kernels, gather_and_exchange(): pl.pallas_call(functools.partial(start_kernel, n, moves), out_shape=[jax....  57.2 us
    pallas_call x1, Pallas kernels, chain_sum(): pl.pallas_call(functools.partial(chain_kernel, axis, count, tuple(cuts)),...  52 us
    pallas_call x1, Pallas kernels, scan_forward(): pl.pallas_call(scan_fwd_kernel, grid=(seqs, n), in_specs=[big(proj.shape[...  41.8 us
  transfers between devices with their start and end apart: 11, of which 2 were waited for; matrix products, arithmetic and copies ran while one was open for 19% of the time, Pallas kernels for 54%

profile of v3, /device:TPU:0, one launch (start us, length us, event | category | flops | bytes accessed | tf_op | source)
XLA Modules:
  0.0 1057.6 jit_solution(13196019381169711737)
XLA Ops:
  11.5 57.2 %shard_map.357 = (bf16[8,256,1600]{2,1,0:T(8,128)(2,1)}, bf16[8,200,512]{2,1,0:T(8,128)(2,1)}, bf16[8,200,400]{2,1,0:T(8,128)(2,1)}, bf16[8,200,400]{2,1,0:T(8,128)(2,1)}) custom-call(bf16[256,1600]{1,0:T(8,128)(2,1)} %bitcast.252, f32[1,1600]{1,0:T(1,128)} %broadcast_in_dim.62.gain_ref, bf16[200,2240]{1,0:T(8,128)(2,1)} %w_ref.1, bf16[200,6400]{1,0:T(8,128)(2,1)} %in_ref.1), custom_call_target="tpu_custom_call" | custom-call | tf_op jit(solution)/shard_map/pallas_call | solution.py:886
  68.7 20.5 %shard_map.358 = (f32[8,2,128,256]{3,2,1,0:T(8,128)S(1)}, f32[8,2,128,4]{3,2,1,0:T(8,128)}, bf16[8,2,128,256]{3,2,1,0:T(8,128)(2,1)}, bf16[8,2,128,128]{3,2,1,0:T(8,128)(2,1)S(1)}, bf16[8,2,128,128]{3,2,1,0:T(8,128)(2,1)}) custom-call(s32[8]{0:T(128)S(1)} %fusion.33.slot_ref, s32[2]{0:T(128)S(1)} %copy-done.49, bf16[8,2,128,1600]{3,2,1,0:T(8,128)(2,1)} %bitcast.216, ...), custom_call_target="tpu_custom_call" | custom-call | tf_op jit(solution)/shard_map/pallas_call | solution.py:339
  96.8 2.7 copy.103
  102.0 4.5 all-to-all-start
  106.5 20.6 %shard_map.359 = (f32[8,2,128,256]{3,2,1,0:T(8,128)S(1)}, f32[8,2,128,4]{3,2,1,0:T(8,128)}, bf16[8,2,128,256]{3,2,1,0:T(8,128)(2,1)}, bf16[8,2,128,128]{3,2,1,0:T(8,128)(2,1)S(1)}, bf16[8,2,128,128]{3,2,1,0:T(8,128)(2,1)}) custom-call(s32[8]{0:T(128)S(1)} %fusion.33.slot_ref, ...), custom_call_target="tpu_custom_call", output_to_operand_aliasing={{0}: (4, {}), {1}: (5, {}), {2}: (6, {}), {3}: (7, {}), {4}... | custom-call | tf_op jit(solution)/shard_map/pallas_call | solution.py:339
  129.8 3.4 all-to-all-done
  133.2 4.7 all-to-all-start.1
  147.2 4.8 slice_bitcast_fusion
  151.9 2.7 broadcast_add_fusion
  154.6 18.3 %shard_map.360 = (bf16[8,2,128,400]{3,2,1,0:T(8,128)(2,1)}, f32[8,2,128,400]{3,2,1,0:T(8,128)}, f32[8,2,128,400]{3,2,1,0:T(8,128)}, bf16[8,2,128,400]{3,2,1,0:T(8,128)(2,1)}, bf16[8,2,128,132]{3,2,1,0:T(8,128)(2,1)}) custom-call(bf16[8,2,128,1600]{3,2,1,0:T(8,128)(2,1)} %bitcast.218, bf16[1600,400]{1,0:T(8,128)(2,1)} %bitcast.232, ...), custom_call_target="tpu_custom_call" | custom-call | tf_op jit(solution)/shard_map/pallas_call | solution.py:451
  173.5 12.4 %shard_map.361 = f32[256,132]{1,0:T(8,128)} custom-call(bf16[8,256,132]{2,1,0:T(8,128)(2,1)} %bitcast.258, f32[8,128]{1,0:T(8,128)} %broadcast_47_after_ref_refs_4__refs_6_.2.after_ref.refs_4_.refs_6_), custom_call_target="tpu_custom_call" | custom-call | tf_op jit(solution)/shard_map/pallas_call | solution.py:833
  187.5 14.3 %shard_map.362 = bf16[8,256,132]{2,1,0:T(8,128)(2,1)} custom-call(bf16[256,132]{1,0:T(8,128)(2,1)} %convert_element_type.261.x_ref), custom_call_target="tpu_custom_call" | custom-call | tf_op jit(solution)/shard_map/pallas_call | solution.py:760
  201.9 41.8 %shard_map.363 = (f32[8,2,128,400]{3,2,1,0:T(8,128)}, f32[8,2,128,400]{3,2,1,0:T(8,128)}, f32[8,2,128,1]{3,2,1,0:T(8,128)}, f32[8,2,16,400]{3,2,1,0:T(8,128)}) custom-call(bf16[8,2,128,132]{3,2,1,0:T(8,128)(2,1)} %bitcast.237, f32[8,2,128,400]{3,2,1,0:T(8,128)} %get-tuple-element.265.mix_ref, bf16[8,2,128,1600]{3,2,1,0:T(8,128)(2,1)} %bitcast.219, ...), custom_call_target="tpu_custom_call" | custom-call | tf_op jit(solution)/shard_map/pallas_call | solution.py:117
  245.9 6.2 shard_map.364
  254.2 7.8 shard_map.365
  264.2 38.1 %shard_map.366 = f32[256,1600]{1,0:T(8,128)} custom-call(bf16[8,256,256]{2,1,0:T(8,128)(2,1)} %get-tuple-element.270.refs_0_, bf16[8,256,400]{2,1,0:T(8,128)(2,1)} %get-tuple-element.271.refs_1_, bf16[256,1600]{1,0:T(8,128)(2,1)} %pad_dynamic-slice_fusion.refs_2_.refs_0_, bf16[400,1600]{1,0:T(8,128)(2,1)} %refs_1_.2, ...), custom_call_target="tpu_custom_call" | custom-call | tf_op jit(solution)/shard_map/pallas_call | solution.py:1029
  307.0 42.1 %shard_map.367 = (bf16[8,256,1600]{2,1,0:T(8,128)(2,1)}, bf16[8,256,688]{2,1,0:T(8,128)(2,1)}, bf16[8,256,688]{2,1,0:T(8,128)(2,1)}, bf16[8,256,688]{2,1,0:T(8,128)(2,1)}) custom-call(bf16[256,1600]{1,0:T(8,128)(2,1)} %multiply_convert_fusion.x_ref, bf16[688,1600]{1,0:T(8,128)(2,1)} %get-tuple-element.471.refs_0_.refs_2_, ...), custom_call_target="tpu_custom_call" | custom-call | tf_op jit(solution)/shard_map/pallas_call | solution.py:1273
  349.1 13.8 %shard_map.368 = (bf16[8,256,688]{2,1,0:T(8,128)(2,1)}, bf16[8,256,688]{2,1,0:T(8,128)(2,1)}) custom-call(bf16[8,256,1600]{2,1,0:T(8,128)(2,1)} %bitcast.243, bf16[688,1600]{1,0:T(8,128)(2,1)} %refs_1_.3, bf16[8,256,688]{2,1,0:T(8,128)(2,1)} %get-tuple-element.273.gate_ref, bf16[8,256,688]{2,1,0:T(8,128)(2,1)} %get-tuple-element.274.up_ref), custom_call_target="tpu_custom_call" | custom-call | tf_op jit(solution)/shard_map/pallas_call | solution.py:545
  362.9 10.7 %bitcast_convert_fusion.1 = bf16[688,1600]{1,0:T(8,128)(2,1)} fusion(bf16[8,256,688]{2,1,0:T(8,128)(2,1)} %get-tuple-element.275.refs_0_, bf16[8,256,1600]{2,1,0:T(8,128)(2,1)} %get-tuple-element.277), kind=kOutput, calls=%fused_computation.22 | convolution fusion | flops 4509977600 | bytes 11573248 | tf_op jit(solution)/shard_map/dot_general | solution.py:37
  373.7 7.0 bitcast_convert_fusion
  380.7 7.4 convolution_convert_fusion.5
  388.1 5.4 reshape.560
  393.5 5.4 reshape.561
  404.0 43.4 %shard_map.369 = f32[256,1600]{1,0:T(8,128)} custom-call(bf16[8,256,688]{2,1,0:T(8,128)(2,1)} %get-tuple-element.275.refs_0_, bf16[8,256,688]{2,1,0:T(8,128)(2,1)} %get-tuple-element.276.refs_1_, bf16[688,1600]{1,0:T(8,128)(2,1)} %get-tuple-element.471.refs_0_.refs_2_, bf16[688,1600]{1,0:T(8,128)(2,1)} %get-tuple-element.470.refs_1_.refs_3_, ...), custom_call_target="tpu_custom_call" | custom-call | tf_op jit(solution)/shard_map/pallas_call | solution.py:1029
  450.4 3.4 fusion.35
  453.8 42.9 %shard_map.370 = (bf16[8,256,1600]{2,1,0:T(8,128)(2,1)}, f32[8,256,256]{2,1,0:T(8,128)}, f32[8,256,400]{2,1,0:T(8,128)}, f32[8,256,2]{2,1,0:T(8,128)}) custom-call(bf16[256,1600]{1,0:T(8,128)(2,1)} %get-tuple-element.463.x_ref, bf16[256,1600]{1,0:T(8,128)(2,1)} %pad_dynamic-slice_fusion.refs_2_.refs_0_, bf16[400,1600]{1,0:T(8,128)(2,1)} %refs_1_.2, ...), custom_call_target="tpu_custom_call" | custom-call | tf_op jit(solution)/shard_map/pallas_call | solution.py:1273
  496.7 3.3 fusion.37
  503.7 6.8 shard_map.371
  511.8 141.0 %conditional.2 = (f32[256]{0:T(256)S(1)}, bf16[2048,400]{1,0:T(8,128)(2,1)S(1)}, f32[8,2,128,400]{3,2,1,0:T(8,128)}, f32[16,400]{1,0:T(8,128)}, bf16[400,1600]{1...) conditional(s32[]{:T(128)} %bitcast.51, () %tuple.46, ...), branch_computations={%region_3.4_spmd, %region_4.5_spmd} | conditional | flops 10279668736 | bytes 105777616 | solution.py:1398
  514.0 27.3 %branch_1_fun.5 = (bf16[8,2,128,256]{3,2,1,0:T(8,128)(2,1)}, bf16[8,2,128,128]{3,2,1,0:T(8,128)(2,1)}, bf16[8,2,128,128]{3,2,1,0:T(8,128)(2,1)}, f32[8,256]{1,0:T(8,128)}) custom-call(s32[8]{0:T(128)} %get-tuple-element.126.slot_ref, s32[2]{0:T(128)} %get-tuple-element.127.len_ref, bf16[8,2,128,256]{3,2,1,0:T(8,128)(2,1)} %get-tuple-element.128.q_ref, ...), custom_call_target="tpu_custom_call" | custom-call | tf_op jit(solution)/shard_map/cond/branch_1_fun/pallas_call | solution.py:410
  542.0 74.3 %branch_1_fun.6 = (bf16[8,2,128,400]{3,2,1,0:T(8,128)(2,1)S(1)}, f32[8,2,128,400]{3,2,1,0:T(8,128)}, bf16[8,2,128,400]{3,2,1,0:T(8,128)(2,1)}, f32[8,2,128,16]{3...) custom-call(s32[2]{0:T(128)S(1)} %copy-done.51, ...), custom_call_target="tpu_custom_call" | custom-call | tf_op jit(solution)/shard_map/cond/branch_1_fun/pallas_call | solution.py:256
  616.4 8.0 fusion.1
  624.3 8.0 fusion.4
  635.3 6.5 fusion.2
  644.0 3.7 fusion.5
  652.9 4.4 all-to-all-start.2
  659.1 2.7 constant_dynamic-slice_fusion.2
  663.5 3.1 collective-permute-start
  666.6 3.4 copy.127
  670.0 2.8 pad_maximum_fusion.1.p_ref
  672.8 6.3 all-to-all-done.2
  679.1 4.3 all-to-all-start.4
  694.6 5.6 reshape.565
  701.4 4.2 reshape.566
  706.8 4.4 reshape.567
  714.3 11.2 %shard_map.372 = f32[256,132]{1,0:T(8,128)} custom-call(bf16[8,256,132]{2,1,0:T(8,128)(2,1)} %pad_maximum_fusion.1.p_ref, f32[8,128]{1,0:T(8,128)} %broadcast_in_dim.69.after_ref), custom_call_target="tpu_custom_call" | custom-call | tf_op jit(solution)/shard_map/pallas_call | solution.py:833
  727.1 9.4 shard_map.373
  745.5 4.4 add.353
  750.9 3.4 add_add_fusion
  757.5 25.8 %conditional.3 = (bf16[1600,400]{0,1:T(8,128)(2,1)}, bf16[132,400]{1,0:T(8,128)(2,1)S(1)}, bf16[400,100]{1,0:T(8,128)(2,1)S(1)}, bf16[8,256,400]{2,1,0:T(8,128)(2,1)}, f32[5,400]{1,0:T(8,128)S(1)}) conditional(s32[]{:T(128)} %bitcast.51, () %tuple.45, (bf16[8,256,132]{2,1,0:T(8,128)(2,1)S(1)}, f32[8,2,128,400]{3,2,1,0:T(8,128)}, ...), branch_computations={%region_8.9_spmd, %region_9.10_spmd} | conditional | flops 3002281472 | bytes 27565408 | solution.py:1398
  757.5 15.3 %branch_1_fun.7 = (bf16[8,2,128,400]{3,2,1,0:T(8,128)(2,1)}, f32[8,400]{1,0:T(8,128)S(1)}) custom-call(f32[8,2,128,400]{3,2,1,0:T(8,128)} %get-tuple-element.162.gmix_ref, bf16[8,2,128,132]{3,2,1,0:T(8,128)(2,1)S(1)} %bitcast.230, bf16[132,400]{1,0:T(8,128)(2,1)S(1)} %get-tuple-element.164.xp_ref, f32[8,2,128,400]{3,2,1,0:T(8,128)} %get-tuple-element.165.pre_ref, ...), custom_call_target="tpu_custom_call" | custom-call | tf_op jit(solution)/shard_map/cond/branch_1_fun/pallas_call | solution.py:498
  772.8 8.0 fusion.6
  783.3 43.9 %shard_map.374 = f32[256,1600]{1,0:T(8,128)} custom-call(bf16[8,256,400]{2,1,0:T(8,128)(2,1)} %get-tuple-element.296.refs_0_, bf16[8,256,400]{2,1,0:T(8,128)(2,1)} %get-tuple-element.297.refs_1_, bf16[8,256,512]{2,1,0:T(8,128)(2,1)} %get-tuple-element.298.refs_2_, bf16[1600,400]{1,0:T(8,128)(2,1)} %bitcast.233, bf16[1600,400]{1,0:T(8,128)(2,1)} %bitcast.37.wz_ref.refs_4_, ...), custom_call_target="tpu_custom_call" | custom-call | tf_op jit(solution)/shard_map/pallas_call | solution.py:1029
  831.2 38.1 %shard_map.375 = f32[256,1600]{1,0:T(8,128)} custom-call(bf16[8,256,688]{2,1,0:T(8,128)(2,1)} %get-tuple-element.272.refs_0_, bf16[688,1600]{1,0:T(8,128)(2,1)} %refs_1_.3, f32[8,128]{1,0:T(8,128)} %broadcast_in_dim.70.refs_2_), custom_call_target="tpu_custom_call" | custom-call | tf_op jit(solution)/shard_map/pallas_call | solution.py:1029
  869.3 3.5 copy.125
  872.8 4.4 all-to-all-start.3
  880.6 20.0 %shard_map.377 = f32[40,128]{1,0:T(8,128)} custom-call(f32[40,128]{1,0:T(8,128)} %pad_bitcast_fusion.x_ref), custom_call_target="tpu_custom_call" | custom-call | tf_op jit(solution)/shard_map/pallas_call | solution.py:691
  901.4 3.3 fusion.34
  910.8 33.3 %shard_map.378 = f32[80,128]{1,0:T(8,128)} custom-call(f32[80,128]{1,0:T(8,128)} %fusion.32.x_ref), custom_call_target="tpu_custom_call" | custom-call | tf_op jit(solution)/shard_map/pallas_call | solution.py:691
  949.4 3.4 reshape.574
  958.2 5.9 convert_bitcast_fusion
  966.1 3.0 reshape.573.refs_0_
  988.6 52.0 %shard_map.376 = (f32[200,3200]{1,0:T(8,128)}, f32[132,400]{1,0:T(8,128)}, f32[400,100]{1,0:T(8,128)}) custom-call(bf16[200,3200]{1,0:T(8,128)(2,1)} %reshape.573.refs_0_, bf16[132,400]{1,0:T(8,128)(2,1)S(1)} %get-tuple-element.302.refs_1_, bf16[400,100]{1,0:T(8,128)(2,1)S(1)} %copy-done.36, f32[8,128]{1,0:T(8,128)} %broadcast_in_dim.72.refs_3_), custom_call_target="tpu_custom_call" | custom-call | tf_op jit(solution)/shard_map/pallas_call | solution.py:1162
  1045.1 4.4 pad_maximum_fusion
  (298 shorter events, 145.9 us)
Async XLA Ops:
  7.2 122.2 %copy-start = (bf16[100,3200]{1,0:T(8,128)(2,1)S(1)}, bf16[100,3200]{1,0:T(8,128)(2,1)}, u32[]{:S(2)}) copy-start(bf16[100,3200]{1,0:T(8,128)(2,1)} %param.33) | copy-start | bytes 1920004
  7.2 254.7 %all-gather.3.cloned.1.call-start = ((), (), s32[]{:S(2)}) async-start(), calls=%async_computation.5 | async-start | bytes 5990400 | tf_op jit(solution)/shard_map/all_gather | solution.py:1424
  11.5 95.0 %copy-start.59 = (s32[8]{0:T(128)}, s32[8]{0:T(128)S(1)}, u32[]{:S(2)}) copy-start(s32[8]{0:T(128)S(1)} %fusion.33.slot_ref) | copy-start | bytes 100
  11.5 57.2 %copy-start.49 = (s32[2]{0:T(128)S(1)}, s32[2]{0:T(128)}, u32[]{:S(2)}) copy-start(s32[2]{0:T(128)} %len_ref.3) | copy-start | bytes 28
  94.3 254.9 %all-gather.5.cloned.1.call-start = ((), (), s32[]{:S(2)}) async-start(), calls=%async_computation.6 | async-start | bytes 7667712 | tf_op jit(solution)/shard_map/all_gather | solution.py:1429
  102.0 31.2 %all-to-all-start = ((bf16[8,200,400]{2,1,0:T(8,128)(2,1)}), bf16[8,200,400]{2,1,0:T(8,128)(2,1)}, u32[]{:S(2)}, u32[]{:S(2)}) async-start(bf16[8,200,400]{2,1,0:T(8,128)(2,1)} %get-tuple-element.262), calls=%async_computation | async-start | bytes 3276800 | tf_op jit(solution)/shard_map/all_to_all | solution.py:1390
  129.8 8.1 copy-start.58
  129.8 8.2 copy-start.41
  133.2 68.7 %all-to-all-start.1 = ((bf16[8,200,400]{2,1,0:T(8,128)(2,1)}), bf16[8,200,400]{2,1,0:T(8,128)(2,1)}, u32[]{:S(2)}, u32[]{:S(2)}) async-start(bf16[8,200,400]{2,1,0:T(8,128)(2,1)} %get-tuple-element.266), calls=%async_computation.1 | async-start | bytes 3276800 | tf_op jit(solution)/shard_map/all_to_all | solution.py:1390
  145.6 56.3 %copy-start.45 = (f32[400]{0:T(512)}, f32[400]{0:T(512)S(1)}, u32[]{:S(2)}) copy-start(f32[400]{0:T(512)S(1)} %dynamic_slice.49) | copy-start | bytes 4804
  146.4 55.5 %copy-start.47 = (f32[400]{0:T(512)}, f32[400]{0:T(512)S(1)}, u32[]{:S(2)}) copy-start(f32[400]{0:T(512)S(1)} %dynamic_slice.51) | copy-start | bytes 4804
  172.9 29.0 %copy-start.37 = (f32[16,400]{1,0:T(8,128)S(1)}, f32[16,400]{1,0:T(8,128)}, u32[]{:S(2)}) copy-start(f32[16,400]{1,0:T(8,128)} %exponential_negate_fusion.rate_ref) | copy-start | bytes 76804
  302.3 3.5 copy-start.43
  362.9 10.8 %copy-start.23 = (bf16[8,256,688]{2,1,0:T(8,128)(2,1)S(1)}, bf16[8,256,688]{2,1,0:T(8,128)(2,1)}, u32[]{:S(2)}) copy-start(bf16[8,256,688]{2,1,0:T(8,128)(2,1)} %get-tuple-element.276.refs_1_) | copy-start | bytes 8454148
  362.9 10.8 %copy-start.62 = (bf16[8,256,1600]{2,1,0:T(8,128)(2,1)S(1)}, bf16[8,256,1600]{2,1,0:T(8,128)(2,1)}, u32[]{:S(2)}) copy-start(bf16[8,256,1600]{2,1,0:T(8,128)(2,1)} %get-tuple-element.277) | copy-start | bytes 19660804
  362.9 17.7 %slice-start.2 = ((s8[6815744]{0:T(1024)(128)(4,1)}), s8[4194304]{0:T(1024)(128)(4,1)S(1)}, s32[]{:S(2)}) async-start(s8[6815744]{0:T(1024)(128)(4,1)} %bitcast.244), calls=%async_computation.11 | async-start | bytes 8388608
  373.7 7.0 slice-start.3
  373.7 7.0 copy-start.22
  399.0 295.6 %all-reduce.13.cloned.1.call-start = ((), (), s32[]{:S(2)}) async-start(), calls=%async_computation.8 | async-start | bytes 13737984 | tf_op jit(solution)/shard_map/psum | solution.py:1393
  447.5 3.0 copy-start.7
  511.8 29.5 %copy-start.38 = (f32[16,400]{1,0:T(8,128)}, f32[16,400]{1,0:T(8,128)S(1)}, u32[]{:S(2)}) copy-start(f32[16,400]{1,0:T(8,128)S(1)} %get-tuple-element.145.rate_ref) | copy-start | bytes 76804 | tf_op jit(solution)/shard_map/cond
  513.9 28.1 %copy-start.10 = (bf16[8,2,128,132]{3,2,1,0:T(8,128)(2,1)S(1)}, bf16[8,2,128,132]{3,2,1,0:T(8,128)(2,1)}, u32[]{:S(2)}) copy-start(bf16[8,2,128,132]{3,2,1,0:T(8,128)(2,1)} %get-tuple-element.137.proj_ref) | copy-start | bytes 1622020 | tf_op jit(solution)/shard_map/cond
  513.9 28.1 %copy-start.46 = (f32[400]{0:T(512)S(1)}, f32[400]{0:T(512)}, u32[]{:S(2)}) copy-start(f32[400]{0:T(512)} %get-tuple-element.144) | copy-start | bytes 4804 | tf_op jit(solution)/shard_map/cond
  514.0 28.1 %copy-start.48 = (f32[400]{0:T(512)S(1)}, f32[400]{0:T(512)}, u32[]{:S(2)}) copy-start(f32[400]{0:T(512)} %get-tuple-element.146) | copy-start | bytes 4804 | tf_op jit(solution)/shard_map/cond
  514.0 28.1 %copy-start.51 = (s32[2]{0:T(128)S(1)}, s32[2]{0:T(128)}, u32[]{:S(2)}) copy-start(s32[2]{0:T(128)} %get-tuple-element.127.len_ref) | copy-start | bytes 28 | tf_op jit(solution)/shard_map/cond
  616.4 18.9 %slice-start = ((s8[6815744]{0:T(1024)(128)(4,1)}), s8[4194304]{0:T(1024)(128)(4,1)S(1)}, s32[]{:S(2)}) async-start(s8[6815744]{0:T(1024)(128)(4,1)} %bitcast.222), calls=%async_computation.9 | async-start | bytes 8388608 | tf_op jit(solution)/shard_map/cond
  624.3 8.0 copy-start.31
  624.3 10.9 %slice-start.1 = ((s8[6815744]{0:T(1024)(128)(4,1)}), s8[2621440]{0:T(1024)(128)(4,1)S(1)}, s32[]{:S(2)}) async-start(s8[6815744]{0:T(1024)(128)(4,1)} %bitcast.222), calls=%async_computation.10 | async-start | bytes 5242880 | tf_op jit(solution)/shard_map/cond
  635.2 8.7 slice-start.4
  635.3 7.4 copy-start.30
  635.3 8.7 slice-start.5
  652.8 5.2 copy-start.26
  652.8 5.9 copy-start.14
  652.8 5.9 copy-start.52
  652.8 5.9 copy-start.54
  652.9 5.9 copy-start.56
  652.9 5.9 copy-start.60
  652.9 4.5 copy-start.63
  652.9 26.2 %all-to-all-start.2 = ((bf16[8,200,512]{2,1,0:T(8,128)(2,1)}), bf16[8,200,512]{2,1,0:T(8,128)(2,1)}, u32[]{:S(2)}, u32[]{:S(2)}) async-start(bf16[8,200,512]{2,1,0:T(8,128)(2,1)} %bitcast.72), calls=%async_computation.2 | async-start | bytes 3276800 | tf_op jit(solution)/shard_map/all_to_all | solution.py:1390
  661.8 8.2 copy-start.27
  661.8 89.1 %collective-permute-start.1 = (bf16[200,1600]{1,0:T(8,128)(2,1)}, bf16[200,1600]{1,0:T(8,128)(2,1)}, u32[]{:S(2)}, u32[]{:S(2)}) collective-permute-start(bf16[200,1600]{1,0:T(8,128)(2,1)} %get-tuple-element.473), channel_id=1, source_target_pairs={{3,5},{4,6},{5,7},{11,13},{12,14},{13,15},{19,21},{20,22},{21,23},... | collective-permute-start | bytes 1920008 | tf_op jit(solution)/shard_map/ppermute | solution.py:1362
  663.5 87.5 %collective-permute-start = (bf16[200,1600]{1,0:T(8,128)(2,1)}, bf16[200,1600]{1,0:T(8,128)(2,1)}, u32[]{:S(2)}, u32[]{:S(2)}) collective-permute-start(bf16[200,1600]{1,0:T(8,128)(2,1)} %get-tuple-element.472), channel_id=1, source_target_pairs={{0,1},{1,2},{2,3},{3,4},{4,5},{5,6},{6,7},{8,9},{9,10},{10,11},{11... | collective-permute-start | bytes 1920008 | tf_op jit(solution)/shard_map/ppermute | solution.py:1362
  679.1 63.2 %all-to-all-start.4 = ((bf16[8,200,400]{2,1,0:T(8,128)(2,1)}), bf16[8,200,400]{2,1,0:T(8,128)(2,1)}, u32[]{:S(2)}, u32[]{:S(2)}) async-start(bf16[8,200,400]{2,1,0:T(8,128)(2,1)} %bitcast.94), calls=%async_computation.4 | async-start | bytes 3276800 | tf_op jit(solution)/shard_map/all_to_all | solution.py:1390
  683.4 285.7 %all-reduce.11.cloned.1.call-start = ((), (), s32[]{:S(2)}) async-start(), calls=%async_computation.7 | async-start | bytes 8396800 | tf_op jit(solution)/shard_map/psum | solution.py:1393
  694.6 6.8 copy-start.11
  745.5 4.4 copy-start.20
  754.4 3.1 copy-start.9
  772.8 8.0 copy-start.28
  783.3 43.9 %copy-start.35 = (bf16[400,100]{1,0:T(8,128)(2,1)}, bf16[400,100]{1,0:T(8,128)(2,1)S(1)}, u32[]{:S(2)}) copy-start(bf16[400,100]{1,0:T(8,128)(2,1)S(1)} %get-tuple-element.303.refs_2_) | copy-start | bytes 240004
  872.8 4.4 copy-start.44
  872.8 91.3 %all-to-all-start.3 = ((bf16[8,200,400]{2,1,0:T(8,128)(2,1)}), bf16[8,200,400]{2,1,0:T(8,128)(2,1)}, u32[]{:S(2)}, u32[]{:S(2)}) async-start(bf16[8,200,400]{2,1,0:T(8,128)(2,1)} %bitcast.92), calls=%async_computation.3 | async-start | bytes 3276800 | tf_op jit(solution)/shard_map/all_to_all | solution.py:1390
  877.3 24.1 %copy-start.4 = (f32[256,1600]{1,0:T(8,128)S(1)}, f32[256,1600]{1,0:T(8,128)}, u32[]{:S(2)}) copy-start(f32[256,1600]{1,0:T(8,128)} %copy-done.2) | copy-start | bytes 4915204
  901.4 3.3 copy-start.5
  901.4 3.3 copy-start.6
  901.4 3.6 copy-start.16
  909.7 38.1 %copy-start.17 = (f32[256,1600]{1,0:T(8,128)S(1)}, f32[256,1600]{1,0:T(8,128)}, u32[]{:S(2)}) copy-start(f32[256,1600]{1,0:T(8,128)} %fusion.11) | copy-start | bytes 4915204
  949.4 8.8 copy-start.12
  969.1 3.2 copy-start.21
  972.3 3.3 copy-start.19
  977.3 3.1 copy-start.18
  977.3 11.3 %copy-start.36 = (bf16[400,100]{1,0:T(8,128)(2,1)S(1)}, bf16[400,100]{1,0:T(8,128)(2,1)}, u32[]{:S(2)}) copy-start(bf16[400,100]{1,0:T(8,128)(2,1)} %copy-done.35) | copy-start | bytes 240004
  1042.4 2.7 copy-start.8
  1045.1 5.2 copy-start.39
  1045.1 5.9 copy-start.1
  (17 other events, 31.4 us)
Sparse Core Ops, SparseCore 0:
  94.4 56.0 all-gather.2
  152.4 55.8 all-gather.4
  402.4 242.6 all-reduce.12
  754.5 181.5 all-reduce.10

commit v4 on v3

--- a/solution.py
+++ b/solution.py
@@ -345,6 +345,11 @@
         out_shape=[jax.ShapeDtypeStruct((n, seqs, length, c), t) for c, t in outs],
         input_output_aliases={4 + i: i for i in range(len(before))},
         compiler_params=pltpu.CompilerParams(vmem_limit_bytes=GIANT),
+        cost_estimate=pl.CostEstimate(
+            flops=2 * n * length * w.shape[1] * depth + 16 * (n * length) ** 2 * width,
+            bytes_accessed=2 * n * length * (depth + 6 * width),
+            transcendentals=(n * length) ** 2 * (width // HEAD),
+        ),
     )(slot, lengths, rows, w, *before)
 
 
@@ -894,6 +899,35 @@
     )(x, gain[None], w, w_in)
 
 
+def sum4_kernel(p_ref, after_ref, o_ref, total, low, *rest):
+    rs4_kernel(p_ref, after_ref, total, *rest[:8])
+    low[...] = total[...].astype(BF)
+    begin, finish = ag4_parts(8, low, o_ref, *rest[8:])
+    begin()
+    finish()
+
+
+def all_sum(p, n, cid, after=None):
+    after = jnp.zeros((8, 128), F32) if after is None else after
+    if n != 8:
+        return all_gather(reduce_scatter(p, n, cid, after).astype(BF), n, cid + 1)
+    blk = p.shape[1:]
+    dma = pltpu.SemaphoreType.DMA
+    return pl.pallas_call(
+        sum4_kernel,
+        out_shape=jax.ShapeDtypeStruct(p.shape, BF),
+        in_specs=[pl.BlockSpec(memory_space=pl.ANY)] * 2,
+        out_specs=pl.BlockSpec(memory_space=pl.ANY),
+        scratch_shapes=[
+            pltpu.VMEM(blk, F32), pltpu.VMEM(blk, BF),
+            pltpu.VMEM((4,) + blk, BF), pltpu.VMEM((4,) + blk, BF), pltpu.VMEM((6, blk[0] // 2) + blk[1:], BF),
+            dma((4,)), dma((4,)), dma((4,)), dma((6,)), dma((6,)),
+            dma, dma((6,)), dma((6,)), dma((7,)), dma((7,)),
+        ],
+        compiler_params=pltpu.CompilerParams(collective_id=cid, has_side_effects=True, vmem_limit_bytes=GIANT),
+    )(p, after)
+
+
 def all_gather(x, n, cid):
     return (all_gather4 if n == 8 else all_gather_any)(x, n, cid)
 
@@ -903,10 +937,11 @@
     return (reduce_scatter4 if n == 8 else reduce_scatter_any)(p, after, n, cid)
 
 
-def mm_rs4_kernel(turned, *refs):
+def mm_rs4_kernel(turned, seconds, firsts, *refs):
     terms = len(turned)
-    a_refs, b_refs = refs[:terms], refs[terms : 2 * terms]
-    after_ref, o_ref, part, near, got, near_send, near_recv, far_send, far_recv = refs[2 * terms :]
+    count = max(seconds) + 1
+    a_refs, b_refs = refs[:terms], refs[terms : terms + count]
+    after_ref, o_ref, part, near, got, near_send, near_recv, far_send, far_recv = refs[terms + count :]
     me = lax.axis_index("seq")
     core, (sib, east, north, across) = square(me)
     x, y = (me // 2) % 2, me // 4
@@ -947,8 +982,9 @@
         yy, xx = (y + (i + 1) % 2) % 2, (x + 1 - i // 2) % 2
         seat = (yy * 2 + xx) * 2 + (core + 1 - mine) % 2
         total = None
-        for a, b, t in zip(a_refs, b_refs, turned):
-            term = (ntdot if t else dot)(a[seat], b[...])
+        for a, t, at, first in zip(a_refs, turned, seconds, firsts):
+            b = b_refs[at]
+            term = ntdot(a[seat], b[...]) if t else dot(a[seat], b[first : first + a.shape[2]])
             total = term if total is None else total + term
         part[mine, i] = total.astype(BF)
 
@@ -956,13 +992,13 @@
         def _():
             near_copy(i).start()
 
-        @pl.when(s == 3)
+        @pl.when(s == 2)
         def _():
             fold(0)
             far_copy(0).start()
             far_copy(1).start()
 
-        @pl.when(s == 5)
+        @pl.when(s == 4)
         def _():
             fold(1)
             far_copy(2).start()
@@ -1021,15 +1057,27 @@
     after = jnp.zeros((8, 128), F32) if after is None else after
     rows = pairs[0][0].shape[0] // n
     cols = pairs[0][1].shape[0 if pairs[0][2] else 1]
+    bs, seconds, firsts, used = [], [], [], []
+    for a, b, t in pairs:
+        if not any(b is other for other in bs):
+            bs.append(b)
+            used.append(0)
+        at = [b is other for other in bs].index(True)
+        seconds.append(at)
+        firsts.append(used[at])
+        used[at] += a.shape[1]
     if n != 8:
-        total = sum((ntdot if t else dot)(a, b) for a, b, t in pairs)
+        total = sum(
+            ntdot(a, b) if t else dot(a, b[first : first + a.shape[1]])
+            for (a, b, t), first in zip(pairs, firsts)
+        )
         return reduce_scatter(total.astype(BF).reshape(n, rows, cols), n, cid, after)
     vmem = pl.BlockSpec(memory_space=pltpu.VMEM)
     dma = pltpu.SemaphoreType.DMA
     return pl.pallas_call(
-        functools.partial(mm_rs4_kernel, tuple(t for _, _, t in pairs)),
+        functools.partial(mm_rs4_kernel, tuple(t for _, _, t in pairs), tuple(seconds), tuple(firsts)),
         out_shape=jax.ShapeDtypeStruct((rows, cols), F32),
-        in_specs=[vmem] * (2 * len(pairs)) + [pl.BlockSpec(memory_space=pl.ANY)],
+        in_specs=[vmem] * (len(pairs) + len(bs)) + [pl.BlockSpec(memory_space=pl.ANY)],
         out_specs=vmem,
         scratch_shapes=[
             pltpu.VMEM((2, 4, rows, cols), BF),
@@ -1038,7 +1086,7 @@
             dma((4,)), dma((4,)), dma((6,)), dma((6,)),
         ],
         compiler_params=pltpu.CompilerParams(collective_id=cid, has_side_effects=True, vmem_limit_bytes=GIANT),
-    )(*(a.reshape(n, rows, a.shape[1]) for a, _, _ in pairs), *(b for _, b, _ in pairs), after)
+    )(*(a.reshape(n, rows, a.shape[1]) for a, _, _ in pairs), *bs, after)
 
 
 def chain_kernel(axis, count, cuts, *refs):
@@ -1380,13 +1428,10 @@
     table = plan.head_table()[me]
     tie = lax.optimization_barrier
     flat = lambda v: v.reshape(rows, v.shape[-1])
-    gather = lambda v, cid: flat(all_gather(v, n, cid))
-    scatter = lambda v, cid, after=None: reduce_scatter(
-        v.astype(BF).reshape(n, local, v.shape[-1]), n, cid, after
-    )
     later = lambda g, zero: g + zero.astype(g.dtype)
     nothing = lambda *sums: 0.0 * sum(g.reshape(-1)[0].astype(F32) for g in sums)
     mark = lambda zero: jnp.full((8, 128), zero)
+    by_device = lambda m: m.reshape(n, local, m.shape[-1])
     exchange = lambda v: lax.all_to_all(v, "seq", 0, 0, tiled=True)
     blocks = lambda v: v.reshape(n, seqs, slot_len, v.shape[-1])
     mine = lambda v: lax.dynamic_slice_in_dim(v, me * cols, cols, v.ndim - 1)
@@ -1433,11 +1478,10 @@
     xp = jnp.concatenate([xp[DTR:], xp[:DTR]], axis=0)
     x_conv, conv_pre, mixer_in, mixer_low, projected = signal_forward(blocks(normed), wx, taps, bias[None], xp)
     mixer_low = flat(mixer_low)
-    projected = blocks(gather(scatter(flat(projected), 15).astype(BF), 16))
+    projected = blocks(all_sum(by_device(projected), n, 15))
     core, z_gate, ssm_sq, start = scan_forward(
         projected, mixer_in, blocks(normed), wz, wdt, dtb[None], rate, skip[None]
     )
-    by_device = lambda m: m.reshape(n, local, m.shape[-1])
     squares = row_sums(jnp.sum(attended * attended, axis=3).reshape(rows), ssm_sq.reshape(rows), 2)
     r_attn = lax.rsqrt(squares[0] / (HEADS * HEAD) + EPSILON)
     r_ssm = lax.rsqrt(squares[1] / INNER + EPSILON)
@@ -1523,7 +1567,7 @@
     g_qkv = plan.join_columns(g_qkv).astype(BF)
     first_sums = nothing(s_down, s_gate, s_up)
     grad_projected = jnp.concatenate([gb, gc, ntdot(grad_step, wdt)], axis=1)
-    grad_projected = gather(scatter(grad_projected, 9, mark(first_sums)).astype(BF), 10)
+    grad_projected = flat(all_sum(by_device(grad_projected.astype(BF)), n, 9, mark(first_sums)))
     after_one = first_sums + nothing(grad_projected)
     s_ao, s_so, s_qkv, s_z = over(tuple(later(g, after_one) for g in (g_ao, g_so, g_qkv, g_z)))
 

time: 1070 us -> 1040 us (0.972); the launches traced: 1060 us -> 1040 us
  Pallas kernels: 711 us -> 699 us
    pallas_call x4, Pallas kernels: 66.2 us -> 38.6 us  [small_sum(): pl.pallas_call(functools.partial(stat_kernel, n, axis), out_shape=jax.Sha...]
    pallas_call x1, Pallas kernels: 74.3 us -> 90.1 us  [scan_backward(): pl.pallas_call(scan_bwd_kernel, grid=(seqs, n), in_specs=[pl.BlockSpec(me...]
    pallas_call x4 -> x2, Pallas kernels: 47.4 us -> 44.2 us  [all_sum(): pl.pallas_call(sum4_kernel, out_shape=jax.ShapeDtypeStruct(p.shape, BF),...]
  transfers between devices with their start and end apart: 11 -> 11, of which waited for: 2 -> 2; matrix products, arithmetic and copies ran while one was open for 19% -> 20% of each run, Pallas kernels for 54% -> 53%
where the time goes in v4:
time: 1040 us
  Pallas kernels  699 us (67%)
  local copies, waits for them, and re-layouts  152 us (15%)
  other arithmetic  68.7 us (7%)
  matrix products  64.9 us (6%)
  starting transfers between devices  25.6 us (2%)
  between operations  24.1 us (2%)
    pallas_call x4, Pallas kernels, product_scatter(): pl.pallas_call(functools.partial(mm_rs4_kernel, tuple((t for _, _, t in p...  159 us
    pallas_call x1, Pallas kernels, scan_backward(): pl.pallas_call(scan_bwd_kernel, grid=(seqs, n), in_specs=[pl.BlockSpec(me...  90.1 us
    pallas_call x2, Pallas kernels, gather_product(): pl.pallas_call(functools.partial(gather_product4_kernel, body, len(weight...  84.8 us
    dot_general x10, matrix products, tndot(): return lax.dot_general(a, b, TN, preferred_element_type=F32)  61.8 us
    pallas_call x1, Pallas kernels, gather_and_exchange(): pl.pallas_call(functools.partial(start_kernel, n, moves), out_shape=[jax....  57.4 us
    pallas_call x1, Pallas kernels, chain_sum(): pl.pallas_call(functools.partial(chain_kernel, axis, count, tuple(cuts)),...  50.6 us
    pallas_call x2, Pallas kernels, all_sum(): pl.pallas_call(sum4_kernel, out_shape=jax.ShapeDtypeStruct(p.shape, BF),...  44.2 us
    reshape x13, local copies, waits for them, and re-layouts, per_device(): g.reshape(-1)[0].astype(F32)  41.8 us
  transfers between devices with their start and end apart: 11, of which 2 were waited for; matrix products, arithmetic and copies ran while one was open for 20% of the time, Pallas kernels for 53%

profile of v4, /device:TPU:0, one launch (start us, length us, event | category | flops | bytes accessed | tf_op | source)
XLA Modules:
  0.0 1040.7 jit_solution(3463382992137502273)
XLA Ops:
  11.5 57.4 %shard_map.357 = (bf16[8,256,1600]{2,1,0:T(8,128)(2,1)}, bf16[8,200,512]{2,1,0:T(8,128)(2,1)}, bf16[8,200,400]{2,1,0:T(8,128)(2,1)}, bf16[8,200,400]{2,1,0:T(8,128)(2,1)}) custom-call(bf16[256,1600]{1,0:T(8,128)(2,1)} %bitcast.252, f32[1,1600]{1,0:T(1,128)} %broadcast_in_dim.62.gain_ref, bf16[200,2240]{1,0:T(8,128)(2,1)} %w_ref.1, bf16[200,6400]{1,0:T(8,128)(2,1)} %in_ref.1), custom_call_target="tpu_custom_call" | custom-call | tf_op jit(solution)/shard_map/pallas_call | solution.py:891
  68.9 20.8 %shard_map.358 = (f32[8,2,128,256]{3,2,1,0:T(8,128)}, f32[8,2,128,4]{3,2,1,0:T(8,128)S(1)}, bf16[8,2,128,256]{3,2,1,0:T(8,128)(2,1)}, bf16[8,2,128,128]{3,2,1,0:T(8,128)(2,1)}, bf16[8,2,128,128]{3,2,1,0:T(8,128)(2,1)}) custom-call(s32[8]{0:T(128)S(1)} %fusion.33.slot_ref, s32[2]{0:T(128)S(1)} %copy-done.75, bf16[8,2,128,1600]{3,2,1,0:T(8,128)(2,1)} %bitcast.222, ...), custom_call_target="tpu_custom_call" | custom-call | flops 5972688896 | bytes 6422528 | tf_op jit(solution)/shard_map/pallas_call | solution.py:339
  97.3 4.3 all-to-all-start
  103.4 20.7 %shard_map.359 = (f32[8,2,128,256]{3,2,1,0:T(8,128)}, f32[8,2,128,4]{3,2,1,0:T(8,128)}, bf16[8,2,128,256]{3,2,1,0:T(8,128)(2,1)}, bf16[8,2,128,128]{3,2,1,0:T(8,128)(2,1)S(1)}, bf16[8,2,128,128]{3,2,1,0:T(8,128)(2,1)}) custom-call(s32[8]{0:T(128)S(1)} %fusion.33.slot_ref, ...), custom_call_target="tpu_custom_call", output_to_operand_aliasing={{0}: (4, {}), {1}: (5, {}), {2}: (6, {}), {3}: (7, {}), {4}... | custom-call | flops 5972688896 | bytes 6422528 | tf_op jit(solution)/shard_map/pallas_call | solution.py:339
  126.2 2.6 all-to-all-done
  128.8 4.1 all-to-all-start.1
  135.1 3.1 reshape.553
  144.7 5.0 slice_bitcast_fusion
  149.7 2.7 broadcast_add_fusion
  152.4 18.2 %shard_map.360 = (bf16[8,2,128,400]{3,2,1,0:T(8,128)(2,1)}, f32[8,2,128,400]{3,2,1,0:T(8,128)}, f32[8,2,128,400]{3,2,1,0:T(8,128)}, bf16[8,2,128,400]{3,2,1,0:T(8,128)(2,1)}, bf16[8,2,128,132]{3,2,1,0:T(8,128)(2,1)}) custom-call(bf16[8,2,128,1600]{3,2,1,0:T(8,128)(2,1)} %bitcast.224, bf16[1600,400]{1,0:T(8,128)(2,1)} %bitcast.234, ...), custom_call_target="tpu_custom_call" | custom-call | tf_op jit(solution)/shard_map/pallas_call | solution.py:456
  171.1 25.0 %shard_map.361 = bf16[8,256,132]{2,1,0:T(8,128)(2,1)} custom-call(bf16[8,256,132]{2,1,0:T(8,128)(2,1)} %bitcast.261, f32[8,128]{1,0:T(8,128)} %broadcast_47_after_ref_refs_4__refs_6_.2.after_ref.refs_4_.refs_6_), custom_call_target="tpu_custom_call" | custom-call | tf_op jit(solution)/shard_map/pallas_call | solution.py:916
  197.5 40.2 %shard_map.362 = (f32[8,2,128,400]{3,2,1,0:T(8,128)}, f32[8,2,128,400]{3,2,1,0:T(8,128)}, f32[8,2,128,1]{3,2,1,0:T(8,128)}, f32[8,2,16,400]{3,2,1,0:T(8,128)}) custom-call(bf16[8,2,128,132]{3,2,1,0:T(8,128)(2,1)} %bitcast.236, f32[8,2,128,400]{3,2,1,0:T(8,128)} %get-tuple-element.265.mix_ref, bf16[8,2,128,1600]{3,2,1,0:T(8,128)(2,1)} %bitcast.225, ...), custom_call_target="tpu_custom_call" | custom-call | tf_op jit(solution)/shard_map/pallas_call | solution.py:117
  239.9 6.2 shard_map.363
  248.2 8.1 shard_map.364
  256.3 2.7 pad_dynamic-slice_fusion.refs_2_.refs_0_
  258.9 37.6 %shard_map.365 = f32[256,1600]{1,0:T(8,128)} custom-call(bf16[8,256,256]{2,1,0:T(8,128)(2,1)S(1)} %get-tuple-element.270.refs_0_, bf16[8,256,400]{2,1,0:T(8,128)(2,1)} %get-tuple-element.271.refs_1_, bf16[256,1600]{1,0:T(8,128)(2,1)} %pad_dynamic-slice_fusion.refs_2_.refs_0_, bf16[400,1600]{1,0:T(8,128)(2,1)} %refs_1_.2, ...), custom_call_target="tpu_custom_call" | custom-call | tf_op jit(solution)/shard_map/pallas_call | solution.py:1077
  300.1 42.2 %shard_map.366 = (bf16[8,256,1600]{2,1,0:T(8,128)(2,1)}, bf16[8,256,688]{2,1,0:T(8,128)(2,1)}, bf16[8,256,688]{2,1,0:T(8,128)(2,1)}, bf16[8,256,688]{2,1,0:T(8,128)(2,1)}) custom-call(bf16[256,1600]{1,0:T(8,128)(2,1)} %multiply_convert_fusion.x_ref, bf16[688,1600]{1,0:T(8,128)(2,1)} %get-tuple-element.471.refs_0_.refs_2_, ...), custom_call_target="tpu_custom_call" | custom-call | tf_op jit(solution)/shard_map/pallas_call | solution.py:1321
  342.3 13.8 %shard_map.367 = (bf16[8,256,688]{2,1,0:T(8,128)(2,1)}, bf16[8,256,688]{2,1,0:T(8,128)(2,1)}) custom-call(bf16[8,256,1600]{2,1,0:T(8,128)(2,1)} %bitcast.241, bf16[688,1600]{1,0:T(8,128)(2,1)} %refs_1_.3, bf16[8,256,688]{2,1,0:T(8,128)(2,1)} %get-tuple-element.273.gate_ref, bf16[8,256,688]{2,1,0:T(8,128)(2,1)} %get-tuple-element.274.up_ref), custom_call_target="tpu_custom_call" | custom-call | tf_op jit(solution)/shard_map/pallas_call | solution.py:550
  356.1 10.7 %bitcast_convert_fusion.1 = bf16[688,1600]{1,0:T(8,128)(2,1)} fusion(bf16[8,256,688]{2,1,0:T(8,128)(2,1)} %get-tuple-element.275.refs_0_, bf16[8,256,1600]{2,1,0:T(8,128)(2,1)} %get-tuple-element.277), kind=kOutput, calls=%fused_computation.22 | convolution fusion | flops 4509977600 | bytes 11573248 | tf_op jit(solution)/shard_map/dot_general | solution.py:37
  366.9 7.0 bitcast_convert_fusion
  373.9 7.4 convolution_convert_fusion.5
  381.2 5.5 reshape.568
  386.7 5.4 reshape.569
  397.2 41.7 %shard_map.368 = f32[256,1600]{1,0:T(8,128)} custom-call(bf16[8,256,688]{2,1,0:T(8,128)(2,1)} %get-tuple-element.275.refs_0_, bf16[8,256,688]{2,1,0:T(8,128)(2,1)} %get-tuple-element.276.refs_1_, bf16[688,1600]{1,0:T(8,128)(2,1)} %get-tuple-element.471.refs_0_.refs_2_, bf16[688,1600]{1,0:T(8,128)(2,1)} %get-tuple-element.470.refs_1_.refs_3_, ...), custom_call_target="tpu_custom_call" | custom-call | tf_op jit(solution)/shard_map/pallas_call | solution.py:1077
  438.9 2.7 multiply_reduce_fusion.1
  443.6 42.7 %shard_map.369 = (bf16[8,256,1600]{2,1,0:T(8,128)(2,1)}, f32[8,256,256]{2,1,0:T(8,128)}, f32[8,256,400]{2,1,0:T(8,128)}, f32[8,256,2]{2,1,0:T(8,128)}) custom-call(bf16[256,1600]{1,0:T(8,128)(2,1)} %get-tuple-element.463.x_ref, bf16[256,1600]{1,0:T(8,128)(2,1)} %pad_dynamic-slice_fusion.refs_2_.refs_0_, bf16[400,1600]{1,0:T(8,128)(2,1)} %refs_1_.2, ...), custom_call_target="tpu_custom_call" | custom-call | tf_op jit(solution)/shard_map/pallas_call | solution.py:1321
  486.3 3.2 fusion.37
  493.3 6.7 shard_map.370
  500.8 164.0 %conditional.2 = (f32[256]{0:T(256)S(1)}, bf16[2048,400]{1,0:T(8,128)(2,1)}, f32[8,2,128,400]{3,2,1,0:T(8,128)}, f32[16,400]{1,0:T(8,128)}, bf16[400,1600]{1,0:T...) conditional(s32[]{:T(128)} %bitcast.51, () %tuple.46, ...), branch_computations={%region_3.4_spmd, %region_4.5_spmd} | conditional | flops 10279668736 | bytes 107956000 | solution.py:1443
  502.2 37.5 %branch_1_fun.5 = (bf16[8,2,128,256]{3,2,1,0:T(8,128)(2,1)}, bf16[8,2,128,128]{3,2,1,0:T(8,128)(2,1)}, bf16[8,2,128,128]{3,2,1,0:T(8,128)(2,1)}, f32[8,256]{1,0:T(8,128)}) custom-call(s32[8]{0:T(128)S(1)} %get-tuple-element.126.slot_ref, s32[2]{0:T(128)S(1)} %get-tuple-element.127.len_ref, bf16[8,2,128,256]{3,2,1,0:T(8,128)(2,1)} %get-tuple-element.128.q_ref, ...), custom_call_target="tpu_custom_call" | custom-call | tf_op jit(solution)/shard_map/cond/branch_1_fun/pallas_call | solution.py:415
  540.4 90.1 %branch_1_fun.6 = (bf16[8,2,128,400]{3,2,1,0:T(8,128)(2,1)}, f32[8,2,128,400]{3,2,1,0:T(8,128)}, bf16[8,2,128,400]{3,2,1,0:T(8,128)(2,1)}, f32[8,2,128,16]{3,2,1...) custom-call(s32[2]{0:T(128)S(1)} %get-tuple-element.127.len_ref, ...), custom_call_target="tpu_custom_call" | custom-call | tf_op jit(solution)/shard_map/cond/branch_1_fun/pallas_call | solution.py:256
  630.5 7.3 fusion.1
  637.8 7.9 fusion.4
  648.7 6.6 fusion.2
  657.6 3.8 fusion.5
  665.6 3.6 all-to-all-start.2
  669.8 3.1 convolution_convert_fusion.6
  675.0 2.8 constant_dynamic-slice_fusion.2
  679.3 3.1 collective-permute-start
  682.4 3.4 copy.127
  685.8 3.1 pad_maximum_fusion.1.p_ref
  690.9 4.3 all-to-all-start.4
  697.3 3.0 concatenate.45
  700.3 5.4 reshape.573
  706.9 5.4 reshape.574
  713.6 5.4 reshape.575
  722.7 19.2 %shard_map.371 = bf16[8,256,132]{2,1,0:T(8,128)(2,1)S(1)} custom-call(bf16[8,256,132]{2,1,0:T(8,128)(2,1)} %pad_maximum_fusion.1.p_ref, f32[8,128]{1,0:T(8,128)} %broadcast_in_dim.69.after_ref), custom_call_target="tpu_custom_call" | custom-call | tf_op jit(solution)/shard_map/pallas_call | solution.py:916
  750.9 4.3 add.353
  757.3 3.3 add_add_fusion
  765.6 27.5 %conditional.3 = (bf16[1600,400]{0,1:T(8,128)(2,1)}, bf16[132,400]{1,0:T(8,128)(2,1)S(1)}, bf16[400,100]{1,0:T(8,128)(2,1)S(1)}, bf16[8,256,400]{2,1,0:T(8,128)(2,1)}, f32[5,400]{1,0:T(8,128)}) conditional(s32[]{:T(128)} %bitcast.51, () %tuple.45, (bf16[8,256,132]{2,1,0:T(8,128)(2,1)S(1)}, f32[8,2,128,400]{3,2,1,0:T(8,128)}, ...), branch_computations={%region_8.9_spmd, %region_9.10_spmd} | conditional | flops 3002281472 | bytes 22715744 | solution.py:1443
  766.1 15.3 %branch_1_fun.7 = (bf16[8,2,128,400]{3,2,1,0:T(8,128)(2,1)}, f32[8,400]{1,0:T(8,128)}) custom-call(f32[8,2,128,400]{3,2,1,0:T(8,128)} %get-tuple-element.162.gmix_ref, bf16[8,2,128,132]{3,2,1,0:T(8,128)(2,1)S(1)} %bitcast.230, bf16[132,400]{1,0:T(8,128)(2,1)S(1)} %get-tuple-element.164.xp_ref, f32[8,2,128,400]{3,2,1,0:T(8,128)} %get-tuple-element.165.pre_ref, ...), custom_call_target="tpu_custom_call" | custom-call | tf_op jit(solution)/shard_map/cond/branch_1_fun/pallas_call | solution.py:503
  781.4 8.0 fusion.6
  793.8 41.7 %shard_map.372 = f32[256,1600]{1,0:T(8,128)} custom-call(bf16[8,256,400]{2,1,0:T(8,128)(2,1)} %get-tuple-element.296.refs_0_, bf16[8,256,400]{2,1,0:T(8,128)(2,1)} %get-tuple-element.297.refs_1_, bf16[8,256,512]{2,1,0:T(8,128)(2,1)} %get-tuple-element.298.refs_2_, bf16[1600,400]{1,0:T(8,128)(2,1)} %bitcast.235, bf16[1600,400]{1,0:T(8,128)(2,1)} %bitcast.233, ...), custom_call_target="tpu_custom_call" | custom-call | tf_op jit(solution)/shard_map/pallas_call | solution.py:1077
  839.4 38.1 %shard_map.373 = f32[256,1600]{1,0:T(8,128)} custom-call(bf16[8,256,688]{2,1,0:T(8,128)(2,1)} %get-tuple-element.272.refs_0_, bf16[688,1600]{1,0:T(8,128)(2,1)} %refs_1_.3, f32[8,128]{1,0:T(8,128)} %broadcast_in_dim.70.refs_2_), custom_call_target="tpu_custom_call" | custom-call | tf_op jit(solution)/shard_map/pallas_call | solution.py:1077
  877.5 3.4 copy.125
  881.0 4.4 all-to-all-start.3
  891.4 17.3 %shard_map.375 = f32[40,128]{1,0:T(8,128)} custom-call(f32[40,128]{1,0:T(8,128)} %pad_bitcast_fusion.x_ref), custom_call_target="tpu_custom_call" | custom-call | tf_op jit(solution)/shard_map/pallas_call | solution.py:696
  910.9 3.3 fusion.34
  920.1 8.4 shard_map.376
  940.4 6.6 convert_bitcast_fusion
  948.9 3.0 reshape.581.refs_0_
  961.0 2.6 reshape.587
  973.1 50.6 %shard_map.374 = (f32[200,3200]{1,0:T(8,128)}, f32[132,400]{1,0:T(8,128)}, f32[400,100]{1,0:T(8,128)}) custom-call(bf16[200,3200]{1,0:T(8,128)(2,1)} %reshape.581.refs_0_, bf16[132,400]{1,0:T(8,128)(2,1)S(1)} %get-tuple-element.302.refs_1_, bf16[400,100]{1,0:T(8,128)(2,1)S(1)} %copy-done.41, f32[8,128]{1,0:T(8,128)} %broadcast_in_dim.72.refs_3_), custom_call_target="tpu_custom_call" | custom-call | tf_op jit(solution)/shard_map/pallas_call | solution.py:1210
  1028.1 4.4 pad_maximum_fusion
  (332 shorter events, 138.6 us)
Async XLA Ops:
  7.2 96.1 %copy-start = (bf16[100,3200]{1,0:T(8,128)(2,1)S(1)}, bf16[100,3200]{1,0:T(8,128)(2,1)}, u32[]{:S(2)}) copy-start(bf16[100,3200]{1,0:T(8,128)(2,1)} %param.33) | copy-start | bytes 1920004
  7.2 249.1 %all-gather.3.cloned.1.call-start = ((), (), s32[]{:S(2)}) async-start(), calls=%async_computation.5 | async-start | bytes 5990400 | tf_op jit(solution)/shard_map/all_gather | solution.py:1469
  11.5 91.9 %copy-start.79 = (s32[8]{0:T(128)}, s32[8]{0:T(128)S(1)}, u32[]{:S(2)}) copy-start(s32[8]{0:T(128)S(1)} %fusion.33.slot_ref) | copy-start | bytes 100
  11.5 57.4 %copy-start.75 = (s32[2]{0:T(128)S(1)}, s32[2]{0:T(128)}, u32[]{:S(2)}) copy-start(s32[2]{0:T(128)} %len_ref.3) | copy-start | bytes 28
  68.9 22.6 %copy-start.35 = (bf16[200,1600]{1,0:T(8,128)(2,1)S(1)}, bf16[200,1600]{1,0:T(8,128)(2,1)}, u32[]{:S(2)}) copy-start(bf16[200,1600]{1,0:T(8,128)(2,1)} %param.30) | copy-start | bytes 1920004
  89.7 2.9 copy-start.11
  89.7 2.9 copy-start.34
  92.4 249.9 %all-gather.5.cloned.1.call-start = ((), (), s32[]{:S(2)}) async-start(), calls=%async_computation.6 | async-start | bytes 7667712 | tf_op jit(solution)/shard_map/all_gather | solution.py:1474
  96.9 6.4 copy-start.36
  97.3 31.6 %all-to-all-start = ((bf16[8,200,400]{2,1,0:T(8,128)(2,1)}), bf16[8,200,400]{2,1,0:T(8,128)(2,1)}, u32[]{:S(2)}, u32[]{:S(2)}) async-start(bf16[8,200,400]{2,1,0:T(8,128)(2,1)} %get-tuple-element.262), calls=%async_computation | async-start | bytes 3276800 | tf_op jit(solution)/shard_map/all_to_all | solution.py:1435
  102.4 50.0 %copy-start.50 = (f32[4,400]{1,0:T(4,128)}, f32[4,400]{1,0:T(4,128)S(1)}, u32[]{:S(2)}) copy-start(f32[4,400]{1,0:T(4,128)S(1)} %constant_dynamic-slice_fusion.4.taps_ref) | copy-start | bytes 19204
  124.1 4.8 copy-start.37
  126.2 6.7 copy-start.74
  126.2 6.8 copy-start.44
  128.8 67.4 %all-to-all-start.1 = ((bf16[8,200,400]{2,1,0:T(8,128)(2,1)}), bf16[8,200,400]{2,1,0:T(8,128)(2,1)S(1)}, u32[]{:S(2)}, u32[]{:S(2)}) async-start(bf16[8,200,400]{2,1,0:T(8,128)(2,1)} %get-tuple-element.266), calls=%async_computation.1 | async-start | bytes 3276800 | tf_op jit(solution)/shard_map/all_to_all | solution.py:1435
  133.0 115.2 %copy-start.62 = (f32[256]{0:T(256)}, f32[256]{0:T(256)S(1)}, u32[]{:S(2)}) copy-start(f32[256]{0:T(256)S(1)} %pad_dynamic-slice_fusion.1) | copy-start | bytes 3076
  135.1 161.4 %copy-start.3 = (f32[2,128,1600]{2,1,0:T(8,128)}, f32[2,128,1600]{2,1,0:T(8,128)S(1)}, u32[]{:S(2)}) copy-start(f32[2,128,1600]{2,1,0:T(8,128)S(1)} %copy.100) | copy-start | bytes 4915204
  142.2 54.0 %copy-start.58 = (f32[400]{0:T(512)}, f32[400]{0:T(512)S(1)}, u32[]{:S(2)}) copy-start(f32[400]{0:T(512)S(1)} %dynamic_slice.49) | copy-start | bytes 4804
  143.0 53.3 %copy-start.60 = (f32[400]{0:T(512)}, f32[400]{0:T(512)S(1)}, u32[]{:S(2)}) copy-start(f32[400]{0:T(512)S(1)} %dynamic_slice.51) | copy-start | bytes 4804
  143.7 104.5 %copy-start.54 = (f32[400]{0:T(512)}, f32[400]{0:T(512)S(1)}, u32[]{:S(2)}) copy-start(f32[400]{0:T(512)S(1)} %dynamic_slice.53) | copy-start | bytes 4804
  144.7 7.7 copy-start.27
  356.1 10.8 %copy-start.22 = (bf16[8,256,688]{2,1,0:T(8,128)(2,1)S(1)}, bf16[8,256,688]{2,1,0:T(8,128)(2,1)}, u32[]{:S(2)}) copy-start(bf16[8,256,688]{2,1,0:T(8,128)(2,1)} %get-tuple-element.276.refs_1_) | copy-start | bytes 8454148
  356.1 10.8 %copy-start.81 = (bf16[8,256,1600]{2,1,0:T(8,128)(2,1)S(1)}, bf16[8,256,1600]{2,1,0:T(8,128)(2,1)}, u32[]{:S(2)}) copy-start(bf16[8,256,1600]{2,1,0:T(8,128)(2,1)} %get-tuple-element.277) | copy-start | bytes 19660804
  356.1 17.7 %slice-start.2 = ((s8[6815744]{0:T(1024)(128)(4,1)}), s8[4194304]{0:T(1024)(128)(4,1)S(1)}, s32[]{:S(2)}) async-start(s8[6815744]{0:T(1024)(128)(4,1)} %bitcast.242), calls=%async_computation.11 | async-start | bytes 8388608
  366.9 7.0 slice-start.3
  366.9 7.0 copy-start.21
  392.1 308.2 %all-reduce.13.cloned.1.call-start = ((), (), s32[]{:S(2)}) async-start(), calls=%async_computation.8 | async-start | bytes 13737984 | tf_op jit(solution)/shard_map/psum | solution.py:1438
  438.9 2.7 copy-start.67
  489.5 11.3 %copy-start.12 = (f32[8,2,128,4]{3,2,1,0:T(8,128)S(1)}, f32[8,2,128,4]{3,2,1,0:T(8,128)}, u32[]{:S(2)}) copy-start(f32[8,2,128,4]{3,2,1,0:T(8,128)} %get-tuple-element.263) | copy-start | bytes 98308
  489.5 11.3 %copy-start.59 = (f32[400]{0:T(512)S(1)}, f32[400]{0:T(512)}, u32[]{:S(2)}) copy-start(f32[400]{0:T(512)} %copy-done.58) | copy-start | bytes 4804
  489.5 11.3 %copy-start.61 = (f32[400]{0:T(512)S(1)}, f32[400]{0:T(512)}, u32[]{:S(2)}) copy-start(f32[400]{0:T(512)} %copy-done.60) | copy-start | bytes 4804
  489.5 11.3 %copy-start.80 = (s32[8]{0:T(128)S(1)}, s32[8]{0:T(128)}, u32[]{:S(2)}) copy-start(s32[8]{0:T(128)} %copy-done.79) | copy-start | bytes 100
  540.4 90.1 %copy-start.26 = (bf16[8,256,400]{2,1,0:T(8,128)(2,1)S(1)}, bf16[8,256,400]{2,1,0:T(8,128)(2,1)}, u32[]{:S(2)}) copy-start(bf16[8,256,400]{2,1,0:T(8,128)(2,1)} %get-tuple-element.426) | copy-start | bytes 4915204 | tf_op jit(solution)/shard_map/cond
  630.5 18.2 %slice-start = ((s8[6815744]{0:T(1024)(128)(4,1)}), s8[4194304]{0:T(1024)(128)(4,1)S(1)}, s32[]{:S(2)}) async-start(s8[6815744]{0:T(1024)(128)(4,1)} %bitcast.228), calls=%async_computation.9 | async-start | bytes 8388608 | tf_op jit(solution)/shard_map/cond
  637.8 8.0 copy-start.31
  637.8 10.9 %slice-start.1 = ((s8[6815744]{0:T(1024)(128)(4,1)}), s8[2621440]{0:T(1024)(128)(4,1)S(1)}, s32[]{:S(2)}) async-start(s8[6815744]{0:T(1024)(128)(4,1)} %bitcast.228), calls=%async_computation.10 | async-start | bytes 5242880 | tf_op jit(solution)/shard_map/cond
  648.7 8.9 slice-start.4
  648.7 7.6 copy-start.30
  648.7 8.8 slice-start.5
  664.8 4.4 copy-start.82
  665.6 25.3 %all-to-all-start.2 = ((bf16[8,200,512]{2,1,0:T(8,128)(2,1)}), bf16[8,200,512]{2,1,0:T(8,128)(2,1)S(1)}, u32[]{:S(2)}, u32[]{:S(2)}) async-start(bf16[8,200,512]{2,1,0:T(8,128)(2,1)} %bitcast.72), calls=%async_computation.2 | async-start | bytes 3276800 | tf_op jit(solution)/shard_map/all_to_all | solution.py:1435
  677.8 79.5 %collective-permute-start.1 = (bf16[200,1600]{1,0:T(8,128)(2,1)}, bf16[200,1600]{1,0:T(8,128)(2,1)}, u32[]{:S(2)}, u32[]{:S(2)}) collective-permute-start(bf16[200,1600]{1,0:T(8,128)(2,1)} %get-tuple-element.473), channel_id=1, source_target_pairs={{3,5},{4,6},{5,7},{11,13},{12,14},{13,15},{19,21},{20,22},{21,23},... | collective-permute-start | bytes 1920008 | tf_op jit(solution)/shard_map/ppermute | solution.py:1410
  679.3 78.0 %collective-permute-start = (bf16[200,1600]{1,0:T(8,128)(2,1)}, bf16[200,1600]{1,0:T(8,128)(2,1)}, u32[]{:S(2)}, u32[]{:S(2)}) collective-permute-start(bf16[200,1600]{1,0:T(8,128)(2,1)} %get-tuple-element.472), channel_id=1, source_target_pairs={{0,1},{1,2},{2,3},{3,4},{4,5},{5,6},{6,7},{8,9},{9,10},{10,11},{11... | collective-permute-start | bytes 1920008 | tf_op jit(solution)/shard_map/ppermute | solution.py:1410
  690.9 56.8 %all-to-all-start.4 = ((bf16[8,200,400]{2,1,0:T(8,128)(2,1)}), bf16[8,200,400]{2,1,0:T(8,128)(2,1)}, u32[]{:S(2)}, u32[]{:S(2)}) async-start(bf16[8,200,400]{2,1,0:T(8,128)(2,1)} %bitcast.245), calls=%async_computation.4 | async-start | bytes 3276800 | tf_op jit(solution)/shard_map/all_to_all | solution.py:1435
  695.2 256.8 %all-reduce.11.cloned.1.call-start = ((), (), s32[]{:S(2)}) async-start(), calls=%async_computation.7 | async-start | bytes 8396800 | tf_op jit(solution)/shard_map/psum | solution.py:1438
  760.7 3.5 copy-start.46
  760.7 5.0 copy-start.28
  760.7 5.0 copy-start.51
  762.1 3.5 copy-start.65
  781.4 8.0 copy-start.25
  881.0 4.4 copy-start.4
  881.0 4.5 copy-start.49
  881.0 66.0 %all-to-all-start.3 = ((bf16[8,200,400]{2,1,0:T(8,128)(2,1)}), bf16[8,200,400]{2,1,0:T(8,128)(2,1)}, u32[]{:S(2)}, u32[]{:S(2)}) async-start(bf16[8,200,400]{2,1,0:T(8,128)(2,1)} %bitcast.246), calls=%async_computation.3 | async-start | bytes 3276800 | tf_op jit(solution)/shard_map/all_to_all | solution.py:1435
  910.8 3.3 copy-start.5
  910.8 3.3 copy-start.15
  910.8 3.3 copy-start.64
  919.0 14.0 %copy-start.17 = (f32[256,1600]{1,0:T(8,128)S(1)}, f32[256,1600]{1,0:T(8,128)}, u32[]{:S(2)}) copy-start(f32[256,1600]{1,0:T(8,128)} %fusion.11) | copy-start | bytes 4915204
  930.7 4.0 copy-start.16
  952.0 4.0 copy-start.20
  956.0 3.3 copy-start.19
  961.0 3.8 copy-start.18
  961.0 12.1 %copy-start.41 = (bf16[400,100]{1,0:T(8,128)(2,1)S(1)}, bf16[400,100]{1,0:T(8,128)(2,1)}, u32[]{:S(2)}) copy-start(bf16[400,100]{1,0:T(8,128)(2,1)} %copy-done.40) | copy-start | bytes 240004
  1028.1 5.2 copy-start.42
  1028.1 5.9 copy-start.1
  (36 other events, 65.4 us)
Sparse Core Ops, SparseCore 0:
  92.5 69.7 all-gather.2
  164.2 58.2 all-gather.4
  395.5 242.7 all-reduce.12
  760.8 154.2 all-reduce.10

commit v5 on v4

--- a/solution.py
+++ b/solution.py
@@ -1609,7 +1609,7 @@
         v = v.reshape(-1)
         return jnp.pad(v, (0, -v.size % 1024)).reshape(-1, 128)
 
-    shared = jnp.stack([g_norm_in, place(g_norm_attn), g_norm_ffn])
+    shared = jnp.stack([g_norm_in, place(g_norm_attn), g_norm_ffn]) + nothing(g_x)
     total = small_sum(pad_rows(shared), n, 12).reshape(-1)[: shared.size].reshape(shared.shape)
     shared = lax.dynamic_slice_in_dim(total, me * w_rows, w_rows, 1)
     owned = jnp.concatenate(

time: 1040 us -> 1050 us (level)
  Pallas kernels: 699 us -> 687 us
    pallas_call x4, Pallas kernels: 38.6 us -> 64.6 us  [small_sum(): pl.pallas_call(functools.partial(stat_kernel, n, axis), out_shape=jax.Sha...]
    pallas_call x1, Pallas kernels: 90.1 us -> 64.9 us  [scan_backward(): pl.pallas_call(scan_bwd_kernel, grid=(seqs, n), in_specs=[pl.BlockSpec(me...]
    pallas_call x1, Pallas kernels: 37.5 us -> 23.8 us  [attn_backward(): pl.pallas_call(attn_bwd_kernel, grid=(seqs,), in_specs=[smem, smem, big(w...]
  transfers between devices with their start and end apart: 11 -> 11, of which waited for: 2 -> 3; matrix products, arithmetic and copies ran while one was open for 20% -> 20% of each run, Pallas kernels for 53% -> 52%
where the time goes in v5:
time: 1050 us
  Pallas kernels  687 us (65%)
  local copies, waits for them, and re-layouts  160 us (15%)
  other arithmetic  67 us (6%)
  matrix products  64.7 us (6%)
  starting transfers between devices  28.2 us (3%)
  between operations  24.4 us (2%)
  waiting for transfers between devices  13.7 us (1%)
    pallas_call x4, Pallas kernels, product_scatter(): pl.pallas_call(functools.partial(mm_rs4_kernel, tuple((t for _, _, t in p...  159 us
    pallas_call x2, Pallas kernels, gather_product(): pl.pallas_call(functools.partial(gather_product4_kernel, body, len(weight...  85.1 us
    pallas_call x1, Pallas kernels, scan_backward(): pl.pallas_call(scan_bwd_kernel, grid=(seqs, n), in_specs=[pl.BlockSpec(me...  64.9 us
    pallas_call x4, Pallas kernels, small_sum(): pl.pallas_call(functools.partial(stat_kernel, n, axis), out_shape=jax.Sha...  64.6 us
    dot_general x10, matrix products, tndot(): return lax.dot_general(a, b, TN, preferred_element_type=F32)  62.4 us
    pallas_call x1, Pallas kernels, gather_and_exchange(): pl.pallas_call(functools.partial(start_kernel, n, moves), out_shape=[jax....  57.3 us
    pallas_call x1, Pallas kernels, chain_sum(): pl.pallas_call(functools.partial(chain_kernel, axis, count, tuple(cuts)),...  51.1 us
    reshape x13, local copies, waits for them, and re-layouts, per_device(): g.reshape(-1)[0].astype(F32)  48.6 us
  transfers between devices with their start and end apart: 11, of which 3 were waited for; matrix products, arithmetic and copies ran while one was open for 20% of the time, Pallas kernels for 52%

profile of v5, /device:TPU:0, one launch (start us, length us, event | category | flops | bytes accessed | tf_op | source)
XLA Modules:
  0.0 1046.3 jit_solution(7752750389543769387)
XLA Ops:
  11.5 57.3 %shard_map.357 = (bf16[8,256,1600]{2,1,0:T(8,128)(2,1)}, bf16[8,200,512]{2,1,0:T(8,128)(2,1)}, bf16[8,200,400]{2,1,0:T(8,128)(2,1)}, bf16[8,200,400]{2,1,0:T(8,128)(2,1)}) custom-call(bf16[256,1600]{1,0:T(8,128)(2,1)} %bitcast.250, f32[1,1600]{1,0:T(1,128)} %broadcast_in_dim.62.gain_ref, bf16[200,2240]{1,0:T(8,128)(2,1)} %w_ref.1, bf16[200,6400]{1,0:T(8,128)(2,1)} %in_ref.1), custom_call_target="tpu_custom_call" | custom-call | tf_op jit(solution)/shard_map/pallas_call | solution.py:891
  68.8 21.0 %shard_map.358 = (f32[8,2,128,256]{3,2,1,0:T(8,128)S(1)}, f32[8,2,128,4]{3,2,1,0:T(8,128)}, bf16[8,2,128,256]{3,2,1,0:T(8,128)(2,1)}, bf16[8,2,128,128]{3,2,1,0:T(8,128)(2,1)}, bf16[8,2,128,128]{3,2,1,0:T(8,128)(2,1)}) custom-call(s32[8]{0:T(128)S(1)} %fusion.33.slot_ref, s32[2]{0:T(128)S(1)} %copy-done.43, bf16[8,2,128,1600]{3,2,1,0:T(8,128)(2,1)} %bitcast.223, ...), custom_call_target="tpu_custom_call" | custom-call | flops 5972688896 | bytes 6422528 | tf_op jit(solution)/shard_map/pallas_call | solution.py:339
  101.5 5.0 all-to-all-start
  108.2 20.5 %shard_map.359 = (f32[8,2,128,256]{3,2,1,0:T(8,128)S(1)}, f32[8,2,128,4]{3,2,1,0:T(8,128)}, bf16[8,2,128,256]{3,2,1,0:T(8,128)(2,1)}, bf16[8,2,128,128]{3,2,1,0:T(8,128)(2,1)S(1)}, bf16[8,2,128,128]{3,2,1,0:T(8,128)(2,1)}) custom-call(s32[8]{0:T(128)S(1)} %fusion.33.slot_ref, ...), custom_call_target="tpu_custom_call", output_to_operand_aliasing={{0}: (4, {}), {1}: (5, {}), {2}: (6, {}), {3}: (7, {}), {4}... | custom-call | flops 5972688896 | bytes 6422528 | tf_op jit(solution)/shard_map/pallas_call | solution.py:339
  129.1 4.0 all-to-all-done
  133.1 4.5 all-to-all-start.1
  146.9 4.9 slice_bitcast_fusion
  154.5 18.2 %shard_map.360 = (bf16[8,2,128,400]{3,2,1,0:T(8,128)(2,1)}, f32[8,2,128,400]{3,2,1,0:T(8,128)}, f32[8,2,128,400]{3,2,1,0:T(8,128)}, bf16[8,2,128,400]{3,2,1,0:T(8,128)(2,1)}, bf16[8,2,128,132]{3,2,1,0:T(8,128)(2,1)}) custom-call(bf16[8,2,128,1600]{3,2,1,0:T(8,128)(2,1)} %bitcast.225, bf16[1600,400]{1,0:T(8,128)(2,1)} %bitcast.233, ...), custom_call_target="tpu_custom_call" | custom-call | tf_op jit(solution)/shard_map/pallas_call | solution.py:456
  173.3 24.7 %shard_map.361 = bf16[8,256,132]{2,1,0:T(8,128)(2,1)} custom-call(bf16[8,256,132]{2,1,0:T(8,128)(2,1)} %bitcast.260, f32[8,128]{1,0:T(8,128)} %broadcast_47_after_ref_refs_4__refs_6_.2.after_ref.refs_4_.refs_6_), custom_call_target="tpu_custom_call" | custom-call | tf_op jit(solution)/shard_map/pallas_call | solution.py:916
  198.0 41.7 %shard_map.362 = (f32[8,2,128,400]{3,2,1,0:T(8,128)}, f32[8,2,128,400]{3,2,1,0:T(8,128)}, f32[8,2,128,1]{3,2,1,0:T(8,128)}, f32[8,2,16,400]{3,2,1,0:T(8,128)}) custom-call(bf16[8,2,128,132]{3,2,1,0:T(8,128)(2,1)} %bitcast.235, f32[8,2,128,400]{3,2,1,0:T(8,128)} %get-tuple-element.265.mix_ref, bf16[8,2,128,1600]{3,2,1,0:T(8,128)(2,1)} %bitcast.226, ...), custom_call_target="tpu_custom_call" | custom-call | tf_op jit(solution)/shard_map/pallas_call | solution.py:117
  241.9 6.2 shard_map.363
  250.3 7.8 shard_map.364
  260.5 37.5 %shard_map.365 = f32[256,1600]{1,0:T(8,128)} custom-call(bf16[8,256,256]{2,1,0:T(8,128)(2,1)} %get-tuple-element.270.refs_0_, bf16[8,256,400]{2,1,0:T(8,128)(2,1)S(1)} %copy-done.19, bf16[256,1600]{1,0:T(8,128)(2,1)} %pad_dynamic-slice_fusion.refs_2_.refs_0_, bf16[400,1600]{1,0:T(8,128)(2,1)} %refs_1_.2, ...), custom_call_target="tpu_custom_call" | custom-call | tf_op jit(solution)/shard_map/pallas_call | solution.py:1077
  301.5 41.9 %shard_map.366 = (bf16[8,256,1600]{2,1,0:T(8,128)(2,1)}, bf16[8,256,688]{2,1,0:T(8,128)(2,1)}, bf16[8,256,688]{2,1,0:T(8,128)(2,1)}, bf16[8,256,688]{2,1,0:T(8,128)(2,1)}) custom-call(bf16[256,1600]{1,0:T(8,128)(2,1)} %multiply_convert_fusion.x_ref, bf16[688,1600]{1,0:T(8,128)(2,1)} %get-tuple-element.515.refs_0_.refs_2_, ...), custom_call_target="tpu_custom_call" | custom-call | tf_op jit(solution)/shard_map/pallas_call | solution.py:1321
  343.4 13.8 %shard_map.367 = (bf16[8,256,688]{2,1,0:T(8,128)(2,1)}, bf16[8,256,688]{2,1,0:T(8,128)(2,1)}) custom-call(bf16[8,256,1600]{2,1,0:T(8,128)(2,1)} %bitcast.240, bf16[688,1600]{1,0:T(8,128)(2,1)} %refs_1_.3, bf16[8,256,688]{2,1,0:T(8,128)(2,1)} %get-tuple-element.273.gate_ref, bf16[8,256,688]{2,1,0:T(8,128)(2,1)} %get-tuple-element.274.up_ref), custom_call_target="tpu_custom_call" | custom-call | tf_op jit(solution)/shard_map/pallas_call | solution.py:550
  357.2 10.8 %bitcast_convert_fusion.1 = bf16[688,1600]{1,0:T(8,128)(2,1)} fusion(bf16[8,256,688]{2,1,0:T(8,128)(2,1)} %get-tuple-element.275.refs_0_, bf16[8,256,1600]{2,1,0:T(8,128)(2,1)} %get-tuple-element.277), kind=kOutput, calls=%fused_computation.22 | convolution fusion | flops 4509977600 | bytes 11573248 | tf_op jit(solution)/shard_map/dot_general | solution.py:37
  368.0 6.9 bitcast_convert_fusion
  375.0 7.5 convolution_convert_fusion.5
  382.4 5.5 reshape.572
  387.9 5.5 reshape.573
  398.4 41.7 %shard_map.368 = f32[256,1600]{1,0:T(8,128)} custom-call(bf16[8,256,688]{2,1,0:T(8,128)(2,1)} %get-tuple-element.275.refs_0_, bf16[8,256,688]{2,1,0:T(8,128)(2,1)} %get-tuple-element.276.refs_1_, bf16[688,1600]{1,0:T(8,128)(2,1)} %get-tuple-element.515.refs_0_.refs_2_, bf16[688,1600]{1,0:T(8,128)(2,1)} %get-tuple-element.514.refs_1_.refs_3_, ...), custom_call_target="tpu_custom_call" | custom-call | tf_op jit(solution)/shard_map/pallas_call | solution.py:1077
  444.5 43.2 %shard_map.369 = (bf16[8,256,1600]{2,1,0:T(8,128)(2,1)}, f32[8,256,256]{2,1,0:T(8,128)}, f32[8,256,400]{2,1,0:T(8,128)}, f32[8,256,2]{2,1,0:T(8,128)}) custom-call(bf16[256,1600]{1,0:T(8,128)(2,1)} %get-tuple-element.507.x_ref, bf16[256,1600]{1,0:T(8,128)(2,1)} %pad_dynamic-slice_fusion.refs_2_.refs_0_, bf16[400,1600]{1,0:T(8,128)(2,1)} %refs_1_.2, ...), custom_call_target="tpu_custom_call" | custom-call | tf_op jit(solution)/shard_map/pallas_call | solution.py:1321
  487.8 3.2 fusion.37
  494.9 6.7 shard_map.370
  502.4 125.6 %conditional.2 = (f32[256]{0:T(256)S(1)}, bf16[2048,400]{1,0:T(8,128)(2,1)}, f32[8,2,128,400]{3,2,1,0:T(8,128)}, f32[16,400]{1,0:T(8,128)}, bf16[400,1600]{1,0:T...) conditional(s32[]{:T(128)} %bitcast.51, () %tuple.46, ...), branch_computations={%region_3.4_spmd, %region_4.5_spmd} | conditional | flops 10279668736 | bytes 103040800 | solution.py:1443
  503.7 23.8 %branch_1_fun.5 = (bf16[8,2,128,256]{3,2,1,0:T(8,128)(2,1)}, bf16[8,2,128,128]{3,2,1,0:T(8,128)(2,1)}, bf16[8,2,128,128]{3,2,1,0:T(8,128)(2,1)}, f32[8,256]{1,0:T(8,128)}) custom-call(s32[8]{0:T(128)S(1)} %get-tuple-element.126.slot_ref, s32[2]{0:T(128)S(1)} %get-tuple-element.127.len_ref, bf16[8,2,128,256]{3,2,1,0:T(8,128)(2,1)} %get-tuple-element.128.q_ref, ...), custom_call_target="tpu_custom_call" | custom-call | tf_op jit(solution)/shard_map/cond/branch_1_fun/pallas_call | solution.py:415
  528.2 64.9 %branch_1_fun.6 = (bf16[8,2,128,400]{3,2,1,0:T(8,128)(2,1)}, f32[8,2,128,400]{3,2,1,0:T(8,128)}, bf16[8,2,128,400]{3,2,1,0:T(8,128)(2,1)}, f32[8,2,128,16]{3,2,1...) custom-call(s32[2]{0:T(128)S(1)} %get-tuple-element.127.len_ref, ...), custom_call_target="tpu_custom_call" | custom-call | tf_op jit(solution)/shard_map/cond/branch_1_fun/pallas_call | solution.py:256
  593.1 8.0 fusion.1
  601.2 8.0 fusion.4
  612.2 6.5 fusion.2
  620.9 3.7 fusion.5
  628.0 4.5 all-to-all-start.2
  640.2 3.2 collective-permute-start
  643.4 3.4 copy.158
  646.8 2.8 pad_maximum_fusion.1.p_ref
  649.6 4.6 all-to-all-done.2
  654.2 4.3 all-to-all-start.4
  669.7 5.4 reshape.577
  676.3 5.4 reshape.578
  682.9 5.4 reshape.579
  692.1 18.6 %shard_map.371 = bf16[8,256,132]{2,1,0:T(8,128)(2,1)S(1)} custom-call(bf16[8,256,132]{2,1,0:T(8,128)(2,1)} %pad_maximum_fusion.1.p_ref, f32[8,128]{1,0:T(8,128)} %broadcast_in_dim.69.after_ref), custom_call_target="tpu_custom_call" | custom-call | tf_op jit(solution)/shard_map/pallas_call | solution.py:916
  719.7 4.3 add.363
  726.2 3.4 add_add_fusion
  732.2 4.1 convert_element_type.310
  736.3 27.2 %conditional.3 = (bf16[1600,400]{0,1:T(8,128)(2,1)}, bf16[132,400]{1,0:T(8,128)(2,1)S(1)}, bf16[400,100]{1,0:T(8,128)(2,1)S(1)}, bf16[8,256,400]{2,1,0:T(8,128)(2,1)}, f32[5,400]{1,0:T(8,128)S(1)}) conditional(s32[]{:T(128)} %bitcast.51, () %tuple.45, (bf16[8,256,132]{2,1,0:T(8,128)(2,1)S(1)}, f32[8,2,128,400]{3,2,1,0:T(8,128)}, ...), branch_computations={%region_8.9_spmd, %region_9.10_spmd} | conditional | flops 3002281472 | bytes 22715744 | solution.py:1443
  736.5 15.3 %branch_1_fun.7 = (bf16[8,2,128,400]{3,2,1,0:T(8,128)(2,1)}, f32[8,400]{1,0:T(8,128)S(1)}) custom-call(f32[8,2,128,400]{3,2,1,0:T(8,128)} %get-tuple-element.162.gmix_ref, bf16[8,2,128,132]{3,2,1,0:T(8,128)(2,1)S(1)} %bitcast.231, bf16[132,400]{1,0:T(8,128)(2,1)S(1)} %get-tuple-element.164.xp_ref, f32[8,2,128,400]{3,2,1,0:T(8,128)} %get-tuple-element.165.pre_ref, ...), custom_call_target="tpu_custom_call" | custom-call | tf_op jit(solution)/shard_map/cond/branch_1_fun/pallas_call | solution.py:503
  751.8 8.0 fusion.6
  763.6 41.7 %shard_map.372 = f32[256,1600]{1,0:T(8,128)} custom-call(bf16[8,256,400]{2,1,0:T(8,128)(2,1)} %get-tuple-element.296.refs_0_, bf16[8,256,400]{2,1,0:T(8,128)(2,1)} %get-tuple-element.297.refs_1_, bf16[8,256,512]{2,1,0:T(8,128)(2,1)} %get-tuple-element.298.refs_2_, bf16[1600,400]{1,0:T(8,128)(2,1)} %bitcast.234, bf16[1600,400]{1,0:T(8,128)(2,1)} %bitcast.37.wz_ref.refs_4_, ...), custom_call_target="tpu_custom_call" | custom-call | tf_op jit(solution)/shard_map/pallas_call | solution.py:1077
  805.3 3.1 reshape.580
  810.8 38.0 %shard_map.373 = f32[256,1600]{1,0:T(8,128)} custom-call(bf16[8,256,688]{2,1,0:T(8,128)(2,1)} %get-tuple-element.272.refs_0_, bf16[688,1600]{1,0:T(8,128)(2,1)} %refs_1_.3, f32[8,128]{1,0:T(8,128)} %broadcast_in_dim.70.refs_2_), custom_call_target="tpu_custom_call" | custom-call | tf_op jit(solution)/shard_map/pallas_call | solution.py:1077
  848.8 3.2 fusion.34
  853.2 3.4 copy.156
  856.7 4.8 all-to-all-start.3
  868.4 3.2 reshape.586
  873.1 5.9 convert_bitcast_fusion
  879.0 4.3 all-to-all-done.3
  885.2 3.1 reshape.585.refs_0_
  888.3 4.4 reshape_reshape.20
  895.3 6.3 shard_map.375
  903.3 45.4 %shard_map.376 = f32[80,128]{1,0:T(8,128)} custom-call(f32[80,128]{1,0:T(8,128)} %fusion.32.x_ref), custom_call_target="tpu_custom_call" | custom-call | tf_op jit(solution)/shard_map/pallas_call | solution.py:696
  963.4 3.9 reshape.591
  968.5 3.8 reshape.588
  979.4 51.1 %shard_map.374 = (f32[200,3200]{1,0:T(8,128)}, f32[132,400]{1,0:T(8,128)}, f32[400,100]{1,0:T(8,128)}) custom-call(bf16[200,3200]{1,0:T(8,128)(2,1)} %reshape.585.refs_0_, bf16[132,400]{1,0:T(8,128)(2,1)S(1)} %copy-done.28, bf16[400,100]{1,0:T(8,128)(2,1)S(1)} %get-tuple-element.303.refs_2_, f32[8,128]{1,0:T(8,128)} %broadcast_in_dim.72.refs_3_), custom_call_target="tpu_custom_call" | custom-call | tf_op jit(solution)/shard_map/pallas_call | solution.py:1210
  1032.4 3.2 convert_element_type.307
  (270 shorter events, 144.9 us)
Async XLA Ops:
  7.2 100.9 %copy-start = (bf16[100,3200]{1,0:T(8,128)(2,1)S(1)}, bf16[100,3200]{1,0:T(8,128)(2,1)}, u32[]{:S(2)}) copy-start(bf16[100,3200]{1,0:T(8,128)(2,1)} %param.33) | copy-start | bytes 1920004
  7.2 250.9 %all-gather.3.cloned.1.call-start = ((), (), s32[]{:S(2)}) async-start(), calls=%async_computation.5 | async-start | bytes 5990400 | tf_op jit(solution)/shard_map/all_gather | solution.py:1469
  11.5 96.7 %copy-start.47 = (s32[8]{0:T(128)}, s32[8]{0:T(128)S(1)}, u32[]{:S(2)}) copy-start(s32[8]{0:T(128)S(1)} %fusion.33.slot_ref) | copy-start | bytes 100
  11.5 57.3 %copy-start.43 = (s32[2]{0:T(128)S(1)}, s32[2]{0:T(128)}, u32[]{:S(2)}) copy-start(s32[2]{0:T(128)} %len_ref.3) | copy-start | bytes 28
  68.8 24.0 %copy-start.26 = (bf16[200,1600]{1,0:T(8,128)(2,1)S(1)}, bf16[200,1600]{1,0:T(8,128)(2,1)}, u32[]{:S(2)}) copy-start(bf16[200,1600]{1,0:T(8,128)(2,1)} %param.30) | copy-start | bytes 1920004
  93.7 249.7 %all-gather.5.cloned.1.call-start = ((), (), s32[]{:S(2)}) async-start(), calls=%async_computation.6 | async-start | bytes 7667712 | tf_op jit(solution)/shard_map/all_gather | solution.py:1474
  101.4 6.8 copy-start.30
  101.5 31.7 %all-to-all-start = ((bf16[8,200,400]{2,1,0:T(8,128)(2,1)}), bf16[8,200,400]{2,1,0:T(8,128)(2,1)}, u32[]{:S(2)}, u32[]{:S(2)}) async-start(bf16[8,200,400]{2,1,0:T(8,128)(2,1)} %get-tuple-element.262), calls=%async_computation | async-start | bytes 3276800 | tf_op jit(solution)/shard_map/all_to_all | solution.py:1435
  108.1 89.9 %copy-start.34 = (f32[16,400]{1,0:T(8,128)}, f32[16,400]{1,0:T(8,128)S(1)}, u32[]{:S(2)}) copy-start(f32[16,400]{1,0:T(8,128)S(1)} %exponential_negate_fusion.rate_ref) | copy-start | bytes 76804
  128.8 4.4 copy-start.31
  128.8 121.5 %copy-start.2 = (f32[8,2,128,256]{3,2,1,0:T(8,128)}, f32[8,2,128,256]{3,2,1,0:T(8,128)S(1)}, u32[]{:S(2)}) copy-start(f32[8,2,128,256]{3,2,1,0:T(8,128)S(1)} %get-tuple-element.261) | copy-start | bytes 6291460
  129.1 8.5 copy-start.42
  129.1 8.6 copy-start.38
  133.1 64.9 %all-to-all-start.1 = ((bf16[8,200,400]{2,1,0:T(8,128)(2,1)}), bf16[8,200,400]{2,1,0:T(8,128)(2,1)}, u32[]{:S(2)}, u32[]{:S(2)}) async-start(bf16[8,200,400]{2,1,0:T(8,128)(2,1)} %get-tuple-element.266), calls=%async_computation.1 | async-start | bytes 3276800 | tf_op jit(solution)/shard_map/all_to_all | solution.py:1435
  146.9 7.6 copy-start.20
  258.1 2.5 copy-start.19
  298.0 2.3 copy-start.40
  357.2 10.8 %copy-start.13 = (bf16[8,256,688]{2,1,0:T(8,128)(2,1)S(1)}, bf16[8,256,688]{2,1,0:T(8,128)(2,1)}, u32[]{:S(2)}) copy-start(bf16[8,256,688]{2,1,0:T(8,128)(2,1)} %get-tuple-element.276.refs_1_) | copy-start | bytes 8454148
  357.2 10.8 %copy-start.49 = (bf16[8,256,1600]{2,1,0:T(8,128)(2,1)S(1)}, bf16[8,256,1600]{2,1,0:T(8,128)(2,1)}, u32[]{:S(2)}) copy-start(bf16[8,256,1600]{2,1,0:T(8,128)(2,1)} %get-tuple-element.277) | copy-start | bytes 19660804
  357.2 17.7 %slice-start.2 = ((s8[6815744]{0:T(1024)(128)(4,1)}), s8[4194304]{0:T(1024)(128)(4,1)S(1)}, s32[]{:S(2)}) async-start(s8[6815744]{0:T(1024)(128)(4,1)} %bitcast.241), calls=%async_computation.11 | async-start | bytes 8388608
  368.0 6.9 slice-start.3
  368.0 6.9 copy-start.12
  393.3 276.3 %all-reduce.13.cloned.1.call-start = ((), (), s32[]{:S(2)}) async-start(), calls=%async_computation.8 | async-start | bytes 13737984 | tf_op jit(solution)/shard_map/psum | solution.py:1438
  440.1 2.1 copy-start.5
  440.1 2.5 copy-start.6
  491.0 11.3 %copy-start.7 = (f32[8,2,128,4]{3,2,1,0:T(8,128)S(1)}, f32[8,2,128,4]{3,2,1,0:T(8,128)}, u32[]{:S(2)}) copy-start(f32[8,2,128,4]{3,2,1,0:T(8,128)} %get-tuple-element.263) | copy-start | bytes 98308
  491.0 11.3 %copy-start.35 = (f32[16,400]{1,0:T(8,128)S(1)}, f32[16,400]{1,0:T(8,128)}, u32[]{:S(2)}) copy-start(f32[16,400]{1,0:T(8,128)} %copy-done.34) | copy-start | bytes 76804
  491.0 11.3 %copy-start.44 = (s32[2]{0:T(128)S(1)}, s32[2]{0:T(128)}, u32[]{:S(2)}) copy-start(s32[2]{0:T(128)} %len_ref.3) | copy-start | bytes 28
  491.0 11.3 %copy-start.48 = (s32[8]{0:T(128)S(1)}, s32[8]{0:T(128)}, u32[]{:S(2)}) copy-start(s32[8]{0:T(128)} %copy-done.47) | copy-start | bytes 100
  503.7 24.5 %copy-start.29 = (f32[8,2,16,400]{3,2,1,0:T(8,128)S(1)}, f32[8,2,16,400]{3,2,1,0:T(8,128)}, u32[]{:S(2)}) copy-start(f32[8,2,16,400]{3,2,1,0:T(8,128)} %get-tuple-element.142.start_ref) | copy-start | bytes 1228804 | tf_op jit(solution)/shard_map/cond
  593.1 19.1 %slice-start = ((s8[6815744]{0:T(1024)(128)(4,1)}), s8[4194304]{0:T(1024)(128)(4,1)S(1)}, s32[]{:S(2)}) async-start(s8[6815744]{0:T(1024)(128)(4,1)} %bitcast.229), calls=%async_computation.9 | async-start | bytes 8388608 | tf_op jit(solution)/shard_map/cond
  601.2 8.0 copy-start.24
  601.2 11.0 %slice-start.1 = ((s8[6815744]{0:T(1024)(128)(4,1)}), s8[2621440]{0:T(1024)(128)(4,1)S(1)}, s32[]{:S(2)}) async-start(s8[6815744]{0:T(1024)(128)(4,1)} %bitcast.229), calls=%async_computation.10 | async-start | bytes 5242880 | tf_op jit(solution)/shard_map/cond
  609.2 2.1 copy-start.32
  612.2 8.7 slice-start.4
  612.2 7.5 copy-start.23
  612.2 8.7 slice-start.5
  618.7 2.2 copy-start.25
  628.0 5.1 copy-start.16
  628.0 7.5 copy-start.45
  628.0 4.5 copy-start.50
  628.0 26.2 %all-to-all-start.2 = ((bf16[8,200,512]{2,1,0:T(8,128)(2,1)}), bf16[8,200,512]{2,1,0:T(8,128)(2,1)}, u32[]{:S(2)}, u32[]{:S(2)}) async-start(bf16[8,200,512]{2,1,0:T(8,128)(2,1)} %bitcast.72), calls=%async_computation.2 | async-start | bytes 3276800 | tf_op jit(solution)/shard_map/all_to_all | solution.py:1435
  638.5 8.3 copy-start.17
  638.5 87.6 %collective-permute-start.1 = (bf16[200,1600]{1,0:T(8,128)(2,1)}, bf16[200,1600]{1,0:T(8,128)(2,1)}, u32[]{:S(2)}, u32[]{:S(2)}) collective-permute-start(bf16[200,1600]{1,0:T(8,128)(2,1)} %get-tuple-element.517), channel_id=1, source_target_pairs={{3,5},{4,6},{5,7},{11,13},{12,14},{13,15},{19,21},{20,22},{21,23},... | collective-permute-start | bytes 1920008 | tf_op jit(solution)/shard_map/ppermute | solution.py:1410
  640.2 85.9 %collective-permute-start = (bf16[200,1600]{1,0:T(8,128)(2,1)}, bf16[200,1600]{1,0:T(8,128)(2,1)}, u32[]{:S(2)}, u32[]{:S(2)}) collective-permute-start(bf16[200,1600]{1,0:T(8,128)(2,1)} %get-tuple-element.516), channel_id=1, source_target_pairs={{0,1},{1,2},{2,3},{3,4},{4,5},{5,6},{6,7},{8,9},{9,10},{10,11},{11... | collective-permute-start | bytes 1920008 | tf_op jit(solution)/shard_map/ppermute | solution.py:1410
  654.2 62.2 %all-to-all-start.4 = ((bf16[8,200,400]{2,1,0:T(8,128)(2,1)}), bf16[8,200,400]{2,1,0:T(8,128)(2,1)}, u32[]{:S(2)}, u32[]{:S(2)}) async-start(bf16[8,200,400]{2,1,0:T(8,128)(2,1)} %bitcast.244), calls=%async_computation.4 | async-start | bytes 3276800 | tf_op jit(solution)/shard_map/all_to_all | solution.py:1435
  658.5 296.0 %all-reduce.11.cloned.1.call-start = ((), (), s32[]{:S(2)}) async-start(), calls=%async_computation.7 | async-start | bytes 8396800 | tf_op jit(solution)/shard_map/psum | solution.py:1438
  729.6 1.4 copy-start.46
  729.6 1.7 copy-start.39
  732.2 4.1 copy-start.21
  751.8 8.0 copy-start.18
  763.6 41.7 %copy-start.27 = (bf16[132,400]{1,0:T(8,128)(2,1)}, bf16[132,400]{1,0:T(8,128)(2,1)S(1)}, u32[]{:S(2)}) copy-start(bf16[132,400]{1,0:T(8,128)(2,1)S(1)} %get-tuple-element.302.refs_1_) | copy-start | bytes 316804
  856.7 4.9 copy-start.3
  856.7 4.9 copy-start.41
  856.7 26.6 %all-to-all-start.3 = ((bf16[8,200,400]{2,1,0:T(8,128)(2,1)}), bf16[8,200,400]{2,1,0:T(8,128)(2,1)}, u32[]{:S(2)}, u32[]{:S(2)}) async-start(bf16[8,200,400]{2,1,0:T(8,128)(2,1)} %bitcast.245), calls=%async_computation.3 | async-start | bytes 3276800 | tf_op jit(solution)/shard_map/all_to_all | solution.py:1435
  861.6 2.1 copy-start.4
  861.6 2.5 copy-start.10
  868.3 4.7 copy-start.9
  954.5 2.4 copy-start.14
  954.5 4.0 copy-start.11
  963.4 16.0 %copy-start.28 = (bf16[132,400]{1,0:T(8,128)(2,1)S(1)}, bf16[132,400]{1,0:T(8,128)(2,1)}, u32[]{:S(2)}) copy-start(bf16[132,400]{1,0:T(8,128)(2,1)} %copy-done.27) | copy-start | bytes 316804
  1032.4 3.2 copy-start.15
  1035.5 3.4 copy-start.36
  1035.5 4.1 copy-start.1
  (4 other events, 4.4 us)
Sparse Core Ops, SparseCore 0:
  93.8 55.8 all-gather.2
  151.6 56.3 all-gather.4
  396.7 242.7 all-reduce.12
  729.7 192.0 all-reduce.10
